TPU v7x, 32 devices: a whole 2x2x4 slice. The times are simulated.
32 devices in a mesh: dp: 16 (over z, y, core), tensor: 2 (over x).
Axes of the slice: x: 2, y: 2, z: 4, core: 2. Of those that a mesh axis runs over, the one named last changes fastest.
Arguments:
- tokens: bfloat16 [1024, 8192], P(('dp', 'tensor')), may hold values from -6 to 6
- gain: float32 [8192], replicated, may hold values from 0.1 to 1.9
- stale: bfloat16 [8192, 2048], P(None, 'tensor'), may hold values from -0.0625 to 0.0625
- bias: float32 [2048], P('tensor'), may hold values from -3 to 3
- first: float32 [8192, 2048], P(('dp', 'tensor')), may hold values from -6 to 6
- second: float32 [8192, 2048], P(('dp', 'tensor')), may hold values from 0.1 to 10
- grad: float32 [8192, 2048], P(('dp', 'tensor')), may hold values from -6 to 6
- residual: float32 [8192, 2048], P(('dp', 'tensor')), may hold values from -0.12 to 0.12
- exponent: int32 [256, 16], P(('dp', 'tensor')), may hold values from 10 to 17
Outputs:
- new_first: float32 [8192, 2048], P(('dp', 'tensor'))
- new_second: float32 [8192, 2048], P(('dp', 'tensor'))
- projected: bfloat16 [1024, 2048], P('dp', 'tensor')
All inputs are finite; a program needn't handle non-finite values.
Results may differ from a plain program's by a relative error of at most 0.0062.
Values may be sent and summed in bfloat16 or wider, within the bound.
No kernel may reach another device: no remote copies, remote signals or barrier semaphores. Data moves between devices by JAX's collectives and lax.ppermute only.
A program may use at most 128 MiB of HBM per device.

v0:
```python
import jax
import jax.numpy as jnp
from jax import lax
from jax.sharding import PartitionSpec as P

QROWS = 32
QCOL = 128


def on_device(tokens, gain, stale, bias, first, second, grad, residual, exponent):
    values = tokens.astype(jnp.float32)
    meansq = jnp.mean(values * values, axis=1, keepdims=True)
    normed = (values * lax.rsqrt(meansq + 1e-06) * gain[None, :]).astype(jnp.bfloat16)
    whole = lax.all_gather(normed, "tensor", axis=0, tiled=True)
    new_first = 0.9 * first + 0.1 * grad
    new_second = 0.95 * second + 0.05 * grad * grad
    corrected = 0.02 * new_first / (jnp.sqrt(new_second) + 1e-08) + residual
    expo = exponent.astype(jnp.float32)
    upward = jnp.exp2(expo)[:, None, :, None]
    downward = jnp.exp2(-expo)[:, None, :, None]
    local_rows = first.shape[0]
    full_cols = first.shape[1]
    blocked = corrected.reshape(exponent.shape[0], QROWS, exponent.shape[1], QCOL) * upward
    quant = jnp.clip(blocked, -448.0, 448.0).astype(jnp.bfloat16)
    quant = lax.optimization_barrier(quant)
    delta = (
        (quant.astype(jnp.float32) * downward).reshape(local_rows, full_cols).astype(jnp.bfloat16)
    )
    owned = lax.all_to_all(delta, "tensor", split_axis=1, concat_axis=0, tiled=True)
    merged = (
        stale.astype(jnp.float32)
        + lax.all_gather(owned, "dp", axis=0, tiled=True).astype(jnp.float32)
    ).astype(jnp.bfloat16)
    product = jnp.dot(whole, merged, preferred_element_type=jnp.float32)
    projected = (product + bias[None, :]).astype(jnp.bfloat16)
    return (new_first, new_second, projected)


def solution(mesh):
    return jax.shard_map(
        on_device,
        mesh=mesh,
        in_specs=(
            P(("dp", "tensor"), None),
            P(),
            P(None, "tensor"),
            P("tensor"),
            P(("dp", "tensor"), None),
            P(("dp", "tensor"), None),
            P(("dp", "tensor"), None),
            P(("dp", "tensor"), None),
            P(("dp", "tensor"), None),
        ),
        out_specs=(P(("dp", "tensor"), None), P(("dp", "tensor"), None), P("dp", "tensor")),
        check_vma=False,
    )
```

profile of v0, /device:TPU:0, one launch (start us, length us, event | category | flops | bytes accessed | tf_op | source)
XLA Modules:
  0.0 195.9 jit_solution(6196986288604967033)
XLA Ops:
  7.2 0.0 copy-start
  7.2 0.0 all-gather.3.cloned.1.call-start
  7.2 1.4 fusion.6
  8.6 2.0 %fusion.8 = bf16[32,8192]{1,0:T(8,128)(2,1)} fusion(bf16[32,8192]{1,0:T(8,128)(2,1)} %param.9, f32[8192]{0:T(1024)} %param.10, f32[32]{0:T(128)S(1)} %add_rsqrt_fusion), kind=kLoop, calls=%fused_computation.16 | loop fusion | flops 1048576 | bytes 1081472 | tf_op jit(solution)/shard_map/convert_element_type | solution.py:13
  10.7 0.0 all-gather.3.cloned.1.call-update
  10.7 0.0 all-gather.5.cloned.1.call-start
  10.7 0.0 copy-done
  10.8 6.3 %add_bitcast_fusion = (f32[32,8,16,128]{3,1,2,0:T(8,128)S(1)}, f32[256,2048]{1,0:T(8,128)}, f32[256,2048]{1,0:T(8,128)}) fusion(f32[256,2048]{1,0:T(8,128)S(1)} %copy-done, f32[256,2048]{1,0:T(8,128)} %param.15, f32[256,2048]{1,0:T(8,128)} %param.14, f32[256,2048]{1,0:T(8,128)} %param.13), kind=kLoop, calls=%fused_computation.8 | loop fusion | flops 5767168 | bytes 14680064
  17.1 0.0 copy-start.2
  17.1 0.4 copy.13
  17.5 0.3 copy-done.2
  17.8 0.3 fusion.3
  18.1 0.3 multiply_convert_fusion
  18.4 0.3 convert_element_type.41
  18.7 0.3 copy.12
  19.0 0.0 copy-start.1
  19.0 27.0 %all_to_all.16 = bf16[256,2,1024]{2,0,1:T(8,128)(2,1)} all-to-all(bf16[256,2,1024]{2,0,1:T(8,128)(2,1)S(1)} %copy.12), channel_id=1, replica_groups=mesh['dp'=16,'tensor'=2] {'tensor'}, dimensions={1} | all-to-all | bytes 2097152 | tf_op jit(solution)/shard_map/all_to_all | solution.py:29
  45.9 0.0 all-gather.5.cloned.1.call-update
  46.0 0.0 all-gather.3.cloned.1.call-done
  46.0 127.0 %all-gather.5.cloned.1.call-done = bf16[8192,1024]{1,0:T(8,128)(2,1)} async-done(((bf16[512,1024]{1,0:T(8,128)(2,1)}), bf16[8192,1024]{1,0:T(8,128)(2,1)}) %all-gather.5.cloned.1.call-update) | async-done | bytes 16777232 | tf_op jit(solution)/shard_map/all_gather | solution.py:32
  173.0 0.0 copy-done.1
  173.0 16.1 %fusion.5 = bf16[64,1024]{1,0:T(8,128)(2,1)} fusion(bf16[64,8192]{1,0:T(8,128)(2,1)} %all-gather.3.cloned.1.call-done, bf16[8192,1024]{1,0:T(8,128)(2,1)} %all-gather.5.cloned.1.call-done, bf16[8192,1024]{1,0:T(8,128)(2,1)} %param.11, f32[1024]{0:T(1024)S(1)} %copy-done.1), kind=kOutput, calls=%fused_computation.13 | convolution fusion | flops 1107427328 | bytes 34738176 | tf_op jit(solution)/shard_map/dot_general | solution.py:34
  (2 shorter events, 0.0 us)
Async XLA Ops:
  7.2 3.6 %copy-start = (f32[256,2048]{1,0:T(8,128)S(1)}, f32[256,2048]{1,0:T(8,128)}, u32[]{:S(2)}) copy-start(f32[256,2048]{1,0:T(8,128)} %param.16) | copy-start | bytes 6291460
  7.2 38.8 %all-gather.3.cloned.1.call-start = ((), (), s32[]{:S(2)}) async-start(), calls=%async_computation.1 | async-start | bytes 1572864 | tf_op jit(solution)/shard_map/all_gather | solution.py:14
  10.7 162.3 %all-gather.5.cloned.1.call-start = ((), (), s32[]{:S(2)}) async-start(), calls=%async_computation.2 | async-start | bytes 17825792 | tf_op jit(solution)/shard_map/all_gather | solution.py:32
  17.1 0.7 copy-start.2
  19.0 154.1 %copy-start.1 = (f32[1024]{0:T(1024)S(1)}, f32[1024]{0:T(1024)}, u32[]{:S(2)}) copy-start(f32[1024]{0:T(1024)} %param.12) | copy-start | bytes 12292
Sparse Core Ops, SparseCore 0:
  10.8 32.6 all-gather.2
  46.1 126.8 all-gather.4
where the time goes:
time: 196 us
  waiting for transfers between devices  127 us (65%)
  blocking collectives  27 us (14%)
  matrix products  16.1 us (8%)
  between operations  14.1 us (7%)
  other arithmetic  10.4 us (5%)
    all_gather x1, waiting for transfers between devices, on_device(): lax.all_gather(owned, 'dp', axis=0, tiled=True).astype(jnp.float32)  127 us
    all_to_all x1, blocking collectives, on_device(): lax.all_to_all(delta, 'tensor', split_axis=1, concat_axis=0, tiled=True)  27 us
    dot_general x1, matrix products, on_device(): product = jnp.dot(whole, merged, preferred_element_type=jnp.float32)  16.1 us
    unnamed x1, other arithmetic  6.34 us
  transfers between devices with their start and end apart: 2, of which 1 were waited for; matrix products, arithmetic and copies ran while one was open for 4% of the time, Pallas kernels for 0%

commit v1 on v0

v1 whole, which is shorter than its diff:
```python
import functools

import jax
import jax.numpy as jnp
from jax import lax
from jax.experimental import pallas as pl
from jax.experimental.pallas import tpu as pltpu
from jax.sharding import PartitionSpec as P

PAIR = 2
CLIP = 448.0
LIMIT = 28 * 1024 * 1024
F32 = jnp.float32
BF16 = jnp.bfloat16
FAR = pl.BlockSpec(memory_space=pltpu.HBM)
NEAR = pl.BlockSpec(memory_space=pltpu.VMEM)


def far(x):
    return pltpu.with_memory_space_constraint(x, pltpu.HBM)


def like(shape, dtype):
    return jax.ShapeDtypeStruct(shape, dtype)


def normalise(tokens_ref, gain_ref, piece_refs):
    slab = lax.axis_index("dp") // PAIR
    values = tokens_ref[...].astype(F32)
    scale = lax.rsqrt(jnp.mean(values * values, axis=1, keepdims=True) + 1e-06)
    width = piece_refs[0].shape[1]
    for k, piece_ref in enumerate(piece_refs):
        columns = pl.ds(pl.multiple_of((slab ^ k) * width, width), width)
        piece_ref[...] = (tokens_ref[:, columns].astype(F32) * scale * gain_ref[:, columns]).astype(BF16)


def adam_kernel(slabs, chunks, qrows, qcol, heads, start, count, *refs):
    expo_far, *inputs = refs[:5]
    extra = refs[5 : 5 + 2]
    n_in = 7
    new_first_out, new_second_out, delta_out = refs[n_in : n_in + 3]
    pieces = refs[n_in + 3 : n_in + 3 + slabs]
    b0, b1, b2, b3, n1, n2, expo_ref, sems, expo_sem, *rest = refs[n_in + 3 + slabs :]
    bufs = (b0, b1, b2, b3)
    mine = lax.axis_index("tensor")
    rows = inputs[0].shape[0]
    cols = inputs[0].shape[1] // heads
    groups = cols // qcol
    high = rows // chunks

    if slabs:
        tokens_ref, gain_ref, token_sem = rest
        loads = [
            pltpu.make_async_copy(extra[0], tokens_ref, token_sem.at[0]),
            pltpu.make_async_copy(extra[1], gain_ref, token_sem.at[1]),
        ]
        for load in loads:
            load.start()
    fetch_expo = pltpu.make_async_copy(expo_far, expo_ref, expo_sem)
    fetch_expo.start()

    def window(j, c):
        head = mine ^ (start + j)
        return pl.ds(c * high, high), pl.ds(pl.multiple_of(head * cols, cols), cols)

    steps = [(j, c) for j in range(count) for c in range(chunks)]
    fetches, stores = [], []
    for n, (j, c) in enumerate(steps):
        at = window(j, c)
        here = (j, pl.ds(c * high, high), slice(None))
        fetches.append([pltpu.make_async_copy(inputs[a].at[at], bufs[a].at[here], sems.at[n, a]) for a in range(4)])
        for f in fetches[-1]:
            f.start()
    if slabs:
        for load in loads:
            load.wait()
        normalise(tokens_ref, gain_ref, pieces)
    fetch_expo.wait()
    for n, (j, c) in enumerate(steps):
        head = mine ^ (start + j)
        for f in fetches[n]:
            f.wait()
        for b in range(high // qrows):
            row = c * (high // qrows) + b
            here = pl.ds(row * qrows, qrows)
            for g in range(groups):
                lanes = pl.ds(g * qcol, qcol)
                grad = b2[j, here, lanes]
                new_first = 0.9 * b0[j, here, lanes] + 0.1 * grad
                new_second = 0.95 * b1[j, here, lanes] + 0.05 * grad * grad
                n1[j, here, lanes] = new_first
                n2[j, here, lanes] = new_second
                bottom = new_second * lax.rsqrt(new_second) + 1e-08
                inverse = pl.reciprocal(bottom, approx=True)
                inverse = inverse * (2.0 - bottom * inverse)
                corrected = 0.02 * new_first * inverse + b3[j, here, lanes]
                expo = jnp.full((1, qcol), expo_ref[row, head * groups + g], jnp.int32).astype(F32)
                most = CLIP * jnp.exp2(-expo)
                delta_out[j, here, lanes] = jnp.clip(corrected, -most, most).astype(BF16)
        at = window(j, c)
        here = (j, pl.ds(c * high, high), slice(None))
        stores += [
            pltpu.make_async_copy(n1.at[here], new_first_out.at[at], sems.at[n, 4]),
            pltpu.make_async_copy(n2.at[here], new_second_out.at[at], sems.at[n, 5]),
        ]
        for s in stores[-2:]:
            s.start()
    for s in stores:
        s.wait()


def adam(arrays, exponent, heads, start, count, made=(), tokens=None, gain=None, slabs=0, chunks=2):
    rows, full = arrays[0].shape
    qrows, qcol = rows // exponent.shape[0], full // exponent.shape[1]
    cols = full // heads
    chunks = min(chunks, rows // qrows)
    held = pltpu.VMEM((count, rows, cols), F32)
    extra = tuple(made)
    scratch = [held] * 6 + [
        pltpu.SMEM(exponent.shape, jnp.int32),
        pltpu.SemaphoreType.DMA((count * chunks, 6)),
        pltpu.SemaphoreType.DMA(()),
    ]
    pieces = []
    if slabs:
        extra = (tokens, gain.reshape(1, -1))
        height, features = tokens.shape
        pieces = [like((height, features // slabs), BF16)] * slabs
        scratch += [pltpu.VMEM((height, features), BF16), pltpu.VMEM((1, features), F32), pltpu.SemaphoreType.DMA((2,))]
    size = 4 * rows * cols * count
    return pl.pallas_call(
        functools.partial(adam_kernel, slabs, chunks, qrows, qcol, heads, start, count),
        in_specs=[FAR] * (5 + len(extra)),
        out_specs=[FAR] * 2 + [NEAR] * (1 + slabs),
        out_shape=[like((rows, full), F32)] * 2 + [like((count, rows, cols), BF16)] + pieces,
        scratch_shapes=scratch,
        input_output_aliases={5: 0, 6: 1} if made else {},
        compiler_params=pltpu.CompilerParams(vmem_limit_bytes=LIMIT),
        cost_estimate=pl.CostEstimate(flops=0, bytes_accessed=0, transcendentals=0),
    )(*[far(x) for x in (exponent, *arrays, *extra)])


def place_rows(refs, heads, rows):
    core, mine = lax.axis_index("dp") % PAIR, lax.axis_index("tensor")
    for n, ref in enumerate(refs):
        at = ((core ^ (n // heads)) * heads + (mine ^ (n % heads))) * rows
        yield ref, pl.ds(pl.multiple_of(at, rows), rows)


def multiply(piece_refs, weight, out_refs):
    rows = piece_refs[0].shape[0]
    stacked = jnp.concatenate([r[...] for r in piece_refs], axis=0)
    total = jnp.dot(stacked, weight, preferred_element_type=F32)
    for k, out_ref in enumerate(out_refs):
        out_ref[...] = total[k * rows : (k + 1) * rows].astype(out_ref.dtype)


def merge_kernel(slabs, heads, stale_ref, *refs):
    delta_refs, piece_refs = refs[: PAIR * heads], refs[PAIR * heads : PAIR * heads + slabs]
    weight_ref, out_refs = refs[PAIR * heads + slabs], refs[PAIR * heads + slabs + 1 :]
    for ref, here in place_rows(delta_refs, heads, delta_refs[0].shape[0]):
        weight_ref[here, :] = (stale_ref[here, :].astype(F32) + ref[...].astype(F32)).astype(BF16)
    multiply(piece_refs, weight_ref[...], out_refs)


def product_kernel(slabs, *refs):
    multiply(refs[:slabs], refs[slabs][...], refs[slabs + 1 :])


def results_of(pieces, cols, own):
    shape = (pieces[0].shape[0], cols)
    return [like(shape, F32 if own and k == 0 else BF16) for k in range(len(pieces))]


def cost_of(pieces, depth, cols):
    rows = len(pieces) * pieces[0].shape[0]
    return pl.CostEstimate(flops=0, bytes_accessed=0, transcendentals=0)


def merge_product(stale, deltas, pieces, heads):
    depth, cols = stale.shape
    return pl.pallas_call(
        functools.partial(merge_kernel, len(pieces), heads),
        out_shape=[like((depth, cols), BF16)] + results_of(pieces, cols, True),
        compiler_params=pltpu.CompilerParams(vmem_limit_bytes=LIMIT),
        cost_estimate=cost_of(pieces, depth, cols),
    )(stale, *deltas, *pieces)


def product(pieces, weight, own):
    return pl.pallas_call(
        functools.partial(product_kernel, len(pieces)),
        out_shape=results_of(pieces, weight.shape[1], own),
        compiler_params=pltpu.CompilerParams(vmem_limit_bytes=LIMIT),
        cost_estimate=cost_of(pieces, *weight.shape),
    )(*pieces, weight)


def on_device(tokens, gain, stale, bias, first, second, grad, residual, exponent):
    heads = lax.axis_size("tensor")
    replicas = lax.axis_size("dp")
    slabs = replicas // PAIR
    slab, mine = lax.axis_index("dp") // PAIR, lax.axis_index("tensor")
    height = tokens.shape[0]

    def over_tensor(x, j):
        return x if j == 0 else lax.ppermute(x, "tensor", [(i, i ^ j) for i in range(heads)])

    def over_core(x, c):
        return x if c == 0 else lax.ppermute(x, "dp", [(i, i ^ c) for i in range(replicas)])

    def over_slab(x, k):
        return x if k == 0 else lax.ppermute(x, "dp", [(i, i ^ (k * PAIR)) for i in range(replicas)])

    arrays = (first, second, grad, residual)
    *made, theirs, normed = (lambda r: (r[0], r[1], r[2], r[3:]))(
        adam(arrays, exponent, heads, 1, heads - 1, tokens=tokens, gain=gain, slabs=slabs)
    )
    arrived = [over_tensor(theirs[j], j + 1) for j in range(heads - 1)]
    pieces = [None] * slabs
    for k in reversed(range(slabs)):
        pieces[k] = over_slab(normed[k], k)
    new_first, new_second, ours = adam(arrays, exponent, heads, 0, 1, made=made)
    ours, *pieces = lax.optimization_barrier((ours, *pieces))
    owned = [ours[0]] + arrived
    shared = [over_core(x, c) for c in range(PAIR) for x in owned]

    depth = stale.shape[0] // slabs
    held = lax.dynamic_slice_in_dim(stale, slab * depth, depth, axis=0)
    weight, *mine_out = merge_product(held, shared, pieces, heads)
    half = slabs // 2
    results = []
    for j in range(heads):
        if j == 0:
            parts = mine_out
        else:
            parts = []
            for group in (pieces[:half], pieces[half:]):
                moved = over_tensor(jnp.concatenate(group, axis=0), j)
                split = [moved[k * height : (k + 1) * height] for k in range(len(group))]
                parts += product(split, weight, not parts)
        total = parts[0] + bias[None, :]
        for k in range(1, slabs):
            total = total + over_slab(parts[k], k).astype(F32)
        results.append(total.astype(BF16))
    stacked = jnp.stack(results)
    if heads == 2:
        ordered = jnp.where(mine == 0, stacked, stacked[::-1])
    else:
        ordered = jnp.take(stacked, jnp.arange(heads) ^ mine, axis=0)
    projected = ordered.reshape(-1, stacked.shape[-1])
    return (new_first, new_second, projected)


def solution(mesh):
    rows = P(("dp", "tensor"), None)
    return jax.shard_map(
        on_device,
        mesh=mesh,
        in_specs=(rows, P(), P(None, "tensor"), P("tensor"), rows, rows, rows, rows, rows),
        out_specs=(rows, rows, P("dp", "tensor")),
        check_vma=False,
    )
```

time: 196 us -> 62.4 us (0.32)
  waiting for transfers between devices: 127 us -> 8.18 us
  starting transfers between devices: 0.08 us -> 40.5 us
  blocking collectives: 27 us -> 0 us
  matrix products: 16.1 us -> 0 us
  between operations: 14.1 us -> 0.79 us
  Pallas kernels: 0 us -> 10.1 us
  other arithmetic: 10.4 us -> 0.9 us
    all_gather x2 -> x0, waiting for transfers between devices: 127 us -> none  [the longest x1 127 us: on_device(): lax.all_gather(owned, 'dp', axis=0, tiled=True).astype(jnp.float32)]
    ppermute x0 -> x26, starting transfers between devices: none -> 40.5 us  [the longest x21 34.9 us: over_slab(): lax.ppermute(x, 'dp', [(i, i ^ k * PAIR) for i in range(replicas)])]
    all_to_all x1 -> x0, blocking collectives: 27 us -> none  [on_device(): lax.all_to_all(delta, 'tensor', split_axis=1, concat_axis=0, tiled=True)]
    dot_general x1 -> x0, matrix products: 16.1 us -> none  [on_device(): product = jnp.dot(whole, merged, preferred_element_type=jnp.float32)]
    pallas_call x0 -> x5, Pallas kernels: none -> 10.1 us  [the longest x2 7.46 us: adam(): pl.pallas_call(functools.partial(adam_kernel, slabs, chunks, qrows, qcol,...]
    ppermute x0 -> x26, waiting for transfers between devices: none -> 8.18 us  [the longest x21 8.17 us: over_slab(): lax.ppermute(x, 'dp', [(i, i ^ k * PAIR) for i in range(replicas)])]
    unnamed x1 -> x0, other arithmetic: 6.34 us -> none
    convert_element_type x3 -> x0, other arithmetic: 2.64 us -> none  [the longest x1 2.05 us: on_device(): (values * lax.rsqrt(meansq + 1e-06) * gain[None, :]).astype(jnp.bfloat16)]
  transfers between devices with their start and end apart: 2 -> 26, of which waited for: 1 -> 6; matrix products, arithmetic and copies ran while one was open for 4% -> 3% of each run, Pallas kernels for 0% -> 10%
where the time goes in v1:
time: 62.4 us; the launch traced here: 62.3 us
  starting transfers between devices  40.5 us (65%)
  Pallas kernels  10.1 us (16%)
  waiting for transfers between devices  8.18 us (13%)
  local copies, waits for them, and re-layouts  1.8 us (3%)
  other arithmetic  0.9 us (1%)
  between operations  0.79 us (1%)
    ppermute x21, starting transfers between devices, over_slab(): lax.ppermute(x, 'dp', [(i, i ^ k * PAIR) for i in range(replicas)])  34.9 us
    ppermute x21, waiting for transfers between devices, over_slab(): lax.ppermute(x, 'dp', [(i, i ^ k * PAIR) for i in range(replicas)])  8.17 us
    pallas_call x2, Pallas kernels, adam(): pl.pallas_call(functools.partial(adam_kernel, slabs, chunks, qrows, qcol,...  7.46 us
    ppermute x3, starting transfers between devices, over_tensor(): lax.ppermute(x, 'tensor', [(i, i ^ j) for i in range(heads)])  5.14 us
    dynamic_slice x1, local copies, waits for them, and re-layouts, on_device(): held = lax.dynamic_slice_in_dim(stale, slab * depth, depth, axis=0)  1.76 us
    pallas_call x1, Pallas kernels, merge_product(): pl.pallas_call(functools.partial(merge_kernel, len(pieces), heads), out_s...  1.73 us
  transfers between devices with their start and end apart: 26, of which 6 were waited for; matrix products, arithmetic and copies ran while one was open for 3% of the time, Pallas kernels for 10%

profile of v1, /device:TPU:0, one launch (start us, length us, event | category | flops | bytes accessed | tf_op | source)
XLA Modules:
  0.0 62.3 jit_solution(9952152565309801062)
XLA Ops:
  0.6 4.1 %shard_map.112 = (f32[256,2048]{1,0:T(8,128)}, f32[256,2048]{1,0:T(8,128)}, bf16[1,256,1024]{2,1,0:T(8,128)(2,1)S(1)}, bf16[32,1024]{1,0:T(8,128)(2,1)S(1)}, bf1...) custom-call(s32[8,16]{1,0:T(8,128)} %refs_0_.3, ...), custom_call_target="tpu_custom_call" | custom-call | tf_op jit(solution)/shard_map/pallas_call | solution.py:131
  4.7 3.0 %collective-permute-start.7 = (bf16[256,1024]{1,0:T(8,128)(2,1)S(1)}, bf16[256,1024]{1,0:T(8,128)(2,1)S(1)}, u32[]{:S(2)}, u32[]{:S(2)}) collective-permute-start(bf16[256,1024]{1,0:T(8,128)(2,1)S(1)} %bitcast.10), channel_id=1, source_target_pairs={{0,1},{1,0},{2,3},{3,2},{4,5},{5,4},{6,7},{7,6},{8,9},{9,8},{10,11... | collective-permute-start | bytes 1572872 | tf_op jit(solution)/shard_map/ppermute | solution.py:207
  7.7 1.5 %collective-permute-start = (bf16[32,1024]{1,0:T(8,128)(2,1)S(1)}, bf16[32,1024]{1,0:T(8,128)(2,1)S(1)}, u32[]{:S(2)}, u32[]{:S(2)}) collective-permute-start(bf16[32,1024]{1,0:T(8,128)(2,1)S(1)} %get-tuple-element.49), channel_id=1, source_target_pairs={{0,4},{2,6},{4,0},{6,2},{8,12},{10,14},{12,8},{14,10},{16,20},{18,... | collective-permute-start | bytes 196616 | tf_op jit(solution)/shard_map/ppermute | solution.py:213
  9.2 1.6 %collective-permute-start.1 = (bf16[32,1024]{1,0:T(8,128)(2,1)S(1)}, bf16[32,1024]{1,0:T(8,128)(2,1)S(1)}, u32[]{:S(2)}, u32[]{:S(2)}) collective-permute-start(bf16[32,1024]{1,0:T(8,128)(2,1)S(1)} %get-tuple-element.50), channel_id=1, source_target_pairs={{0,8},{2,10},{4,12},{6,14},{8,0},{10,2},{12,4},{14,6},{16,24},{18,... | collective-permute-start | bytes 196616 | tf_op jit(solution)/shard_map/ppermute | solution.py:213
  10.8 0.4 collective-permute-start.2
  11.1 2.6 %collective-permute-start.3 = (bf16[32,1024]{1,0:T(8,128)(2,1)S(1)}, bf16[32,1024]{1,0:T(8,128)(2,1)S(1)}, u32[]{:S(2)}, u32[]{:S(2)}) collective-permute-start(bf16[32,1024]{1,0:T(8,128)(2,1)S(1)} %get-tuple-element.52), channel_id=1, source_target_pairs={{0,16},{2,18},{4,20},{6,22},{8,24},{10,26},{12,28},{14,30},{16,0},... | collective-permute-start | bytes 196616 | tf_op jit(solution)/shard_map/ppermute | solution.py:213
  13.7 0.0 collective-permute-done.refs_5_
  13.7 1.7 %collective-permute-start.4 = (bf16[32,1024]{1,0:T(8,128)(2,1)S(1)}, bf16[32,1024]{1,0:T(8,128)(2,1)S(1)}, u32[]{:S(2)}, u32[]{:S(2)}) collective-permute-start(bf16[32,1024]{1,0:T(8,128)(2,1)S(1)} %get-tuple-element.53), channel_id=1, source_target_pairs={{0,20},{2,22},{4,16},{6,18},{8,28},{10,30},{12,24},{14,26},{16,4},... | collective-permute-start | bytes 196616 | tf_op jit(solution)/shard_map/ppermute | solution.py:213
  15.5 0.0 collective-permute-done.1.refs_6_
  15.5 3.2 %collective-permute-start.5 = (bf16[32,1024]{1,0:T(8,128)(2,1)S(1)}, bf16[32,1024]{1,0:T(8,128)(2,1)S(1)}, u32[]{:S(2)}, u32[]{:S(2)}) collective-permute-start(bf16[32,1024]{1,0:T(8,128)(2,1)S(1)} %get-tuple-element.54), channel_id=1, source_target_pairs={{0,24},{2,26},{4,28},{6,30},{8,16},{10,18},{12,20},{14,22},{16,8},... | collective-permute-start | bytes 196616 | tf_op jit(solution)/shard_map/ppermute | solution.py:213
  18.6 0.0 collective-permute-done.2.refs_7_
  18.6 0.7 %collective-permute-start.6 = (bf16[32,1024]{1,0:T(8,128)(2,1)S(1)}, bf16[32,1024]{1,0:T(8,128)(2,1)S(1)}, u32[]{:S(2)}, u32[]{:S(2)}) collective-permute-start(bf16[32,1024]{1,0:T(8,128)(2,1)S(1)} %get-tuple-element.55), channel_id=1, source_target_pairs={{0,28},{2,30},{4,24},{6,26},{8,20},{10,22},{12,16},{14,18},{16,12}... | collective-permute-start | bytes 196616 | tf_op jit(solution)/shard_map/ppermute | solution.py:213
  19.3 3.4 %shard_map.113 = (f32[256,2048]{1,0:T(8,128)}, f32[256,2048]{1,0:T(8,128)}, bf16[1,256,1024]{2,1,0:T(8,128)(2,1)S(1)}) custom-call(s32[8,16]{1,0:T(8,128)} %refs_0_.3, f32[256,2048]{1,0:T(8,128)} %refs_1_.3, f32[256,2048]{1,0:T(8,128)} %refs_2_.3, f32[256,2048]{1,0:T(8,128)} %refs_3_.3, ...), custom_call_target="tpu_custom_call", output_to_operand_aliasing={{0}: (5, {}), {1}: (6, {})} | custom-call | tf_op jit(solution)/shard_map/pallas_call | solution.py:131
  22.8 0.0 collective-permute-done.3.refs_8_
  22.8 1.1 %collective-permute-done.4.refs_9_ = bf16[32,1024]{1,0:T(8,128)(2,1)S(1)} collective-permute-done((bf16[32,1024]{1,0:T(8,128)(2,1)S(1)}, bf16[32,1024]{1,0:T(8,128)(2,1)S(1)}, u32[]{:S(2)}, u32[]{:S(2)}) %collective-permute-start.4) | collective-permute-done | bytes 65568 | tf_op jit(solution)/shard_map/ppermute | solution.py:213
  23.8 0.0 collective-permute-done.5.refs_10_
  23.8 1.9 %collective-permute-done.6.refs_11_ = bf16[32,1024]{1,0:T(8,128)(2,1)S(1)} collective-permute-done((bf16[32,1024]{1,0:T(8,128)(2,1)S(1)}, bf16[32,1024]{1,0:T(8,128)(2,1)S(1)}, u32[]{:S(2)}, u32[]{:S(2)}) %collective-permute-start.6) | collective-permute-done | bytes 65568 | tf_op jit(solution)/shard_map/ppermute | solution.py:213
  25.7 0.0 collective-permute-start.8
  25.7 0.0 collective-permute-done.7.refs_1_
  25.7 0.5 collective-permute-start.9
  26.2 0.6 %collective-permute-start.21 = (bf16[128,1024]{1,0:T(8,128)(2,1)S(1)}, bf16[128,1024]{1,0:T(8,128)(2,1)S(1)}, u32[]{:S(2)}, u32[]{:S(2)}) collective-permute-start(bf16[128,1024]{1,0:T(8,128)(2,1)S(1)} %pad_maximum_fusion.1), channel_id=1, source_target_pairs={{0,1},{1,0},{2,3},{3,2},{4,5},{5,4},{6,7},{7,6},{8,9},{9,8},{10,11... | collective-permute-start | bytes 786440 | tf_op jit(solution)/shard_map/ppermute | solution.py:207
  26.9 1.5 %collective-permute-start.17 = (bf16[128,1024]{1,0:T(8,128)(2,1)S(1)}, bf16[128,1024]{1,0:T(8,128)(2,1)S(1)}, u32[]{:S(2)}, u32[]{:S(2)}) collective-permute-start(bf16[128,1024]{1,0:T(8,128)(2,1)S(1)} %pad_maximum_fusion), channel_id=1, source_target_pairs={{0,1},{1,0},{2,3},{3,2},{4,5},{5,4},{6,7},{7,6},{8,9},{9,8},{10,11... | collective-permute-start | bytes 786440 | tf_op jit(solution)/shard_map/ppermute | solution.py:207
  28.5 1.8 %constant_dynamic-slice_fusion.stale_ref = bf16[1024,1024]{1,0:T(8,128)(2,1)S(1)} fusion(bf16[8192,1024]{1,0:T(8,128)(2,1)} %param.11, s32[]{:T(128)S(6)} %select_n.18), kind=kLoop, calls=%fused_computation.8 | loop fusion | bytes 4194308 | tf_op jit(solution)/shard_map/dynamic_slice | solution.py:229
  30.2 0.0 collective-permute-done.8.refs_2_
  30.2 0.0 collective-permute-done.9.refs_3_
  30.2 1.7 %shard_map.114 = (bf16[1024,1024]{1,0:T(8,128)(2,1)S(1)}, f32[32,1024]{1,0:T(8,128)S(1)}, bf16[32,1024]{1,0:T(8,128)(2,1)S(1)}, bf16[32,1024]{1,0:T(8,128)(2,1)S...) custom-call(bf16[1024,1024]{1,0:T(8,128)(2,1)S(1)} %constant_dynamic, ...), custom_call_target="tpu_custom_call" | custom-call | tf_op jit(solution)/shard_map/pallas_call | solution.py:182
  32.0 1.6 %collective-permute-start.16 = (bf16[32,1024]{1,0:T(8,128)(2,1)S(1)}, bf16[32,1024]{1,0:T(8,128)(2,1)S(1)}, u32[]{:S(2)}, u32[]{:S(2)}) collective-permute-start(bf16[32,1024]{1,0:T(8,128)(2,1)S(1)} %get-tuple-element.73), channel_id=1, source_target_pairs={{0,28},{2,30},{4,24},{6,26},{8,20},{10,22},{12,16},{14,18},{16,12}... | collective-permute-start | bytes 196616 | tf_op jit(solution)/shard_map/ppermute | solution.py:213
  33.5 2.3 %collective-permute-start.15 = (bf16[32,1024]{1,0:T(8,128)(2,1)S(1)}, bf16[32,1024]{1,0:T(8,128)(2,1)S(1)}, u32[]{:S(2)}, u32[]{:S(2)}) collective-permute-start(bf16[32,1024]{1,0:T(8,128)(2,1)S(1)} %get-tuple-element.72), channel_id=1, source_target_pairs={{0,24},{2,26},{4,28},{6,30},{8,16},{10,18},{12,20},{14,22},{16,8},... | collective-permute-start | bytes 196616 | tf_op jit(solution)/shard_map/ppermute | solution.py:213
  35.8 1.6 %collective-permute-start.14 = (bf16[32,1024]{1,0:T(8,128)(2,1)S(1)}, bf16[32,1024]{1,0:T(8,128)(2,1)S(1)}, u32[]{:S(2)}, u32[]{:S(2)}) collective-permute-start(bf16[32,1024]{1,0:T(8,128)(2,1)S(1)} %get-tuple-element.71), channel_id=1, source_target_pairs={{0,20},{2,22},{4,16},{6,18},{8,28},{10,30},{12,24},{14,26},{16,4},... | collective-permute-start | bytes 196616 | tf_op jit(solution)/shard_map/ppermute | solution.py:213
  37.5 0.0 collective-permute-done.21
  37.5 2.2 %collective-permute-start.13 = (bf16[32,1024]{1,0:T(8,128)(2,1)S(1)}, bf16[32,1024]{1,0:T(8,128)(2,1)S(1)}, u32[]{:S(2)}, u32[]{:S(2)}) collective-permute-start(bf16[32,1024]{1,0:T(8,128)(2,1)S(1)} %get-tuple-element.70), channel_id=1, source_target_pairs={{0,16},{2,18},{4,20},{6,22},{8,24},{10,26},{12,28},{14,30},{16,0},... | collective-permute-start | bytes 196616 | tf_op jit(solution)/shard_map/ppermute | solution.py:213
  39.7 0.0 copy-start
  39.7 0.5 shard_map.116
  40.2 0.0 collective-permute-done.17
  40.2 1.7 %collective-permute-start.12 = (bf16[32,1024]{1,0:T(8,128)(2,1)S(1)}, bf16[32,1024]{1,0:T(8,128)(2,1)S(1)}, u32[]{:S(2)}, u32[]{:S(2)}) collective-permute-start(bf16[32,1024]{1,0:T(8,128)(2,1)S(1)} %get-tuple-element.69), channel_id=1, source_target_pairs={{0,12},{2,14},{4,8},{6,10},{8,4},{10,6},{12,0},{14,2},{16,28},{18,... | collective-permute-start | bytes 196616 | tf_op jit(solution)/shard_map/ppermute | solution.py:213
  41.9 0.0 collective-permute-done.16
  41.9 2.5 %collective-permute-start.11 = (bf16[32,1024]{1,0:T(8,128)(2,1)S(1)}, bf16[32,1024]{1,0:T(8,128)(2,1)S(1)}, u32[]{:S(2)}, u32[]{:S(2)}) collective-permute-start(bf16[32,1024]{1,0:T(8,128)(2,1)S(1)} %get-tuple-element.68), channel_id=1, source_target_pairs={{0,8},{2,10},{4,12},{6,14},{8,0},{10,2},{12,4},{14,6},{16,24},{18,... | collective-permute-start | bytes 196616 | tf_op jit(solution)/shard_map/ppermute | solution.py:213
  44.4 0.0 collective-permute-done.15
  44.4 0.1 collective-permute-start.10
  44.5 2.2 %collective-permute-done.14 = bf16[32,1024]{1,0:T(8,128)(2,1)S(1)} collective-permute-done((bf16[32,1024]{1,0:T(8,128)(2,1)S(1)}, bf16[32,1024]{1,0:T(8,128)(2,1)S(1)}, u32[]{:S(2)}, u32[]{:S(2)}) %collective-permute-start.14) | collective-permute-done | bytes 65568 | tf_op jit(solution)/shard_map/ppermute | solution.py:213
  46.7 2.3 %collective-permute-start.25 = (bf16[32,1024]{1,0:T(8,128)(2,1)S(1)}, bf16[32,1024]{1,0:T(8,128)(2,1)S(1)}, u32[]{:S(2)}, u32[]{:S(2)}) collective-permute-start(bf16[32,1024]{1,0:T(8,128)(2,1)S(1)} %get-tuple-element.82), channel_id=1, source_target_pairs={{0,28},{2,30},{4,24},{6,26},{8,20},{10,22},{12,16},{14,18},{16,12}... | collective-permute-start | bytes 196616 | tf_op jit(solution)/shard_map/ppermute | solution.py:213
  49.0 0.0 collective-permute-done.13
  49.0 1.6 %collective-permute-start.24 = (bf16[32,1024]{1,0:T(8,128)(2,1)S(1)}, bf16[32,1024]{1,0:T(8,128)(2,1)S(1)}, u32[]{:S(2)}, u32[]{:S(2)}) collective-permute-start(bf16[32,1024]{1,0:T(8,128)(2,1)S(1)} %get-tuple-element.81), channel_id=1, source_target_pairs={{0,24},{2,26},{4,28},{6,30},{8,16},{10,18},{12,20},{14,22},{16,8},... | collective-permute-start | bytes 196616 | tf_op jit(solution)/shard_map/ppermute | solution.py:213
  50.6 0.4 shard_map.115
  51.1 0.0 collective-permute-done.12
  51.1 0.1 collective-permute-start.23
  51.2 0.0 collective-permute-done.11
  51.2 3.7 %collective-permute-start.22 = (bf16[32,1024]{1,0:T(8,128)(2,1)S(1)}, bf16[32,1024]{1,0:T(8,128)(2,1)S(1)}, u32[]{:S(2)}, u32[]{:S(2)}) collective-permute-start(bf16[32,1024]{1,0:T(8,128)(2,1)S(1)} %get-tuple-element.79), channel_id=1, source_target_pairs={{0,16},{2,18},{4,20},{6,22},{8,24},{10,26},{12,28},{14,30},{16,0},... | collective-permute-start | bytes 196616 | tf_op jit(solution)/shard_map/ppermute | solution.py:213
  54.9 0.0 collective-permute-done.10
  54.9 0.0 collective-permute-start.20
  54.9 0.0 collective-permute-done.25
  54.9 2.1 %collective-permute-start.19 = (bf16[32,1024]{1,0:T(8,128)(2,1)S(1)}, bf16[32,1024]{1,0:T(8,128)(2,1)S(1)}, u32[]{:S(2)}, u32[]{:S(2)}) collective-permute-start(bf16[32,1024]{1,0:T(8,128)(2,1)S(1)} %get-tuple-element.77), channel_id=1, source_target_pairs={{0,8},{2,10},{4,12},{6,14},{8,0},{10,2},{12,4},{14,6},{16,24},{18,... | collective-permute-start | bytes 196616 | tf_op jit(solution)/shard_map/ppermute | solution.py:213
  57.0 0.0 collective-permute-done.24
  57.0 1.4 %collective-permute-start.18 = (bf16[32,1024]{1,0:T(8,128)(2,1)S(1)}, bf16[32,1024]{1,0:T(8,128)(2,1)S(1)}, u32[]{:S(2)}, u32[]{:S(2)}) collective-permute-start(bf16[32,1024]{1,0:T(8,128)(2,1)S(1)} %get-tuple-element.76), channel_id=1, source_target_pairs={{0,4},{2,6},{4,0},{6,2},{8,12},{10,14},{12,8},{14,10},{16,20},{18,... | collective-permute-start | bytes 196616 | tf_op jit(solution)/shard_map/ppermute | solution.py:213
  58.4 0.4 collective-permute-done.23
  58.8 0.0 collective-permute-done.22
  58.8 1.9 %collective-permute-done.20 = bf16[32,1024]{1,0:T(8,128)(2,1)S(1)} collective-permute-done((bf16[32,1024]{1,0:T(8,128)(2,1)S(1)}, bf16[32,1024]{1,0:T(8,128)(2,1)S(1)}, u32[]{:S(2)}, u32[]{:S(2)}) %collective-permute-start.20) | collective-permute-done | bytes 65568 | tf_op jit(solution)/shard_map/ppermute | solution.py:213
  60.7 0.0 collective-permute-done.19
  60.7 0.7 %collective-permute-done.18 = bf16[32,1024]{1,0:T(8,128)(2,1)S(1)} collective-permute-done((bf16[32,1024]{1,0:T(8,128)(2,1)S(1)}, bf16[32,1024]{1,0:T(8,128)(2,1)S(1)}, u32[]{:S(2)}, u32[]{:S(2)}) %collective-permute-start.18) | collective-permute-done | bytes 65568 | tf_op jit(solution)/shard_map/ppermute | solution.py:213
  61.4 0.0 copy-done
  61.4 0.2 fusion
  61.6 0.7 %reverse_select_fusion = bf16[2,32,1024]{2,1,0:T(8,128)(2,1)} fusion(bf16[2,32,1024]{2,1,0:T(8,128)(2,1)S(1)} %pad_maximum_fusion.2, pred[]{:T(512)S(6)} %eq.3), kind=kLoop, calls=%fused_computation.2 | loop fusion | flops 65536 | bytes 262145 | tf_op jit(solution)/shard_map/jit(_where)/select_n | solution.py:248
  (5 shorter events, 0.1 us)
Async XLA Ops:
  4.7 21.0 %collective-permute-start.7 = (bf16[256,1024]{1,0:T(8,128)(2,1)S(1)}, bf16[256,1024]{1,0:T(8,128)(2,1)S(1)}, u32[]{:S(2)}, u32[]{:S(2)}) collective-permute-start(bf16[256,1024]{1,0:T(8,128)(2,1)S(1)} %bitcast.10), channel_id=1, source_target_pairs={{0,1},{1,0},{2,3},{3,2},{4,5},{5,4},{6,7},{7,6},{8,9},{9,8},{10,11... | collective-permute-start | bytes 1572872 | tf_op jit(solution)/shard_map/ppermute | solution.py:207
  7.7 6.1 %collective-permute-start = (bf16[32,1024]{1,0:T(8,128)(2,1)S(1)}, bf16[32,1024]{1,0:T(8,128)(2,1)S(1)}, u32[]{:S(2)}, u32[]{:S(2)}) collective-permute-start(bf16[32,1024]{1,0:T(8,128)(2,1)S(1)} %get-tuple-element.49), channel_id=1, source_target_pairs={{0,4},{2,6},{4,0},{6,2},{8,12},{10,14},{12,8},{14,10},{16,20},{18,... | collective-permute-start | bytes 196616 | tf_op jit(solution)/shard_map/ppermute | solution.py:213
  9.2 6.3 %collective-permute-start.1 = (bf16[32,1024]{1,0:T(8,128)(2,1)S(1)}, bf16[32,1024]{1,0:T(8,128)(2,1)S(1)}, u32[]{:S(2)}, u32[]{:S(2)}) collective-permute-start(bf16[32,1024]{1,0:T(8,128)(2,1)S(1)} %get-tuple-element.50), channel_id=1, source_target_pairs={{0,8},{2,10},{4,12},{6,14},{8,0},{10,2},{12,4},{14,6},{16,24},{18,... | collective-permute-start | bytes 196616 | tf_op jit(solution)/shard_map/ppermute | solution.py:213
  10.8 7.9 %collective-permute-start.2 = (bf16[32,1024]{1,0:T(8,128)(2,1)S(1)}, bf16[32,1024]{1,0:T(8,128)(2,1)S(1)}, u32[]{:S(2)}, u32[]{:S(2)}) collective-permute-start(bf16[32,1024]{1,0:T(8,128)(2,1)S(1)} %get-tuple-element.51), channel_id=1, source_target_pairs={{0,12},{2,14},{4,8},{6,10},{8,4},{10,6},{12,0},{14,2},{16,28},{18,... | collective-permute-start | bytes 196616 | tf_op jit(solution)/shard_map/ppermute | solution.py:213
  11.1 11.6 %collective-permute-start.3 = (bf16[32,1024]{1,0:T(8,128)(2,1)S(1)}, bf16[32,1024]{1,0:T(8,128)(2,1)S(1)}, u32[]{:S(2)}, u32[]{:S(2)}) collective-permute-start(bf16[32,1024]{1,0:T(8,128)(2,1)S(1)} %get-tuple-element.52), channel_id=1, source_target_pairs={{0,16},{2,18},{4,20},{6,22},{8,24},{10,26},{12,28},{14,30},{16,0},... | collective-permute-start | bytes 196616 | tf_op jit(solution)/shard_map/ppermute | solution.py:213
  13.7 10.1 %collective-permute-start.4 = (bf16[32,1024]{1,0:T(8,128)(2,1)S(1)}, bf16[32,1024]{1,0:T(8,128)(2,1)S(1)}, u32[]{:S(2)}, u32[]{:S(2)}) collective-permute-start(bf16[32,1024]{1,0:T(8,128)(2,1)S(1)} %get-tuple-element.53), channel_id=1, source_target_pairs={{0,20},{2,22},{4,16},{6,18},{8,28},{10,30},{12,24},{14,26},{16,4},... | collective-permute-start | bytes 196616 | tf_op jit(solution)/shard_map/ppermute | solution.py:213
  15.5 8.4 %collective-permute-start.5 = (bf16[32,1024]{1,0:T(8,128)(2,1)S(1)}, bf16[32,1024]{1,0:T(8,128)(2,1)S(1)}, u32[]{:S(2)}, u32[]{:S(2)}) collective-permute-start(bf16[32,1024]{1,0:T(8,128)(2,1)S(1)} %get-tuple-element.54), channel_id=1, source_target_pairs={{0,24},{2,26},{4,28},{6,30},{8,16},{10,18},{12,20},{14,22},{16,8},... | collective-permute-start | bytes 196616 | tf_op jit(solution)/shard_map/ppermute | solution.py:213
  18.6 7.1 %collective-permute-start.6 = (bf16[32,1024]{1,0:T(8,128)(2,1)S(1)}, bf16[32,1024]{1,0:T(8,128)(2,1)S(1)}, u32[]{:S(2)}, u32[]{:S(2)}) collective-permute-start(bf16[32,1024]{1,0:T(8,128)(2,1)S(1)} %get-tuple-element.55), channel_id=1, source_target_pairs={{0,28},{2,30},{4,24},{6,26},{8,20},{10,22},{12,16},{14,18},{16,12}... | collective-permute-start | bytes 196616 | tf_op jit(solution)/shard_map/ppermute | solution.py:213
  25.7 4.5 %collective-permute-start.8 = (bf16[256,1024]{1,0:T(8,128)(2,1)S(1)}, bf16[256,1024]{1,0:T(8,128)(2,1)S(1)}, u32[]{:S(2)}, u32[]{:S(2)}) collective-permute-start(bf16[256,1024]{1,0:T(8,128)(2,1)S(1)} %bitcast.8), channel_id=1, source_target_pairs={{0,2},{2,0},{4,6},{6,4},{8,10},{10,8},{12,14},{14,12},{16,18},{18,... | collective-permute-start | bytes 1572872 | tf_op jit(solution)/shard_map/ppermute | solution.py:210
  25.7 4.5 %collective-permute-start.9 = (bf16[256,1024]{1,0:T(8,128)(2,1)S(1)}, bf16[256,1024]{1,0:T(8,128)(2,1)S(1)}, u32[]{:S(2)}, u32[]{:S(2)}) collective-permute-start(bf16[256,1024]{1,0:T(8,128)(2,1)S(1)} %collective-permute-done.7.refs_1_), channel_id=1, source_target_pairs={{0,2},{2,0},{4,6},{6,4},{8,10},{10,8},{12,14},{14,12},{16,18},{18,... | collective-permute-start | bytes 1572872 | tf_op jit(solution)/shard_map/ppermute | solution.py:210
  26.2 11.2 %collective-permute-start.21 = (bf16[128,1024]{1,0:T(8,128)(2,1)S(1)}, bf16[128,1024]{1,0:T(8,128)(2,1)S(1)}, u32[]{:S(2)}, u32[]{:S(2)}) collective-permute-start(bf16[128,1024]{1,0:T(8,128)(2,1)S(1)} %pad_maximum_fusion.1), channel_id=1, source_target_pairs={{0,1},{1,0},{2,3},{3,2},{4,5},{5,4},{6,7},{7,6},{8,9},{9,8},{10,11... | collective-permute-start | bytes 786440 | tf_op jit(solution)/shard_map/ppermute | solution.py:207
  26.9 13.3 %collective-permute-start.17 = (bf16[128,1024]{1,0:T(8,128)(2,1)S(1)}, bf16[128,1024]{1,0:T(8,128)(2,1)S(1)}, u32[]{:S(2)}, u32[]{:S(2)}) collective-permute-start(bf16[128,1024]{1,0:T(8,128)(2,1)S(1)} %pad_maximum_fusion), channel_id=1, source_target_pairs={{0,1},{1,0},{2,3},{3,2},{4,5},{5,4},{6,7},{7,6},{8,9},{9,8},{10,11... | collective-permute-start | bytes 786440 | tf_op jit(solution)/shard_map/ppermute | solution.py:207
  32.0 9.9 %collective-permute-start.16 = (bf16[32,1024]{1,0:T(8,128)(2,1)S(1)}, bf16[32,1024]{1,0:T(8,128)(2,1)S(1)}, u32[]{:S(2)}, u32[]{:S(2)}) collective-permute-start(bf16[32,1024]{1,0:T(8,128)(2,1)S(1)} %get-tuple-element.73), channel_id=1, source_target_pairs={{0,28},{2,30},{4,24},{6,26},{8,20},{10,22},{12,16},{14,18},{16,12}... | collective-permute-start | bytes 196616 | tf_op jit(solution)/shard_map/ppermute | solution.py:213
  33.5 10.9 %collective-permute-start.15 = (bf16[32,1024]{1,0:T(8,128)(2,1)S(1)}, bf16[32,1024]{1,0:T(8,128)(2,1)S(1)}, u32[]{:S(2)}, u32[]{:S(2)}) collective-permute-start(bf16[32,1024]{1,0:T(8,128)(2,1)S(1)} %get-tuple-element.72), channel_id=1, source_target_pairs={{0,24},{2,26},{4,28},{6,30},{8,16},{10,18},{12,20},{14,22},{16,8},... | collective-permute-start | bytes 196616 | tf_op jit(solution)/shard_map/ppermute | solution.py:213
  35.8 10.9 %collective-permute-start.14 = (bf16[32,1024]{1,0:T(8,128)(2,1)S(1)}, bf16[32,1024]{1,0:T(8,128)(2,1)S(1)}, u32[]{:S(2)}, u32[]{:S(2)}) collective-permute-start(bf16[32,1024]{1,0:T(8,128)(2,1)S(1)} %get-tuple-element.71), channel_id=1, source_target_pairs={{0,20},{2,22},{4,16},{6,18},{8,28},{10,30},{12,24},{14,26},{16,4},... | collective-permute-start | bytes 196616 | tf_op jit(solution)/shard_map/ppermute | solution.py:213
  37.5 11.5 %collective-permute-start.13 = (bf16[32,1024]{1,0:T(8,128)(2,1)S(1)}, bf16[32,1024]{1,0:T(8,128)(2,1)S(1)}, u32[]{:S(2)}, u32[]{:S(2)}) collective-permute-start(bf16[32,1024]{1,0:T(8,128)(2,1)S(1)} %get-tuple-element.70), channel_id=1, source_target_pairs={{0,16},{2,18},{4,20},{6,22},{8,24},{10,26},{12,28},{14,30},{16,0},... | collective-permute-start | bytes 196616 | tf_op jit(solution)/shard_map/ppermute | solution.py:213
  39.7 21.7 %copy-start = (f32[1024]{0:T(1024)S(1)}, f32[1024]{0:T(1024)}, u32[]{:S(2)}) copy-start(f32[1024]{0:T(1024)} %param.12) | copy-start | bytes 12292
  40.2 10.9 %collective-permute-start.12 = (bf16[32,1024]{1,0:T(8,128)(2,1)S(1)}, bf16[32,1024]{1,0:T(8,128)(2,1)S(1)}, u32[]{:S(2)}, u32[]{:S(2)}) collective-permute-start(bf16[32,1024]{1,0:T(8,128)(2,1)S(1)} %get-tuple-element.69), channel_id=1, source_target_pairs={{0,12},{2,14},{4,8},{6,10},{8,4},{10,6},{12,0},{14,2},{16,28},{18,... | collective-permute-start | bytes 196616 | tf_op jit(solution)/shard_map/ppermute | solution.py:213
  41.9 9.3 %collective-permute-start.11 = (bf16[32,1024]{1,0:T(8,128)(2,1)S(1)}, bf16[32,1024]{1,0:T(8,128)(2,1)S(1)}, u32[]{:S(2)}, u32[]{:S(2)}) collective-permute-start(bf16[32,1024]{1,0:T(8,128)(2,1)S(1)} %get-tuple-element.68), channel_id=1, source_target_pairs={{0,8},{2,10},{4,12},{6,14},{8,0},{10,2},{12,4},{14,6},{16,24},{18,... | collective-permute-start | bytes 196616 | tf_op jit(solution)/shard_map/ppermute | solution.py:213
  44.4 10.5 %collective-permute-start.10 = (bf16[32,1024]{1,0:T(8,128)(2,1)S(1)}, bf16[32,1024]{1,0:T(8,128)(2,1)S(1)}, u32[]{:S(2)}, u32[]{:S(2)}) collective-permute-start(bf16[32,1024]{1,0:T(8,128)(2,1)S(1)} %get-tuple-element.67), channel_id=1, source_target_pairs={{0,4},{2,6},{4,0},{6,2},{8,12},{10,14},{12,8},{14,10},{16,20},{18,... | collective-permute-start | bytes 196616 | tf_op jit(solution)/shard_map/ppermute | solution.py:213
  46.7 8.2 %collective-permute-start.25 = (bf16[32,1024]{1,0:T(8,128)(2,1)S(1)}, bf16[32,1024]{1,0:T(8,128)(2,1)S(1)}, u32[]{:S(2)}, u32[]{:S(2)}) collective-permute-start(bf16[32,1024]{1,0:T(8,128)(2,1)S(1)} %get-tuple-element.82), channel_id=1, source_target_pairs={{0,28},{2,30},{4,24},{6,26},{8,20},{10,22},{12,16},{14,18},{16,12}... | collective-permute-start | bytes 196616 | tf_op jit(solution)/shard_map/ppermute | solution.py:213
  49.0 8.0 %collective-permute-start.24 = (bf16[32,1024]{1,0:T(8,128)(2,1)S(1)}, bf16[32,1024]{1,0:T(8,128)(2,1)S(1)}, u32[]{:S(2)}, u32[]{:S(2)}) collective-permute-start(bf16[32,1024]{1,0:T(8,128)(2,1)S(1)} %get-tuple-element.81), channel_id=1, source_target_pairs={{0,24},{2,26},{4,28},{6,30},{8,16},{10,18},{12,20},{14,22},{16,8},... | collective-permute-start | bytes 196616 | tf_op jit(solution)/shard_map/ppermute | solution.py:213
  51.1 7.7 %collective-permute-start.23 = (bf16[32,1024]{1,0:T(8,128)(2,1)S(1)}, bf16[32,1024]{1,0:T(8,128)(2,1)S(1)}, u32[]{:S(2)}, u32[]{:S(2)}) collective-permute-start(bf16[32,1024]{1,0:T(8,128)(2,1)S(1)} %get-tuple-element.80), channel_id=1, source_target_pairs={{0,20},{2,22},{4,16},{6,18},{8,28},{10,30},{12,24},{14,26},{16,4},... | collective-permute-start | bytes 196616 | tf_op jit(solution)/shard_map/ppermute | solution.py:213
  51.2 7.6 %collective-permute-start.22 = (bf16[32,1024]{1,0:T(8,128)(2,1)S(1)}, bf16[32,1024]{1,0:T(8,128)(2,1)S(1)}, u32[]{:S(2)}, u32[]{:S(2)}) collective-permute-start(bf16[32,1024]{1,0:T(8,128)(2,1)S(1)} %get-tuple-element.79), channel_id=1, source_target_pairs={{0,16},{2,18},{4,20},{6,22},{8,24},{10,26},{12,28},{14,30},{16,0},... | collective-permute-start | bytes 196616 | tf_op jit(solution)/shard_map/ppermute | solution.py:213
  54.9 5.8 %collective-permute-start.20 = (bf16[32,1024]{1,0:T(8,128)(2,1)S(1)}, bf16[32,1024]{1,0:T(8,128)(2,1)S(1)}, u32[]{:S(2)}, u32[]{:S(2)}) collective-permute-start(bf16[32,1024]{1,0:T(8,128)(2,1)S(1)} %get-tuple-element.78), channel_id=1, source_target_pairs={{0,12},{2,14},{4,8},{6,10},{8,4},{10,6},{12,0},{14,2},{16,28},{18,... | collective-permute-start | bytes 196616 | tf_op jit(solution)/shard_map/ppermute | solution.py:213
  54.9 5.8 %collective-permute-start.19 = (bf16[32,1024]{1,0:T(8,128)(2,1)S(1)}, bf16[32,1024]{1,0:T(8,128)(2,1)S(1)}, u32[]{:S(2)}, u32[]{:S(2)}) collective-permute-start(bf16[32,1024]{1,0:T(8,128)(2,1)S(1)} %get-tuple-element.77), channel_id=1, source_target_pairs={{0,8},{2,10},{4,12},{6,14},{8,0},{10,2},{12,4},{14,6},{16,24},{18,... | collective-permute-start | bytes 196616 | tf_op jit(solution)/shard_map/ppermute | solution.py:213
  57.0 4.4 %collective-permute-start.18 = (bf16[32,1024]{1,0:T(8,128)(2,1)S(1)}, bf16[32,1024]{1,0:T(8,128)(2,1)S(1)}, u32[]{:S(2)}, u32[]{:S(2)}) collective-permute-start(bf16[32,1024]{1,0:T(8,128)(2,1)S(1)} %get-tuple-element.76), channel_id=1, source_target_pairs={{0,4},{2,6},{4,0},{6,2},{8,12},{10,14},{12,8},{14,10},{16,20},{18,... | collective-permute-start | bytes 196616 | tf_op jit(solution)/shard_map/ppermute | solution.py:213

commit v2 on v1

v2 whole, which is shorter than its diff:
```python
import functools

import jax
import jax.numpy as jnp
from jax import lax
from jax.experimental import pallas as pl
from jax.experimental.pallas import tpu as pltpu
from jax.sharding import PartitionSpec as P

PAIR = 2
CLIP = 448.0
MIB = 1024 * 1024
F32 = jnp.float32
BF16 = jnp.bfloat16
FAR = pl.BlockSpec(memory_space=pltpu.HBM)
NEAR = pl.BlockSpec(memory_space=pltpu.VMEM)
FREE = pl.CostEstimate(flops=0, bytes_accessed=0, transcendentals=0)


def far(x):
    return pltpu.with_memory_space_constraint(x, pltpu.HBM)


def near_by(x):
    return pltpu.with_memory_space_constraint(x, pltpu.VMEM)


def like(shape, dtype):
    return jax.ShapeDtypeStruct(shape, dtype)


def apart(m, core):
    return (m // 2) * 4 + core * 2 + m % 2


def norm_kernel(ours_ref, theirs_ref, gain_ref, *piece_refs):
    dp = lax.axis_index("dp")
    slab, core = dp // PAIR, dp % PAIR
    height = ours_ref.shape[0]
    width = piece_refs[0].shape[1]
    for turn, ref in enumerate((ours_ref, theirs_ref)):
        values = ref[...].astype(F32)
        scale = lax.rsqrt(jnp.mean(values * values, axis=1, keepdims=True) + 1e-06)
        rows = pl.ds(pl.multiple_of((core ^ turn) * height, height), height)
        for m, piece_ref in enumerate(piece_refs):
            columns = pl.ds(pl.multiple_of((slab ^ apart(m, core)) * width, width), width)
            piece_ref[rows, :] = (ref[:, columns].astype(F32) * scale * gain_ref[:, columns]).astype(BF16)


def norm(ours, theirs, gain, slabs):
    height, features = ours.shape
    return pl.pallas_call(
        norm_kernel,
        out_shape=[like((PAIR * height, features // slabs), BF16)] * (slabs // PAIR),
        compiler_params=pltpu.CompilerParams(vmem_limit_bytes=8 * MIB),
        cost_estimate=FREE,
    )(*[near_by(x) for x in (ours, theirs, gain.reshape(1, features))])


def adam_kernel(chunks, qrows, qcol, heads, *refs):
    expo_far, *inputs = refs[:5]
    new_first_out, new_second_out = refs[5:7]
    delta_outs = refs[7 : 7 + heads]
    b0, b1, b2, b3, n1, n2, expo_ref, sems, expo_sem = refs[7 + heads :]
    bufs = (b0, b1, b2, b3)
    mine = lax.axis_index("tensor")
    rows = inputs[0].shape[0]
    cols = inputs[0].shape[1] // heads
    groups = cols // qcol
    high = rows // chunks

    def window(j, c):
        head = mine ^ j
        return pl.ds(c * high, high), pl.ds(pl.multiple_of(head * cols, cols), cols)

    fetch_expo = pltpu.make_async_copy(expo_far, expo_ref, expo_sem)
    fetch_expo.start()
    steps = [(j, c) for j in range(heads) for c in range(chunks)]
    fetches, stores = [], []
    for n, (j, c) in enumerate(steps):
        here = (j, pl.ds(c * high, high), slice(None))
        at = window(j, c)
        fetches.append([pltpu.make_async_copy(inputs[a].at[at], bufs[a].at[here], sems.at[n, a]) for a in range(4)])
        for f in fetches[-1]:
            f.start()
    fetch_expo.wait()
    for n, (j, c) in enumerate(steps):
        head = mine ^ j
        for f in fetches[n]:
            f.wait()
        for b in range(high // qrows):
            row = c * (high // qrows) + b
            here = pl.ds(row * qrows, qrows)
            for g in range(groups):
                lanes = pl.ds(g * qcol, qcol)
                grad = b2[j, here, lanes]
                new_first = 0.9 * b0[j, here, lanes] + 0.1 * grad
                new_second = 0.95 * b1[j, here, lanes] + 0.05 * grad * grad
                n1[j, here, lanes] = new_first
                n2[j, here, lanes] = new_second
                bottom = new_second * lax.rsqrt(new_second) + 1e-08
                inverse = pl.reciprocal(bottom, approx=True)
                inverse = inverse * (2.0 - bottom * inverse)
                corrected = 0.02 * new_first * inverse + b3[j, here, lanes]
                expo = jnp.full((1, qcol), expo_ref[row, head * groups + g], jnp.int32).astype(F32)
                most = CLIP * jnp.exp2(-expo)
                delta_outs[j][here, lanes] = jnp.clip(corrected, -most, most).astype(BF16)
        at = window(j, c)
        here = (j, pl.ds(c * high, high), slice(None))
        stores += [
            pltpu.make_async_copy(n1.at[here], new_first_out.at[at], sems.at[n, 4]),
            pltpu.make_async_copy(n2.at[here], new_second_out.at[at], sems.at[n, 5]),
        ]
        for s in stores[-2:]:
            s.start()
    for s in stores:
        s.wait()


def adam(arrays, exponent, heads, chunks=2):
    rows, full = arrays[0].shape
    qrows, qcol = rows // exponent.shape[0], full // exponent.shape[1]
    cols = full // heads
    chunks = min(chunks, rows // qrows)
    return pl.pallas_call(
        functools.partial(adam_kernel, chunks, qrows, qcol, heads),
        in_specs=[FAR] * 5,
        out_specs=[FAR] * 2 + [NEAR] * heads,
        out_shape=[like((rows, full), F32)] * 2 + [like((rows, cols), BF16)] * heads,
        scratch_shapes=[pltpu.VMEM((heads, rows, cols), F32)] * 6
        + [
            pltpu.SMEM(exponent.shape, jnp.int32),
            pltpu.SemaphoreType.DMA((heads * chunks, 6)),
            pltpu.SemaphoreType.DMA(()),
        ],
        compiler_params=pltpu.CompilerParams(vmem_limit_bytes=20 * MIB),
        cost_estimate=FREE,
    )(*[far(x) for x in (exponent, *arrays)])


def place_rows(refs, heads, rows):
    core, mine = lax.axis_index("dp") % PAIR, lax.axis_index("tensor")
    for n, ref in enumerate(refs):
        at = ((core ^ (n // heads)) * heads + (mine ^ (n % heads))) * rows
        yield ref, pl.ds(pl.multiple_of(at, rows), rows)


def multiply(piece_refs, weight, out_refs):
    rows = out_refs[0].shape[0]
    stacked = jnp.concatenate([r[...] for r in piece_refs], axis=0)
    total = jnp.dot(stacked, weight, preferred_element_type=F32)
    for k, out_ref in enumerate(out_refs):
        out_ref[...] = total[k * rows : (k + 1) * rows].astype(out_ref.dtype)


def merge_kernel(slabs, heads, stale_ref, *refs):
    delta_refs, piece_refs = refs[: PAIR * heads], refs[PAIR * heads : PAIR * heads + slabs]
    weight_ref, out_refs = refs[PAIR * heads + slabs], refs[PAIR * heads + slabs + 1 :]
    for ref, here in place_rows(delta_refs, heads, delta_refs[0].shape[0]):
        weight_ref[here, :] = (stale_ref[here, :].astype(F32) + ref[...].astype(F32)).astype(BF16)
    multiply(piece_refs, weight_ref[...], out_refs)


def product_kernel(joined_ref, weight_ref, *out_refs):
    multiply([joined_ref], weight_ref[...], out_refs)


def merge_product(stale, deltas, pieces, heads, types):
    depth, cols = stale.shape
    return pl.pallas_call(
        functools.partial(merge_kernel, len(pieces), heads),
        out_shape=[like((depth, cols), BF16)] + [like((p.shape[0], cols), t) for p, t in zip(pieces, types)],
        compiler_params=pltpu.CompilerParams(vmem_limit_bytes=16 * MIB),
        cost_estimate=FREE,
    )(*[near_by(x) for x in (stale, *deltas, *pieces)])


def product(joined, weight, types):
    count = len(types)
    return pl.pallas_call(
        product_kernel,
        out_shape=[like((joined.shape[0] // count, weight.shape[1]), t) for t in types],
        compiler_params=pltpu.CompilerParams(vmem_limit_bytes=12 * MIB),
        cost_estimate=FREE,
    )(near_by(joined), near_by(weight))


def on_device(tokens, gain, stale, bias, first, second, grad, residual, exponent):
    heads = lax.axis_size("tensor")
    replicas = lax.axis_size("dp")
    slabs = replicas // PAIR
    partners = slabs // PAIR
    near, remote = range(partners // 2), range(partners // 2, partners)
    slab, core, mine = lax.axis_index("dp") // PAIR, lax.axis_index("dp") % PAIR, lax.axis_index("tensor")
    height = tokens.shape[0]

    def over_tensor(x, j):
        return x if j == 0 else lax.ppermute(x, "tensor", [(i, i ^ j) for i in range(heads)])

    def over_core(x):
        return lax.ppermute(x, "dp", [(i, i ^ 1) for i in range(replicas)])

    def over_slab(x, m):
        pairs = [(i, ((i // PAIR) ^ apart(m, i % PAIR)) * PAIR + i % PAIR) for i in range(replicas)]
        return lax.ppermute(x, "dp", pairs)

    def over_next(x):
        return lax.ppermute(x, "dp", [(i, i ^ PAIR) for i in range(replicas)])

    beside = over_core(tokens)
    new_first, new_second, *deltas = adam((first, second, grad, residual), exponent, heads)
    *deltas, beside = lax.optimization_barrier((*deltas, beside))
    owned = [over_tensor(deltas[j], j) for j in range(heads)]
    normed = norm(tokens, beside, gain, slabs)
    order = (*remote, *near)
    pieces = [over_slab(normed[m], m) for m in order]
    depth = stale.shape[0] // slabs
    held = lax.dynamic_slice_in_dim(stale, slab * depth, depth, axis=0)
    beside_ours = over_core(owned[0])
    held, pieces = lax.optimization_barrier((held, pieces))
    pieces = dict(zip(order, pieces))

    def over_heads(group):
        joined = jnp.concatenate([pieces[m] for m in group], axis=0)
        return [over_tensor(joined, j) for j in range(1, heads)]

    moved = over_heads(order)
    shared = owned + [beside_ours] + [over_core(x) for x in owned[1:]]
    def through_next(parts, group):
        met = over_next(jnp.concatenate(parts[1::2], axis=0))
        tall = parts[0].shape[0]
        sums = [(x + met[i * tall : (i + 1) * tall].astype(F32)).astype(BF16) for i, x in enumerate(parts[::2])]
        return [over_slab(x, m) for x, m in zip(sums, group[::2])]

    mixed = [F32, BF16] * (partners // 2)
    weight, *parts = merge_product(held, shared, [pieces[m] for m in order], heads, mixed)
    terms = [through_next(parts, order)]
    for j in range(1, heads):
        terms.append(through_next(product(moved[j - 1], weight, mixed), order))

    totals = [sum(x.astype(F32) for x in row).reshape(PAIR, height, -1) for row in terms]
    total = jnp.stack(totals, axis=1)
    keep = jnp.where(core == 0, total[0], total[1])
    give = jnp.where(core == 0, total[1], total[0])
    results = (keep + over_core(give) + bias).astype(BF16)
    if heads == 2:
        ordered = jnp.where(mine == 0, results, results[::-1])
    else:
        ordered = jnp.take(results, jnp.arange(heads) ^ mine, axis=0)
    projected = ordered.reshape(-1, results.shape[-1])
    return (new_first, new_second, projected)


def solution(mesh):
    rows = P(("dp", "tensor"), None)
    return jax.shard_map(
        on_device,
        mesh=mesh,
        in_specs=(rows, P(), P(None, "tensor"), P("tensor"), rows, rows, rows, rows, rows),
        out_specs=(rows, rows, P("dp", "tensor")),
        check_vma=False,
    )
```

time: 62.4 us -> 59.9 us (0.960)
  starting transfers between devices: 40.5 us -> 18.3 us
  waiting for transfers between devices: 8.18 us -> 29.6 us
  Pallas kernels: 10.1 us -> 8.29 us
    ppermute x23 -> x14, starting transfers between devices: 35.4 us -> 15 us  [the longest x8 11.6 us: over_slab(): return lax.ppermute(x, 'dp', pairs)]
    ppermute x23 -> x14, waiting for transfers between devices: 8.17 us -> 19.7 us  [the longest x8 15.4 us: over_slab(): return lax.ppermute(x, 'dp', pairs)]
    ppermute x3 -> x2, waiting for transfers between devices: 0.01 us -> 9.94 us  [over_tensor(): lax.ppermute(x, 'tensor', [(i, i ^ j) for i in range(heads)])]
    ppermute x3 -> x2, starting transfers between devices: 5.14 us -> 3.22 us  [over_tensor(): lax.ppermute(x, 'tensor', [(i, i ^ j) for i in range(heads)])]
    pallas_call x4 -> x3, Pallas kernels: 8.36 us -> 6.56 us  [the longest x1 5.49 us: adam(): pl.pallas_call(functools.partial(adam_kernel, chunks, qrows, qcol, heads)...]
  transfers between devices with their start and end apart: 26 -> 16, of which waited for: 6 -> 7; matrix products, arithmetic and copies ran while one was open for 3% -> 3% of each run, Pallas kernels for 10% -> 14%
where the time goes in v2:
time: 59.9 us; the launch traced here: 59.7 us
  waiting for transfers between devices  29.6 us (49%)
  starting transfers between devices  18.3 us (31%)
  Pallas kernels  8.29 us (14%)
  local copies, waits for them, and re-layouts  1.78 us (3%)
  other arithmetic  1 us (2%)
  between operations  0.81 us (1%)
    ppermute x8, waiting for transfers between devices, over_slab(): return lax.ppermute(x, 'dp', pairs)  15.4 us
    ppermute x8, starting transfers between devices, over_slab(): return lax.ppermute(x, 'dp', pairs)  11.6 us
    ppermute x2, waiting for transfers between devices, over_tensor(): lax.ppermute(x, 'tensor', [(i, i ^ j) for i in range(heads)])  9.94 us
    pallas_call x1, Pallas kernels, adam(): pl.pallas_call(functools.partial(adam_kernel, chunks, qrows, qcol, heads)...  5.49 us
    ppermute x2, starting transfers between devices, over_tensor(): lax.ppermute(x, 'tensor', [(i, i ^ j) for i in range(heads)])  3.22 us
    ppermute x2, waiting for transfers between devices, over_next(): return lax.ppermute(x, 'dp', [(i, i ^ PAIR) for i in range(replicas)])  2.75 us
    ppermute x2, starting transfers between devices, over_next(): return lax.ppermute(x, 'dp', [(i, i ^ PAIR) for i in range(replicas)])  2.36 us
    dynamic_slice x1, local copies, waits for them, and re-layouts, on_device(): held = lax.dynamic_slice_in_dim(stale, slab * depth, depth, axis=0)  1.76 us
  transfers between devices with their start and end apart: 16, of which 7 were waited for; matrix products, arithmetic and copies ran while one was open for 3% of the time, Pallas kernels for 14%

profile of v2, /device:TPU:0, one launch (start us, length us, event | category | flops | bytes accessed | tf_op | source)
XLA Modules:
  0.0 59.7 jit_solution(4399005434293750805)
XLA Ops:
  0.6 0.0 copy-start
  0.6 0.0 copy-start.1
  0.7 0.5 collective-permute-start
  1.2 5.5 %shard_map.112 = (f32[256,2048]{1,0:T(8,128)}, f32[256,2048]{1,0:T(8,128)}, bf16[256,1024]{1,0:T(8,128)(2,1)S(1)}, bf16[256,1024]{1,0:T(8,128)(2,1)S(1)}) custom-call(s32[8,16]{1,0:T(8,128)} %refs_0_.1, f32[256,2048]{1,0:T(8,128)} %refs_1_.1, f32[256,2048]{1,0:T(8,128)} %refs_2_.1, f32[256,2048]{1,0:T(8,128)} %refs_3_.1, f32[256,2048]{1,0:T(8,128)} %refs_4_.1), custom_call_target="tpu_custom_call" | custom-call | tf_op jit(solution)/shard_map/pallas_call | solution.py:125
  6.7 0.0 collective-permute-done.theirs_ref
  6.7 2.6 %collective-permute-start.5 = (bf16[256,1024]{1,0:T(8,128)(2,1)S(1)}, bf16[256,1024]{1,0:T(8,128)(2,1)S(1)}, u32[]{:S(2)}, u32[]{:S(2)}) collective-permute-start(bf16[256,1024]{1,0:T(8,128)(2,1)S(1)} %get-tuple-element.39), channel_id=1, source_target_pairs={{0,1},{1,0},{2,3},{3,2},{4,5},{5,4},{6,7},{7,6},{8,9},{9,8},{10,11... | collective-permute-start | bytes 1572872 | tf_op jit(solution)/shard_map/ppermute | solution.py:198
  9.3 0.0 copy-done
  9.3 0.0 copy-done.1
  9.3 0.4 shard_map.113
  9.7 2.7 %collective-permute-start.1 = (bf16[64,1024]{1,0:T(8,128)(2,1)S(1)}, bf16[64,1024]{1,0:T(8,128)(2,1)S(1)}, u32[]{:S(2)}, u32[]{:S(2)}) collective-permute-start(bf16[64,1024]{1,0:T(8,128)(2,1)S(1)} %get-tuple-element.33), channel_id=1, source_target_pairs={{0,16},{2,26},{4,20},{6,30},{8,24},{10,18},{12,28},{14,22},{16,0},... | collective-permute-start | bytes 393224 | tf_op jit(solution)/shard_map/ppermute | solution.py:205
  12.3 1.3 %collective-permute-start.2 = (bf16[64,1024]{1,0:T(8,128)(2,1)S(1)}, bf16[64,1024]{1,0:T(8,128)(2,1)S(1)}, u32[]{:S(2)}, u32[]{:S(2)}) collective-permute-start(bf16[64,1024]{1,0:T(8,128)(2,1)S(1)} %get-tuple-element.34), channel_id=1, source_target_pairs={{0,20},{2,30},{4,16},{6,26},{8,28},{10,22},{12,24},{14,18},{16,4},... | collective-permute-start | bytes 393224 | tf_op jit(solution)/shard_map/ppermute | solution.py:205
  13.6 0.7 %collective-permute-start.3 = (bf16[64,1024]{1,0:T(8,128)(2,1)S(1)}, bf16[64,1024]{1,0:T(8,128)(2,1)S(1)}, u32[]{:S(2)}, u32[]{:S(2)}) collective-permute-start(bf16[64,1024]{1,0:T(8,128)(2,1)S(1)} %get-tuple-element.35), channel_id=1, source_target_pairs={{0,0},{2,10},{4,4},{6,14},{8,8},{10,2},{12,12},{14,6},{16,16},{18,... | collective-permute-start | bytes 393224 | tf_op jit(solution)/shard_map/ppermute | solution.py:205
  14.3 0.6 collective-permute-start.4
  14.9 7.7 %collective-permute-done.1.refs_4_ = bf16[64,1024]{1,0:T(8,128)(2,1)S(1)} collective-permute-done((bf16[64,1024]{1,0:T(8,128)(2,1)S(1)}, bf16[64,1024]{1,0:T(8,128)(2,1)S(1)}, u32[]{:S(2)}, u32[]{:S(2)}) %collective-permute-start.1) | collective-permute-done | bytes 131104 | tf_op jit(solution)/shard_map/ppermute | solution.py:205
  22.6 0.0 collective-permute-start.6
  22.6 0.0 collective-permute-done.5.refs_1_
  22.6 0.5 collective-permute-start.7
  23.1 1.8 %constant_dynamic-slice_fusion.stale_ref = bf16[1024,1024]{1,0:T(8,128)(2,1)S(1)} fusion(bf16[8192,1024]{1,0:T(8,128)(2,1)} %param.11, s32[]{:T(128)S(6)} %select_n.44), kind=kLoop, calls=%fused_computation.20 | loop fusion | bytes 4194308 | tf_op jit(solution)/shard_map/dynamic_slice | solution.py:218
  24.9 0.8 %collective-permute-done.2.refs_5_ = bf16[64,1024]{1,0:T(8,128)(2,1)S(1)} collective-permute-done((bf16[64,1024]{1,0:T(8,128)(2,1)S(1)}, bf16[64,1024]{1,0:T(8,128)(2,1)S(1)}, u32[]{:S(2)}, u32[]{:S(2)}) %collective-permute-start.2) | collective-permute-done | bytes 131104 | tf_op jit(solution)/shard_map/ppermute | solution.py:205
  25.7 0.0 collective-permute-done.3.refs_6_
  25.7 0.0 collective-permute-done.4.refs_7_
  25.7 0.6 %collective-permute-start.11 = (bf16[256,1024]{1,0:T(8,128)(2,1)S(1)}, bf16[256,1024]{1,0:T(8,128)(2,1)S(1)}, u32[]{:S(2)}, u32[]{:S(2)}) collective-permute-start(bf16[256,1024]{1,0:T(8,128)(2,1)S(1)} %pad_maximum_fusion), channel_id=1, source_target_pairs={{0,1},{1,0},{2,3},{3,2},{4,5},{5,4},{6,7},{7,6},{8,9},{9,8},{10,11... | collective-permute-start | bytes 1572872 | tf_op jit(solution)/shard_map/ppermute | solution.py:198
  26.3 0.0 collective-permute-done.6.refs_2_
  26.3 0.0 collective-permute-done.7.refs_3_
  26.4 1.7 %shard_map.114 = (bf16[1024,1024]{1,0:T(8,128)(2,1)S(1)}, f32[64,1024]{1,0:T(8,128)S(1)}, bf16[64,1024]{1,0:T(8,128)(2,1)S(1)}, f32[64,1024]{1,0:T(8,128)S(1)}, bf16[64,1024]{1,0:T(8,128)(2,1)S(1)}) custom-call(bf16[1024,1024]{1,0:T(8,128)(2,1)S(1)} %constant_dynamic-slice_fusion.stale_ref, bf16[256,1024]{1,0:T(8,128)(2,1)S(1)} %get-tuple-element.38.refs_0_, ...), custom_call_target="tpu_custom_call" | custom-call | tf_op jit(solution)/shard_map/pallas_call | solution.py:170
  28.1 0.8 %collective-permute-start.8 = (bf16[128,1024]{1,0:T(8,128)(2,1)S(1)}, bf16[128,1024]{1,0:T(8,128)(2,1)S(1)}, u32[]{:S(2)}, u32[]{:S(2)}) collective-permute-start(bf16[128,1024]{1,0:T(8,128)(2,1)S(1)} %pad_maximum_fusion.2), channel_id=1, source_target_pairs={{0,4},{2,6},{4,0},{6,2},{8,12},{10,14},{12,8},{14,10},{16,20},{18,... | collective-permute-start | bytes 786440 | tf_op jit(solution)/shard_map/ppermute | solution.py:208
  28.9 9.9 %collective-permute-done.11.joined_ref = bf16[256,1024]{1,0:T(8,128)(2,1)S(1)} collective-permute-done((bf16[256,1024]{1,0:T(8,128)(2,1)S(1)}, bf16[256,1024]{1,0:T(8,128)(2,1)S(1)}, u32[]{:S(2)}, u32[]{:S(2)}) %collective-permute-start.11) | collective-permute-done | bytes 524320 | tf_op jit(solution)/shard_map/ppermute | solution.py:198
  38.8 0.7 %shard_map.115 = (f32[64,1024]{1,0:T(8,128)S(1)}, bf16[64,1024]{1,0:T(8,128)(2,1)S(1)}, f32[64,1024]{1,0:T(8,128)S(1)}, bf16[64,1024]{1,0:T(8,128)(2,1)S(1)}) custom-call(bf16[256,1024]{1,0:T(8,128)(2,1)S(1)} %collective-permute-done.11.joined_ref, bf16[1024,1024]{1,0:T(8,128)(2,1)S(1)} %get-tuple-element.48.weight_ref), custom_call_target="tpu_custom_call" | custom-call | tf_op jit(solution)/shard_map/pallas_call | solution.py:180
  39.6 0.0 copy-start.2
  39.6 1.6 %collective-permute-start.12 = (bf16[128,1024]{1,0:T(8,128)(2,1)S(1)}, bf16[128,1024]{1,0:T(8,128)(2,1)S(1)}, u32[]{:S(2)}, u32[]{:S(2)}) collective-permute-start(bf16[128,1024]{1,0:T(8,128)(2,1)S(1)} %pad_maximum_fusion.3), channel_id=1, source_target_pairs={{0,4},{2,6},{4,0},{6,2},{8,12},{10,14},{12,8},{14,10},{16,20},{18,... | collective-permute-start | bytes 786440 | tf_op jit(solution)/shard_map/ppermute | solution.py:208
  41.2 0.0 collective-permute-done.8
  41.2 0.1 add_convert_fusion.3
  41.2 0.7 %collective-permute-start.10 = (bf16[64,1024]{1,0:T(8,128)(2,1)S(1)}, bf16[64,1024]{1,0:T(8,128)(2,1)S(1)}, u32[]{:S(2)}, u32[]{:S(2)}) collective-permute-start(bf16[64,1024]{1,0:T(8,128)(2,1)S(1)} %get-tuple-element.54), channel_id=1, source_target_pairs={{0,0},{2,10},{4,4},{6,14},{8,8},{10,2},{12,12},{14,6},{16,16},{18,... | collective-permute-start | bytes 393224 | tf_op jit(solution)/shard_map/ppermute | solution.py:205
  41.9 2.1 %collective-permute-start.9 = (bf16[64,1024]{1,0:T(8,128)(2,1)S(1)}, bf16[64,1024]{1,0:T(8,128)(2,1)S(1)}, u32[]{:S(2)}, u32[]{:S(2)}) collective-permute-start(bf16[64,1024]{1,0:T(8,128)(2,1)S(1)} %get-tuple-element.53), channel_id=1, source_target_pairs={{0,16},{2,26},{4,20},{6,30},{8,24},{10,18},{12,28},{14,22},{16,0},... | collective-permute-start | bytes 393224 | tf_op jit(solution)/shard_map/ppermute | solution.py:205
  44.0 2.7 %collective-permute-done.12 = bf16[128,1024]{1,0:T(8,128)(2,1)S(1)} collective-permute-done((bf16[128,1024]{1,0:T(8,128)(2,1)S(1)}, bf16[128,1024]{1,0:T(8,128)(2,1)S(1)}, u32[]{:S(2)}, u32[]{:S(2)}) %collective-permute-start.12) | collective-permute-done | bytes 262176 | tf_op jit(solution)/shard_map/ppermute | solution.py:208
  46.8 0.1 add_convert_fusion.1
  46.9 2.9 %collective-permute-start.13 = (bf16[64,1024]{1,0:T(8,128)(2,1)S(1)}, bf16[64,1024]{1,0:T(8,128)(2,1)S(1)}, u32[]{:S(2)}, u32[]{:S(2)}) collective-permute-start(bf16[64,1024]{1,0:T(8,128)(2,1)S(1)} %get-tuple-element.55), channel_id=1, source_target_pairs={{0,16},{2,26},{4,20},{6,30},{8,24},{10,18},{12,28},{14,22},{16,0},... | collective-permute-start | bytes 393224 | tf_op jit(solution)/shard_map/ppermute | solution.py:205
  49.8 0.7 %collective-permute-start.14 = (bf16[64,1024]{1,0:T(8,128)(2,1)S(1)}, bf16[64,1024]{1,0:T(8,128)(2,1)S(1)}, u32[]{:S(2)}, u32[]{:S(2)}) collective-permute-start(bf16[64,1024]{1,0:T(8,128)(2,1)S(1)} %get-tuple-element.56), channel_id=1, source_target_pairs={{0,0},{2,10},{4,4},{6,14},{8,8},{10,2},{12,12},{14,6},{16,16},{18,... | collective-permute-start | bytes 393224 | tf_op jit(solution)/shard_map/ppermute | solution.py:205
  50.5 0.0 collective-permute-done.10
  50.5 2.6 %collective-permute-done.9 = bf16[64,1024]{1,0:T(8,128)(2,1)S(1)} collective-permute-done((bf16[64,1024]{1,0:T(8,128)(2,1)S(1)}, bf16[64,1024]{1,0:T(8,128)(2,1)S(1)}, u32[]{:S(2)}, u32[]{:S(2)}) %collective-permute-start.9) | collective-permute-done | bytes 131104 | tf_op jit(solution)/shard_map/ppermute | solution.py:205
  53.1 4.2 %collective-permute-done.13 = bf16[64,1024]{1,0:T(8,128)(2,1)S(1)} collective-permute-done((bf16[64,1024]{1,0:T(8,128)(2,1)S(1)}, bf16[64,1024]{1,0:T(8,128)(2,1)S(1)}, u32[]{:S(2)}, u32[]{:S(2)}) %collective-permute-start.13) | collective-permute-done | bytes 131104 | tf_op jit(solution)/shard_map/ppermute | solution.py:205
  57.3 0.0 collective-permute-done.14
  57.4 0.1 collective-permute-start.15
  57.5 1.5 %collective-permute-done.15 = f32[2,32,1024]{2,1,0:T(8,128)S(1)} collective-permute-done((f32[2,32,1024]{2,1,0:T(8,128)S(1)}, f32[2,32,1024]{2,1,0:T(8,128)S(1)}, u32[]{:S(2)}, u32[]{:S(2)}) %collective-permute-start.15) | collective-permute-done | bytes 262176 | tf_op jit(solution)/shard_map/ppermute | solution.py:201
  59.0 0.0 copy-done.2
  59.1 0.7 %reverse_select_fusion = bf16[2,32,1024]{2,1,0:T(8,128)(2,1)} fusion(bf16[2,32,1024]{2,1,0:T(8,128)(2,1)S(1)} %fusion.4, pred[]{:T(512)S(6)} %eq.9), kind=kLoop, calls=%fused_computation.19 | loop fusion | flops 65536 | bytes 262145 | tf_op jit(solution)/shard_map/jit(_where)/select_n | solution.py:247
  (7 shorter events, 0.2 us)
Async XLA Ops:
  0.6 8.7 %copy-start = (bf16[32,8192]{1,0:T(8,128)(2,1)S(1)}, bf16[32,8192]{1,0:T(8,128)(2,1)}, u32[]{:S(2)}) copy-start(bf16[32,8192]{1,0:T(8,128)(2,1)} %ours_ref.1) | copy-start | bytes 1572868
  0.6 8.7 %copy-start.1 = (f32[8192]{0:T(1024)S(1)}, f32[8192]{0:T(1024)}, u32[]{:S(2)}) copy-start(f32[8192]{0:T(1024)} %param.10) | copy-start | bytes 98308
  0.7 6.0 %collective-permute-start = (bf16[32,8192]{1,0:T(8,128)(2,1)}, bf16[32,8192]{1,0:T(8,128)(2,1)S(1)}, u32[]{:S(2)}, u32[]{:S(2)}) collective-permute-start(bf16[32,8192]{1,0:T(8,128)(2,1)} %ours_ref.1), channel_id=1, source_target_pairs={{0,2},{2,0},{4,6},{6,4},{8,10},{10,8},{12,14},{14,12},{16,18},{18,... | collective-permute-start | bytes 1572872 | tf_op jit(solution)/shard_map/ppermute | solution.py:201
  6.7 15.9 %collective-permute-start.5 = (bf16[256,1024]{1,0:T(8,128)(2,1)S(1)}, bf16[256,1024]{1,0:T(8,128)(2,1)S(1)}, u32[]{:S(2)}, u32[]{:S(2)}) collective-permute-start(bf16[256,1024]{1,0:T(8,128)(2,1)S(1)} %get-tuple-element.39), channel_id=1, source_target_pairs={{0,1},{1,0},{2,3},{3,2},{4,5},{5,4},{6,7},{7,6},{8,9},{9,8},{10,11... | collective-permute-start | bytes 1572872 | tf_op jit(solution)/shard_map/ppermute | solution.py:198
  9.7 12.9 %collective-permute-start.1 = (bf16[64,1024]{1,0:T(8,128)(2,1)S(1)}, bf16[64,1024]{1,0:T(8,128)(2,1)S(1)}, u32[]{:S(2)}, u32[]{:S(2)}) collective-permute-start(bf16[64,1024]{1,0:T(8,128)(2,1)S(1)} %get-tuple-element.33), channel_id=1, source_target_pairs={{0,16},{2,26},{4,20},{6,30},{8,24},{10,18},{12,28},{14,22},{16,0},... | collective-permute-start | bytes 393224 | tf_op jit(solution)/shard_map/ppermute | solution.py:205
  12.3 13.4 %collective-permute-start.2 = (bf16[64,1024]{1,0:T(8,128)(2,1)S(1)}, bf16[64,1024]{1,0:T(8,128)(2,1)S(1)}, u32[]{:S(2)}, u32[]{:S(2)}) collective-permute-start(bf16[64,1024]{1,0:T(8,128)(2,1)S(1)} %get-tuple-element.34), channel_id=1, source_target_pairs={{0,20},{2,30},{4,16},{6,26},{8,28},{10,22},{12,24},{14,18},{16,4},... | collective-permute-start | bytes 393224 | tf_op jit(solution)/shard_map/ppermute | solution.py:205
  13.6 12.1 %collective-permute-start.3 = (bf16[64,1024]{1,0:T(8,128)(2,1)S(1)}, bf16[64,1024]{1,0:T(8,128)(2,1)S(1)}, u32[]{:S(2)}, u32[]{:S(2)}) collective-permute-start(bf16[64,1024]{1,0:T(8,128)(2,1)S(1)} %get-tuple-element.35), channel_id=1, source_target_pairs={{0,0},{2,10},{4,4},{6,14},{8,8},{10,2},{12,12},{14,6},{16,16},{18,... | collective-permute-start | bytes 393224 | tf_op jit(solution)/shard_map/ppermute | solution.py:205
  14.3 11.4 %collective-permute-start.4 = (bf16[64,1024]{1,0:T(8,128)(2,1)S(1)}, bf16[64,1024]{1,0:T(8,128)(2,1)S(1)}, u32[]{:S(2)}, u32[]{:S(2)}) collective-permute-start(bf16[64,1024]{1,0:T(8,128)(2,1)S(1)} %get-tuple-element.36), channel_id=1, source_target_pairs={{0,4},{2,14},{4,0},{6,10},{8,12},{10,6},{12,8},{14,2},{16,20},{18,... | collective-permute-start | bytes 393224 | tf_op jit(solution)/shard_map/ppermute | solution.py:205
  22.6 3.8 %collective-permute-start.6 = (bf16[256,1024]{1,0:T(8,128)(2,1)S(1)}, bf16[256,1024]{1,0:T(8,128)(2,1)S(1)}, u32[]{:S(2)}, u32[]{:S(2)}) collective-permute-start(bf16[256,1024]{1,0:T(8,128)(2,1)S(1)} %get-tuple-element.38.refs_0_), channel_id=1, source_target_pairs={{0,2},{2,0},{4,6},{6,4},{8,10},{10,8},{12,14},{14,12},{16,18},{18,... | collective-permute-start | bytes 1572872 | tf_op jit(solution)/shard_map/ppermute | solution.py:201
  22.6 3.8 %collective-permute-start.7 = (bf16[256,1024]{1,0:T(8,128)(2,1)S(1)}, bf16[256,1024]{1,0:T(8,128)(2,1)S(1)}, u32[]{:S(2)}, u32[]{:S(2)}) collective-permute-start(bf16[256,1024]{1,0:T(8,128)(2,1)S(1)} %collective-permute-done.5.refs_1_), channel_id=1, source_target_pairs={{0,2},{2,0},{4,6},{6,4},{8,10},{10,8},{12,14},{14,12},{16,18},{18,... | collective-permute-start | bytes 1572872 | tf_op jit(solution)/shard_map/ppermute | solution.py:201
  25.7 13.1 %collective-permute-start.11 = (bf16[256,1024]{1,0:T(8,128)(2,1)S(1)}, bf16[256,1024]{1,0:T(8,128)(2,1)S(1)}, u32[]{:S(2)}, u32[]{:S(2)}) collective-permute-start(bf16[256,1024]{1,0:T(8,128)(2,1)S(1)} %pad_maximum_fusion), channel_id=1, source_target_pairs={{0,1},{1,0},{2,3},{3,2},{4,5},{5,4},{6,7},{7,6},{8,9},{9,8},{10,11... | collective-permute-start | bytes 1572872 | tf_op jit(solution)/shard_map/ppermute | solution.py:198
  28.1 13.1 %collective-permute-start.8 = (bf16[128,1024]{1,0:T(8,128)(2,1)S(1)}, bf16[128,1024]{1,0:T(8,128)(2,1)S(1)}, u32[]{:S(2)}, u32[]{:S(2)}) collective-permute-start(bf16[128,1024]{1,0:T(8,128)(2,1)S(1)} %pad_maximum_fusion.2), channel_id=1, source_target_pairs={{0,4},{2,6},{4,0},{6,2},{8,12},{10,14},{12,8},{14,10},{16,20},{18,... | collective-permute-start | bytes 786440 | tf_op jit(solution)/shard_map/ppermute | solution.py:208
  39.6 19.4 %copy-start.2 = (f32[1024]{0:T(1024)S(1)}, f32[1024]{0:T(1024)}, u32[]{:S(2)}) copy-start(f32[1024]{0:T(1024)} %param.12) | copy-start | bytes 12292
  39.6 7.2 %collective-permute-start.12 = (bf16[128,1024]{1,0:T(8,128)(2,1)S(1)}, bf16[128,1024]{1,0:T(8,128)(2,1)S(1)}, u32[]{:S(2)}, u32[]{:S(2)}) collective-permute-start(bf16[128,1024]{1,0:T(8,128)(2,1)S(1)} %pad_maximum_fusion.3), channel_id=1, source_target_pairs={{0,4},{2,6},{4,0},{6,2},{8,12},{10,14},{12,8},{14,10},{16,20},{18,... | collective-permute-start | bytes 786440 | tf_op jit(solution)/shard_map/ppermute | solution.py:208
  41.2 9.2 %collective-permute-start.10 = (bf16[64,1024]{1,0:T(8,128)(2,1)S(1)}, bf16[64,1024]{1,0:T(8,128)(2,1)S(1)}, u32[]{:S(2)}, u32[]{:S(2)}) collective-permute-start(bf16[64,1024]{1,0:T(8,128)(2,1)S(1)} %get-tuple-element.54), channel_id=1, source_target_pairs={{0,0},{2,10},{4,4},{6,14},{8,8},{10,2},{12,12},{14,6},{16,16},{18,... | collective-permute-start | bytes 393224 | tf_op jit(solution)/shard_map/ppermute | solution.py:205
  41.9 11.2 %collective-permute-start.9 = (bf16[64,1024]{1,0:T(8,128)(2,1)S(1)}, bf16[64,1024]{1,0:T(8,128)(2,1)S(1)}, u32[]{:S(2)}, u32[]{:S(2)}) collective-permute-start(bf16[64,1024]{1,0:T(8,128)(2,1)S(1)} %get-tuple-element.53), channel_id=1, source_target_pairs={{0,16},{2,26},{4,20},{6,30},{8,24},{10,18},{12,28},{14,22},{16,0},... | collective-permute-start | bytes 393224 | tf_op jit(solution)/shard_map/ppermute | solution.py:205
  46.9 10.5 %collective-permute-start.13 = (bf16[64,1024]{1,0:T(8,128)(2,1)S(1)}, bf16[64,1024]{1,0:T(8,128)(2,1)S(1)}, u32[]{:S(2)}, u32[]{:S(2)}) collective-permute-start(bf16[64,1024]{1,0:T(8,128)(2,1)S(1)} %get-tuple-element.55), channel_id=1, source_target_pairs={{0,16},{2,26},{4,20},{6,30},{8,24},{10,18},{12,28},{14,22},{16,0},... | collective-permute-start | bytes 393224 | tf_op jit(solution)/shard_map/ppermute | solution.py:205
  49.8 7.5 %collective-permute-start.14 = (bf16[64,1024]{1,0:T(8,128)(2,1)S(1)}, bf16[64,1024]{1,0:T(8,128)(2,1)S(1)}, u32[]{:S(2)}, u32[]{:S(2)}) collective-permute-start(bf16[64,1024]{1,0:T(8,128)(2,1)S(1)} %get-tuple-element.56), channel_id=1, source_target_pairs={{0,0},{2,10},{4,4},{6,14},{8,8},{10,2},{12,12},{14,6},{16,16},{18,... | collective-permute-start | bytes 393224 | tf_op jit(solution)/shard_map/ppermute | solution.py:205
  57.4 1.6 %collective-permute-start.15 = (f32[2,32,1024]{2,1,0:T(8,128)S(1)}, f32[2,32,1024]{2,1,0:T(8,128)S(1)}, u32[]{:S(2)}, u32[]{:S(2)}) collective-permute-start(f32[2,32,1024]{2,1,0:T(8,128)S(1)} %select_bitcast_fusion), channel_id=1, source_target_pairs={{0,2},{2,0},{4,6},{6,4},{8,10},{10,8},{12,14},{14,12},{16,18},{18,... | collective-permute-start | bytes 786440 | tf_op jit(solution)/shard_map/ppermute | solution.py:201

commit v3 on v2

v3 whole, which is shorter than its diff:
```python
import functools

import jax
import jax.numpy as jnp
from jax import lax
from jax.experimental import pallas as pl
from jax.experimental.pallas import tpu as pltpu
from jax.sharding import PartitionSpec as P

PAIR = 2
CLIP = 448.0
MIB = 1024 * 1024
F32 = jnp.float32
BF16 = jnp.bfloat16
FAR = pl.BlockSpec(memory_space=pltpu.HBM)
NEAR = pl.BlockSpec(memory_space=pltpu.VMEM)
FREE = pl.CostEstimate(flops=0, bytes_accessed=0, transcendentals=0)


def far(x):
    return pltpu.with_memory_space_constraint(x, pltpu.HBM)


def near_by(x):
    return pltpu.with_memory_space_constraint(x, pltpu.VMEM)


def like(shape, dtype):
    return jax.ShapeDtypeStruct(shape, dtype)


def apart(m, core):
    return (m // 2) * 4 + core * 2 + m % 2


def norm_kernel(ours_ref, theirs_ref, gain_ref, *piece_refs):
    dp = lax.axis_index("dp")
    slab, core = dp // PAIR, dp % PAIR
    height = ours_ref.shape[0]
    width = piece_refs[0].shape[1]
    for turn, ref in enumerate((ours_ref, theirs_ref)):
        values = ref[...].astype(F32)
        scale = lax.rsqrt(jnp.mean(values * values, axis=1, keepdims=True) + 1e-06)
        rows = pl.ds(pl.multiple_of((core ^ turn) * height, height), height)
        for m, piece_ref in enumerate(piece_refs):
            columns = pl.ds(pl.multiple_of((slab ^ apart(m, core)) * width, width), width)
            piece_ref[rows, :] = (ref[:, columns].astype(F32) * scale * gain_ref[:, columns]).astype(BF16)


def norm(ours, theirs, gain, slabs):
    height, features = ours.shape
    return pl.pallas_call(
        norm_kernel,
        out_shape=[like((PAIR * height, features // slabs), BF16)] * (slabs // PAIR),
        compiler_params=pltpu.CompilerParams(vmem_limit_bytes=8 * MIB),
        cost_estimate=FREE,
    )(*[near_by(x) for x in (ours, theirs, gain.reshape(1, features))])


def step(first, second, grad):
    return 0.9 * first + 0.1 * grad, 0.95 * second + 0.05 * grad * grad


def delta_kernel(chunks, qrows, qcol, heads, start, count, *refs):
    expo_far, *inputs = refs[:5]
    delta_outs, (b0, b1, b2, b3, expo_ref, sems, expo_sem) = refs[5 : 5 + count], refs[5 + count :]
    bufs = (b0, b1, b2, b3)
    mine = lax.axis_index("tensor")
    rows = inputs[0].shape[0]
    cols = inputs[0].shape[1] // heads
    groups = cols // qcol
    high = rows // chunks
    fetch_expo = pltpu.make_async_copy(expo_far, expo_ref, expo_sem)
    fetch_expo.start()
    turns = [(j, c) for j in range(count) for c in range(chunks)]
    fetches = []
    for n, (j, c) in enumerate(turns):
        here = (j, pl.ds(c * high, high), slice(None))
        at = pl.ds(c * high, high), pl.ds(pl.multiple_of((mine ^ (start + j)) * cols, cols), cols)
        fetches.append([pltpu.make_async_copy(inputs[a].at[at], bufs[a].at[here], sems.at[n, a]) for a in range(4)])
        for f in fetches[-1]:
            f.start()
    fetch_expo.wait()
    for n, (j, c) in enumerate(turns):
        for f in fetches[n]:
            f.wait()
        for b in range(high // qrows):
            row = c * (high // qrows) + b
            here = pl.ds(row * qrows, qrows)
            for g in range(groups):
                lanes = pl.ds(g * qcol, qcol)
                new_first, new_second = step(b0[j, here, lanes], b1[j, here, lanes], b2[j, here, lanes])
                bottom = new_second * lax.rsqrt(new_second) + 1e-08
                inverse = pl.reciprocal(bottom, approx=True)
                inverse = inverse * (2.0 - bottom * inverse)
                corrected = 0.02 * new_first * inverse + b3[j, here, lanes]
                expo = jnp.full((1, qcol), expo_ref[row, (mine ^ (start + j)) * groups + g], jnp.int32).astype(F32)
                most = CLIP * jnp.exp2(-expo)
                delta_outs[j][here, lanes] = jnp.clip(corrected, -most, most).astype(BF16)


def delta(arrays, exponent, heads, start, count, chunks=2):
    rows, full = arrays[0].shape
    qrows, qcol = rows // exponent.shape[0], full // exponent.shape[1]
    cols = full // heads
    chunks = min(chunks, rows // qrows)
    return pl.pallas_call(
        functools.partial(delta_kernel, chunks, qrows, qcol, heads, start, count),
        in_specs=[FAR] * 5,
        out_specs=[NEAR] * count,
        out_shape=[like((rows, cols), BF16)] * count,
        scratch_shapes=[pltpu.VMEM((count, rows, cols), F32)] * 4
        + [
            pltpu.SMEM(exponent.shape, jnp.int32),
            pltpu.SemaphoreType.DMA((count * chunks, 4)),
            pltpu.SemaphoreType.DMA(()),
        ],
        compiler_params=pltpu.CompilerParams(vmem_limit_bytes=16 * MIB),
        cost_estimate=FREE,
    )(*[far(x) for x in (exponent, *arrays)])


def moments_kernel(chunks, *refs):
    inputs, outs, bufs, sems = refs[:3], refs[3:5], refs[5:10], refs[10]
    high = inputs[0].shape[0] // chunks
    at = [pl.ds(c * high, high) for c in range(chunks)]
    fetches = [[pltpu.make_async_copy(inputs[a].at[r], bufs[a].at[r], sems.at[c, a]) for a in range(3)] for c, r in enumerate(at)]
    stores = [[pltpu.make_async_copy(bufs[3 + a].at[r], outs[a].at[r], sems.at[c, 3 + a]) for a in range(2)] for c, r in enumerate(at)]
    for row in fetches:
        for f in row:
            f.start()
    for c, r in enumerate(at):
        for f in fetches[c]:
            f.wait()
        bufs[3][r, :], bufs[4][r, :] = step(bufs[0][r, :], bufs[1][r, :], bufs[2][r, :])
        for s in stores[c]:
            s.start()
    for row in stores:
        for s in row:
            s.wait()


def moments(first, second, grad, chunks=4):
    rows, full = first.shape
    chunks = min(chunks, rows // 8)
    return pl.pallas_call(
        functools.partial(moments_kernel, chunks),
        in_specs=[FAR] * 3,
        out_specs=[FAR] * 2,
        out_shape=[like((rows, full), F32)] * 2,
        scratch_shapes=[pltpu.VMEM((rows, full), F32)] * 5 + [pltpu.SemaphoreType.DMA((chunks, 5))],
        compiler_params=pltpu.CompilerParams(vmem_limit_bytes=16 * MIB),
        cost_estimate=pl.CostEstimate(flops=0, bytes_accessed=60 * rows * full, transcendentals=0),
    )(far(first), far(second), far(grad))


def multiply(piece_refs, weight, out_refs):
    rows = out_refs[0].shape[0]
    stacked = jnp.concatenate([r[...] for r in piece_refs], axis=0)
    total = jnp.dot(stacked, weight, preferred_element_type=F32)
    for k, out_ref in enumerate(out_refs):
        out_ref[...] = total[k * rows : (k + 1) * rows].astype(out_ref.dtype)


def merge_kernel(slabs, heads, stale_far, *refs):
    blocks = PAIR * heads
    delta_refs, piece_refs = refs[:blocks], refs[blocks : blocks + slabs]
    weight_ref, *out_refs, stale_ref, sems = refs[blocks + slabs :]
    dp, mine = lax.axis_index("dp"), lax.axis_index("tensor")
    rows = delta_refs[0].shape[0]
    fetches, places = [], []
    for n in range(blocks):
        at = ((dp % PAIR ^ (n // heads)) * heads + (mine ^ (n % heads))) * rows
        first = (dp // PAIR) * (blocks * rows) + at
        source = stale_far.at[pl.ds(pl.multiple_of(first, rows), rows), :]
        fetches.append(pltpu.make_async_copy(source, stale_ref.at[n], sems.at[n]))
        places.append(pl.ds(pl.multiple_of(at, rows), rows))
        fetches[-1].start()
    for n, here in enumerate(places):
        fetches[n].wait()
        weight_ref[here, :] = (stale_ref[n].astype(F32) + delta_refs[n][...].astype(F32)).astype(BF16)
    multiply(piece_refs, weight_ref[...], out_refs)


def product_kernel(groups, *refs):
    multiply(refs[:groups], refs[groups][...], refs[groups + 1 :])


def merge_product(stale, deltas, pieces, heads, types):
    rows, cols = deltas[0].shape
    blocks = len(deltas)
    return pl.pallas_call(
        functools.partial(merge_kernel, len(pieces), heads),
        in_specs=[FAR] + [NEAR] * (blocks + len(pieces)),
        out_shape=[like((blocks * rows, cols), BF16)]
        + [like((p.shape[0], cols), t) for p, t in zip(pieces, types)],
        scratch_shapes=[pltpu.VMEM((blocks, rows, cols), BF16), pltpu.SemaphoreType.DMA((blocks,))],
        compiler_params=pltpu.CompilerParams(vmem_limit_bytes=16 * MIB),
        cost_estimate=pl.CostEstimate(flops=0, bytes_accessed=8 * blocks * rows * cols, transcendentals=0),
    )(far(stale), *[near_by(x) for x in (*deltas, *pieces)])


def product(groups, weight, types):
    rows = sum(g.shape[0] for g in groups) // len(types)
    return pl.pallas_call(
        functools.partial(product_kernel, len(groups)),
        out_shape=[like((rows, weight.shape[1]), t) for t in types],
        compiler_params=pltpu.CompilerParams(vmem_limit_bytes=12 * MIB),
        cost_estimate=FREE,
    )(*[near_by(x) for x in (*groups, weight)])


def on_device(tokens, gain, stale, bias, first, second, grad, residual, exponent):
    heads = lax.axis_size("tensor")
    replicas = lax.axis_size("dp")
    slabs = replicas // PAIR
    partners = slabs // PAIR
    near, remote = range(partners // 2), range(partners // 2, partners)
    core, mine = lax.axis_index("dp") % PAIR, lax.axis_index("tensor")
    height = tokens.shape[0]

    def over_tensor(x, j):
        return x if j == 0 else lax.ppermute(x, "tensor", [(i, i ^ j) for i in range(heads)])

    def over_core(x):
        return lax.ppermute(x, "dp", [(i, i ^ 1) for i in range(replicas)])

    def over_slab(x, m):
        pairs = [(i, ((i // PAIR) ^ apart(m, i % PAIR)) * PAIR + i % PAIR) for i in range(replicas)]
        return lax.ppermute(x, "dp", pairs)

    def over_next(x):
        return lax.ppermute(x, "dp", [(i, i ^ PAIR) for i in range(replicas)])

    beside = over_core(tokens)
    arrays = (first, second, grad, residual)
    theirs = delta(arrays, exponent, heads, 1, heads - 1)
    theirs, beside = lax.optimization_barrier((theirs, beside))
    arrived = [over_tensor(theirs[j], j + 1) for j in range(heads - 1)]
    normed = norm(tokens, beside, gain, slabs)
    order = (*remote, *near)
    pieces = [over_slab(normed[m], m) for m in order]
    exponent, normed = lax.optimization_barrier((exponent, normed))
    ours = delta(arrays, exponent, heads, 0, 1)
    distant, close = pieces[: len(remote)], pieces[len(remote) :]

    def over_heads(group):
        return [[over_tensor(x, j) for x in group] for j in range(1, heads)]

    ours, close = lax.optimization_barrier((ours, close))
    moved_close = over_heads(close)
    distant, arrived, moved_close = lax.optimization_barrier((distant, arrived, moved_close))
    moved_distant = over_heads([jnp.concatenate(distant, axis=0)])
    shared = [*ours, *arrived]
    shared = shared + [over_core(x) for x in shared]
    pieces = dict(zip(order, (*distant, *close)))

    def added(parts, met):
        tall = parts[0].shape[0]
        return [(x + met[i * tall : (i + 1) * tall].astype(F32)).astype(BF16) for i, x in enumerate(parts[::2])]

    mixed = [F32, BF16] * (partners // 2)
    weight, *parts = merge_product(stale, shared, [pieces[m] for m in order], heads, mixed)
    met = over_next(jnp.concatenate(parts[1::2], axis=0))
    met, moved_distant = lax.optimization_barrier((met, moved_distant))
    rows = [(parts, met)]
    for j in range(1, heads):
        parts = product([*moved_distant[j - 1], *moved_close[j - 1]], weight, mixed)
        rows.append((parts, over_next(jnp.concatenate(parts[1::2], axis=0))))
    terms = [[over_slab(x, m) for x, m in zip(added(*row), order[::2])] for row in rows]
    new_first, new_second = moments(first, second, grad)
    new_first, new_second, terms = lax.optimization_barrier((new_first, new_second, terms))

    totals = [sum(x.astype(F32) for x in row).reshape(PAIR, height, -1) for row in terms]
    total = jnp.stack(totals, axis=1)
    keep = jnp.where(core == 0, total[0], total[1])
    give = jnp.where(core == 0, total[1], total[0])
    results = (keep + over_core(give) + bias).astype(BF16)
    if heads == 2:
        ordered = jnp.where(mine == 0, results, results[::-1])
    else:
        ordered = jnp.take(results, jnp.arange(heads) ^ mine, axis=0)
    projected = ordered.reshape(-1, results.shape[-1])
    return (new_first, new_second, projected)


def solution(mesh):
    rows = P(("dp", "tensor"), None)
    return jax.shard_map(
        on_device,
        mesh=mesh,
        in_specs=(rows, P(), P(None, "tensor"), P("tensor"), rows, rows, rows, rows, rows),
        out_specs=(rows, rows, P("dp", "tensor")),
        check_vma=False,
    )
```

time: 59.9 us -> 57.1 us (0.953)
  waiting for transfers between devices: 29.6 us -> 14.3 us
  starting transfers between devices: 18.3 us -> 27 us
  Pallas kernels: 8.29 us -> 13.8 us
  local copies, waits for them, and re-layouts: 1.78 us -> 0.01 us
    ppermute x8, waiting for transfers between devices: 15.4 us -> 3.64 us  [over_slab(): return lax.ppermute(x, 'dp', pairs)]
    ppermute x2 -> x4, waiting for transfers between devices: 9.94 us -> 2.86 us  [over_tensor(): lax.ppermute(x, 'tensor', [(i, i ^ j) for i in range(heads)])]
    pallas_call x3 -> x5, Pallas kernels: 7.92 us -> 13.4 us  [the longest x2 5.2 us: delta(): pl.pallas_call(functools.partial(delta_kernel, chunks, qrows, qcol, heads...]
    ppermute x4, starting transfers between devices: 1.1 us -> 4.99 us  [over_core(): return lax.ppermute(x, 'dp', [(i, i ^ 1) for i in range(replicas)])]
    ppermute x2, waiting for transfers between devices: 2.75 us -> 6.55 us  [over_next(): return lax.ppermute(x, 'dp', [(i, i ^ PAIR) for i in range(replicas)])]
    ppermute x2 -> x4, starting transfers between devices: 3.22 us -> 6.72 us  [over_tensor(): lax.ppermute(x, 'tensor', [(i, i ^ j) for i in range(heads)])]
    dynamic_slice x1 -> x0, local copies, waits for them, and re-layouts: 1.76 us -> none  [on_device(): held = lax.dynamic_slice_in_dim(stale, slab * depth, depth, axis=0)]
    ppermute x2, starting transfers between devices: 2.36 us -> 3.17 us  [over_next(): return lax.ppermute(x, 'dp', [(i, i ^ PAIR) for i in range(replicas)])]
  transfers between devices with their start and end apart: 16 -> 18, of which waited for: 7 -> 5; matrix products, arithmetic and copies ran while one was open for 3% -> 0% of each run, Pallas kernels for 14% -> 23%
where the time goes in v3:
time: 57.1 us; the launch traced here: 56.9 us
  starting transfers between devices  27 us (47%)
  waiting for transfers between devices  14.3 us (25%)
  Pallas kernels  13.8 us (24%)
  other arithmetic  1 us (2%)
  between operations  0.86 us (2%)
    ppermute x8, starting transfers between devices, over_slab(): return lax.ppermute(x, 'dp', pairs)  12.1 us
    ppermute x4, starting transfers between devices, over_tensor(): lax.ppermute(x, 'tensor', [(i, i ^ j) for i in range(heads)])  6.72 us
    ppermute x2, waiting for transfers between devices, over_next(): return lax.ppermute(x, 'dp', [(i, i ^ PAIR) for i in range(replicas)])  6.55 us
    pallas_call x2, Pallas kernels, delta(): pl.pallas_call(functools.partial(delta_kernel, chunks, qrows, qcol, heads...  5.2 us
    ppermute x4, starting transfers between devices, over_core(): return lax.ppermute(x, 'dp', [(i, i ^ 1) for i in range(replicas)])  4.99 us
    pallas_call x1, Pallas kernels, moments(): pl.pallas_call(functools.partial(moments_kernel, chunks), in_specs=[FAR]...  4.99 us
    ppermute x8, waiting for transfers between devices, over_slab(): return lax.ppermute(x, 'dp', pairs)  3.64 us
    ppermute x2, starting transfers between devices, over_next(): return lax.ppermute(x, 'dp', [(i, i ^ PAIR) for i in range(replicas)])  3.17 us
  transfers between devices with their start and end apart: 18, of which 5 were waited for; matrix products, arithmetic and copies ran while one was open for 0% of the time, Pallas kernels for 23%

profile of v3, /device:TPU:0, one launch (start us, length us, event | category | flops | bytes accessed | tf_op | source)
XLA Modules:
  0.0 56.9 jit_solution(13075767420266239007)
XLA Ops:
  0.6 0.0 copy-start
  0.6 0.0 copy-start.1
  0.6 0.5 collective-permute-start
  1.2 2.6 %shard_map.113 = bf16[256,1024]{1,0:T(8,128)(2,1)S(1)} custom-call(s32[8,16]{1,0:T(8,128)} %refs_0_.4, f32[256,2048]{1,0:T(8,128)} %refs_1_.5, f32[256,2048]{1,0:T(8,128)} %refs_2_.5, f32[256,2048]{1,0:T(8,128)} %refs_3_.3, f32[256,2048]{1,0:T(8,128)} %refs_4_.3), custom_call_target="tpu_custom_call" | custom-call | tf_op jit(solution)/shard_map/pallas_call | solution.py:107
  3.8 0.0 collective-permute-done.theirs_ref
  3.8 2.6 %collective-permute-start.5 = (bf16[256,1024]{1,0:T(8,128)(2,1)S(1)}, bf16[256,1024]{1,0:T(8,128)(2,1)S(1)}, u32[]{:S(2)}, u32[]{:S(2)}) collective-permute-start(bf16[256,1024]{1,0:T(8,128)(2,1)S(1)} %shard_map.113), channel_id=1, source_target_pairs={{0,1},{1,0},{2,3},{3,2},{4,5},{5,4},{6,7},{7,6},{8,9},{9,8},{10,11... | collective-permute-start | bytes 1572872 | tf_op jit(solution)/shard_map/ppermute | solution.py:223
  6.4 0.0 copy-done
  6.4 0.0 copy-done.1
  6.4 0.4 shard_map.114
  6.8 0.7 %collective-permute-start.1 = (bf16[64,1024]{1,0:T(8,128)(2,1)S(1)}, bf16[64,1024]{1,0:T(8,128)(2,1)S(1)}, u32[]{:S(2)}, u32[]{:S(2)}) collective-permute-start(bf16[64,1024]{1,0:T(8,128)(2,1)S(1)} %get-tuple-element.40), channel_id=1, source_target_pairs={{0,0},{2,10},{4,4},{6,14},{8,8},{10,2},{12,12},{14,6},{16,16},{18,... | collective-permute-start | bytes 393224 | tf_op jit(solution)/shard_map/ppermute | solution.py:230
  7.5 1.6 %collective-permute-start.2 = (bf16[64,1024]{1,0:T(8,128)(2,1)S(1)}, bf16[64,1024]{1,0:T(8,128)(2,1)S(1)}, u32[]{:S(2)}, u32[]{:S(2)}) collective-permute-start(bf16[64,1024]{1,0:T(8,128)(2,1)S(1)} %get-tuple-element.41), channel_id=1, source_target_pairs={{0,4},{2,14},{4,0},{6,10},{8,12},{10,6},{12,8},{14,2},{16,20},{18,... | collective-permute-start | bytes 393224 | tf_op jit(solution)/shard_map/ppermute | solution.py:230
  9.1 2.6 %collective-permute-start.3 = (bf16[64,1024]{1,0:T(8,128)(2,1)S(1)}, bf16[64,1024]{1,0:T(8,128)(2,1)S(1)}, u32[]{:S(2)}, u32[]{:S(2)}) collective-permute-start(bf16[64,1024]{1,0:T(8,128)(2,1)S(1)} %get-tuple-element.42), channel_id=1, source_target_pairs={{0,16},{2,26},{4,20},{6,30},{8,24},{10,18},{12,28},{14,22},{16,0},... | collective-permute-start | bytes 393224 | tf_op jit(solution)/shard_map/ppermute | solution.py:230
  11.6 0.3 collective-permute-start.4
  11.9 2.6 %shard_map.115.refs_0_ = bf16[256,1024]{1,0:T(8,128)(2,1)S(1)} custom-call(s32[8,16]{1,0:T(8,128)} %refs_0_.4, f32[256,2048]{1,0:T(8,128)} %refs_1_.5, f32[256,2048]{1,0:T(8,128)} %refs_2_.5, f32[256,2048]{1,0:T(8,128)} %refs_3_.3, f32[256,2048]{1,0:T(8,128)} %refs_4_.3), custom_call_target="tpu_custom_call" | custom-call | tf_op jit(solution)/shard_map/pallas_call | solution.py:107
  14.5 0.0 collective-permute-done.1.refs_6_
  14.5 0.0 collective-permute-done.2.refs_7_
  14.6 0.3 collective-permute-start.6
  14.9 1.8 %collective-permute-start.7 = (bf16[64,1024]{1,0:T(8,128)(2,1)S(1)}, bf16[64,1024]{1,0:T(8,128)(2,1)S(1)}, u32[]{:S(2)}, u32[]{:S(2)}) collective-permute-start(bf16[64,1024]{1,0:T(8,128)(2,1)S(1)} %collective-permute-done.2.refs_7_), channel_id=1, source_target_pairs={{0,1},{1,0},{2,3},{3,2},{4,5},{5,4},{6,7},{7,6},{8,9},{9,8},{10,11... | collective-permute-start | bytes 393224 | tf_op jit(solution)/shard_map/ppermute | solution.py:223
  16.6 0.0 collective-permute-done.3.refs_4_
  16.6 4.0 %collective-permute-start.8 = (bf16[256,1024]{1,0:T(8,128)(2,1)S(1)}, bf16[256,1024]{1,0:T(8,128)(2,1)S(1)}, u32[]{:S(2)}, u32[]{:S(2)}) collective-permute-start(bf16[256,1024]{1,0:T(8,128)(2,1)S(1)} %shard_map.115.refs_0_), channel_id=1, source_target_pairs={{0,2},{2,0},{4,6},{6,4},{8,10},{10,8},{12,14},{14,12},{16,18},{18,... | collective-permute-start | bytes 1572872 | tf_op jit(solution)/shard_map/ppermute | solution.py:226
  20.6 3.6 %collective-permute-done.4.refs_5_ = bf16[64,1024]{1,0:T(8,128)(2,1)S(1)} collective-permute-done((bf16[64,1024]{1,0:T(8,128)(2,1)S(1)}, bf16[64,1024]{1,0:T(8,128)(2,1)S(1)}, u32[]{:S(2)}, u32[]{:S(2)}) %collective-permute-start.4) | collective-permute-done | bytes 131104 | tf_op jit(solution)/shard_map/ppermute | solution.py:230
  24.2 0.0 collective-permute-done.6.refs_1_
  24.2 0.0 collective-permute-done.7.refs_2_
  24.2 0.0 collective-permute-done.5.refs_1_
  24.2 0.1 collective-permute-start.9
  24.4 2.0 %collective-permute-start.11 = (bf16[128,1024]{1,0:T(8,128)(2,1)S(1)}, bf16[128,1024]{1,0:T(8,128)(2,1)S(1)}, u32[]{:S(2)}, u32[]{:S(2)}) collective-permute-start(bf16[128,1024]{1,0:T(8,128)(2,1)S(1)} %pad_maximum_fusion.2), channel_id=1, source_target_pairs={{0,1},{1,0},{2,3},{3,2},{4,5},{5,4},{6,7},{7,6},{8,9},{9,8},{10,11... | collective-permute-start | bytes 786440 | tf_op jit(solution)/shard_map/ppermute | solution.py:223
  26.4 0.0 collective-permute-done.8.refs_2_
  26.4 0.0 collective-permute-done.9.refs_3_
  26.4 2.5 %shard_map.116 = (bf16[1024,1024]{1,0:T(8,128)(2,1)S(1)}, f32[64,1024]{1,0:T(8,128)S(1)}, bf16[64,1024]{1,0:T(8,128)(2,1)S(1)}, f32[64,1024]{1,0:T(8,128)S(1)}, bf16[64,1024]{1,0:T(8,128)(2,1)S(1)}) custom-call(bf16[8192,1024]{1,0:T(8,128)(2,1)} %stale_far.1, bf16[256,1024]{1,0:T(8,128)(2,1)S(1)} %shard_map.115.refs_0_, ...), custom_call_target="tpu_custom_call" | custom-call | bytes 8388608 | tf_op jit(solution)/shard_map/pallas_call | solution.py:192
  28.9 1.6 %collective-permute-start.10 = (bf16[128,1024]{1,0:T(8,128)(2,1)S(1)}, bf16[128,1024]{1,0:T(8,128)(2,1)S(1)}, u32[]{:S(2)}, u32[]{:S(2)}) collective-permute-start(bf16[128,1024]{1,0:T(8,128)(2,1)S(1)} %pad_maximum_fusion.1), channel_id=1, source_target_pairs={{0,4},{2,6},{4,0},{6,2},{8,12},{10,14},{12,8},{14,10},{16,20},{18,... | collective-permute-start | bytes 786440 | tf_op jit(solution)/shard_map/ppermute | solution.py:233
  30.5 2.9 %collective-permute-done.11.refs_0_ = bf16[128,1024]{1,0:T(8,128)(2,1)S(1)} collective-permute-done((bf16[128,1024]{1,0:T(8,128)(2,1)S(1)}, bf16[128,1024]{1,0:T(8,128)(2,1)S(1)}, u32[]{:S(2)}, u32[]{:S(2)}) %collective-permute-start.11) | collective-permute-done | bytes 262176 | tf_op jit(solution)/shard_map/ppermute | solution.py:223
  33.4 4.1 %collective-permute-done.10 = bf16[128,1024]{1,0:T(8,128)(2,1)S(1)} collective-permute-done((bf16[128,1024]{1,0:T(8,128)(2,1)S(1)}, bf16[128,1024]{1,0:T(8,128)(2,1)S(1)}, u32[]{:S(2)}, u32[]{:S(2)}) %collective-permute-start.10) | collective-permute-done | bytes 262176 | tf_op jit(solution)/shard_map/ppermute | solution.py:233
  37.4 0.7 %shard_map.117 = (f32[64,1024]{1,0:T(8,128)S(1)}, bf16[64,1024]{1,0:T(8,128)(2,1)S(1)}, f32[64,1024]{1,0:T(8,128)S(1)}, bf16[64,1024]{1,0:T(8,128)(2,1)S(1)}) custom-call(bf16[128,1024]{1,0:T(8,128)(2,1)S(1)} %collective-permute-done.11.refs_0_, bf16[64,1024]{1,0:T(8,128)(2,1)S(1)} %collective-permute-done.6.refs_1_, ...), custom_call_target="tpu_custom_call" | custom-call | tf_op jit(solution)/shard_map/pallas_call | solution.py:205
  38.2 1.6 %collective-permute-start.14 = (bf16[128,1024]{1,0:T(8,128)(2,1)S(1)}, bf16[128,1024]{1,0:T(8,128)(2,1)S(1)}, u32[]{:S(2)}, u32[]{:S(2)}) collective-permute-start(bf16[128,1024]{1,0:T(8,128)(2,1)S(1)} %pad_maximum_fusion.3), channel_id=1, source_target_pairs={{0,4},{2,6},{4,0},{6,2},{8,12},{10,14},{12,8},{14,10},{16,20},{18,... | collective-permute-start | bytes 786440 | tf_op jit(solution)/shard_map/ppermute | solution.py:233
  39.8 0.1 add_convert_fusion.2
  39.8 2.9 %collective-permute-start.12 = (bf16[64,1024]{1,0:T(8,128)(2,1)S(1)}, bf16[64,1024]{1,0:T(8,128)(2,1)S(1)}, u32[]{:S(2)}, u32[]{:S(2)}) collective-permute-start(bf16[64,1024]{1,0:T(8,128)(2,1)S(1)} %get-tuple-element.74), channel_id=1, source_target_pairs={{0,16},{2,26},{4,20},{6,30},{8,24},{10,18},{12,28},{14,22},{16,0},... | collective-permute-start | bytes 393224 | tf_op jit(solution)/shard_map/ppermute | solution.py:230
  42.7 0.7 %collective-permute-start.13 = (bf16[64,1024]{1,0:T(8,128)(2,1)S(1)}, bf16[64,1024]{1,0:T(8,128)(2,1)S(1)}, u32[]{:S(2)}, u32[]{:S(2)}) collective-permute-start(bf16[64,1024]{1,0:T(8,128)(2,1)S(1)} %get-tuple-element.73), channel_id=1, source_target_pairs={{0,0},{2,10},{4,4},{6,14},{8,8},{10,2},{12,12},{14,6},{16,16},{18,... | collective-permute-start | bytes 393224 | tf_op jit(solution)/shard_map/ppermute | solution.py:230
  43.4 2.5 %collective-permute-done.14 = bf16[128,1024]{1,0:T(8,128)(2,1)S(1)} collective-permute-done((bf16[128,1024]{1,0:T(8,128)(2,1)S(1)}, bf16[128,1024]{1,0:T(8,128)(2,1)S(1)}, u32[]{:S(2)}, u32[]{:S(2)}) %collective-permute-start.14) | collective-permute-done | bytes 262176 | tf_op jit(solution)/shard_map/ppermute | solution.py:233
  45.9 0.1 add_convert_fusion
  45.9 2.7 %collective-permute-start.15 = (bf16[64,1024]{1,0:T(8,128)(2,1)S(1)}, bf16[64,1024]{1,0:T(8,128)(2,1)S(1)}, u32[]{:S(2)}, u32[]{:S(2)}) collective-permute-start(bf16[64,1024]{1,0:T(8,128)(2,1)S(1)} %get-tuple-element.72), channel_id=1, source_target_pairs={{0,16},{2,26},{4,20},{6,30},{8,24},{10,18},{12,28},{14,22},{16,0},... | collective-permute-start | bytes 393224 | tf_op jit(solution)/shard_map/ppermute | solution.py:230
  48.6 0.0 copy-start.2
  48.6 0.8 %collective-permute-start.16 = (bf16[64,1024]{1,0:T(8,128)(2,1)S(1)}, bf16[64,1024]{1,0:T(8,128)(2,1)S(1)}, u32[]{:S(2)}, u32[]{:S(2)}) collective-permute-start(bf16[64,1024]{1,0:T(8,128)(2,1)S(1)} %get-tuple-element.71), channel_id=1, source_target_pairs={{0,0},{2,10},{4,4},{6,14},{8,8},{10,2},{12,12},{14,6},{16,16},{18,... | collective-permute-start | bytes 393224 | tf_op jit(solution)/shard_map/ppermute | solution.py:230
  49.4 5.0 %shard_map.112 = (f32[256,2048]{1,0:T(8,128)}, f32[256,2048]{1,0:T(8,128)}) custom-call(f32[256,2048]{1,0:T(8,128)} %refs_1_.5, f32[256,2048]{1,0:T(8,128)} %refs_2_.5, f32[256,2048]{1,0:T(8,128)} %refs_3_.3), custom_call_target="tpu_custom_call" | custom-call | bytes 31457280 | tf_op jit(solution)/shard_map/pallas_call | solution.py:146
  54.4 0.0 collective-permute-done.12
  54.4 0.0 collective-permute-done.13
  54.4 0.0 collective-permute-done.15
  54.5 0.0 collective-permute-done.16
  54.5 0.1 convert_add_fusion
  54.6 0.4 collective-permute-start.17
  55.0 1.2 %collective-permute-done.17 = f32[2,32,1024]{2,1,0:T(8,128)S(1)} collective-permute-done((f32[2,32,1024]{2,1,0:T(8,128)S(1)}, f32[2,32,1024]{2,1,0:T(8,128)S(1)}, u32[]{:S(2)}, u32[]{:S(2)}) %collective-permute-start.17) | collective-permute-done | bytes 262176 | tf_op jit(solution)/shard_map/ppermute | solution.py:226
  56.2 0.0 copy-done.2
  56.2 0.7 %reverse_select_fusion = bf16[2,32,1024]{2,1,0:T(8,128)(2,1)} fusion(bf16[2,32,1024]{2,1,0:T(8,128)(2,1)S(1)} %fusion.4, pred[]{:T(512)S(6)} %eq.9), kind=kLoop, calls=%fused_computation.19 | loop fusion | flops 65536 | bytes 262145 | tf_op jit(solution)/shard_map/jit(_where)/select_n | solution.py:280
  (5 shorter events, 0.1 us)
Async XLA Ops:
  0.6 5.8 %copy-start = (bf16[32,8192]{1,0:T(8,128)(2,1)S(1)}, bf16[32,8192]{1,0:T(8,128)(2,1)}, u32[]{:S(2)}) copy-start(bf16[32,8192]{1,0:T(8,128)(2,1)} %ours_ref.1) | copy-start | bytes 1572868
  0.6 5.8 %copy-start.1 = (f32[8192]{0:T(1024)S(1)}, f32[8192]{0:T(1024)}, u32[]{:S(2)}) copy-start(f32[8192]{0:T(1024)} %param.10) | copy-start | bytes 98308
  0.6 3.1 %collective-permute-start = (bf16[32,8192]{1,0:T(8,128)(2,1)}, bf16[32,8192]{1,0:T(8,128)(2,1)S(1)}, u32[]{:S(2)}, u32[]{:S(2)}) collective-permute-start(bf16[32,8192]{1,0:T(8,128)(2,1)} %ours_ref.1), channel_id=1, source_target_pairs={{0,2},{2,0},{4,6},{6,4},{8,10},{10,8},{12,14},{14,12},{16,18},{18,... | collective-permute-start | bytes 1572872 | tf_op jit(solution)/shard_map/ppermute | solution.py:226
  3.8 20.5 %collective-permute-start.5 = (bf16[256,1024]{1,0:T(8,128)(2,1)S(1)}, bf16[256,1024]{1,0:T(8,128)(2,1)S(1)}, u32[]{:S(2)}, u32[]{:S(2)}) collective-permute-start(bf16[256,1024]{1,0:T(8,128)(2,1)S(1)} %shard_map.113), channel_id=1, source_target_pairs={{0,1},{1,0},{2,3},{3,2},{4,5},{5,4},{6,7},{7,6},{8,9},{9,8},{10,11... | collective-permute-start | bytes 1572872 | tf_op jit(solution)/shard_map/ppermute | solution.py:223
  6.8 7.7 %collective-permute-start.1 = (bf16[64,1024]{1,0:T(8,128)(2,1)S(1)}, bf16[64,1024]{1,0:T(8,128)(2,1)S(1)}, u32[]{:S(2)}, u32[]{:S(2)}) collective-permute-start(bf16[64,1024]{1,0:T(8,128)(2,1)S(1)} %get-tuple-element.40), channel_id=1, source_target_pairs={{0,0},{2,10},{4,4},{6,14},{8,8},{10,2},{12,12},{14,6},{16,16},{18,... | collective-permute-start | bytes 393224 | tf_op jit(solution)/shard_map/ppermute | solution.py:230
  7.5 7.1 %collective-permute-start.2 = (bf16[64,1024]{1,0:T(8,128)(2,1)S(1)}, bf16[64,1024]{1,0:T(8,128)(2,1)S(1)}, u32[]{:S(2)}, u32[]{:S(2)}) collective-permute-start(bf16[64,1024]{1,0:T(8,128)(2,1)S(1)} %get-tuple-element.41), channel_id=1, source_target_pairs={{0,4},{2,14},{4,0},{6,10},{8,12},{10,6},{12,8},{14,2},{16,20},{18,... | collective-permute-start | bytes 393224 | tf_op jit(solution)/shard_map/ppermute | solution.py:230
  9.1 7.6 %collective-permute-start.3 = (bf16[64,1024]{1,0:T(8,128)(2,1)S(1)}, bf16[64,1024]{1,0:T(8,128)(2,1)S(1)}, u32[]{:S(2)}, u32[]{:S(2)}) collective-permute-start(bf16[64,1024]{1,0:T(8,128)(2,1)S(1)} %get-tuple-element.42), channel_id=1, source_target_pairs={{0,16},{2,26},{4,20},{6,30},{8,24},{10,18},{12,28},{14,22},{16,0},... | collective-permute-start | bytes 393224 | tf_op jit(solution)/shard_map/ppermute | solution.py:230
  11.6 12.6 %collective-permute-start.4 = (bf16[64,1024]{1,0:T(8,128)(2,1)S(1)}, bf16[64,1024]{1,0:T(8,128)(2,1)S(1)}, u32[]{:S(2)}, u32[]{:S(2)}) collective-permute-start(bf16[64,1024]{1,0:T(8,128)(2,1)S(1)} %get-tuple-element.43), channel_id=1, source_target_pairs={{0,20},{2,30},{4,16},{6,26},{8,28},{10,22},{12,24},{14,18},{16,4},... | collective-permute-start | bytes 393224 | tf_op jit(solution)/shard_map/ppermute | solution.py:230
  14.6 9.7 %collective-permute-start.6 = (bf16[64,1024]{1,0:T(8,128)(2,1)S(1)}, bf16[64,1024]{1,0:T(8,128)(2,1)S(1)}, u32[]{:S(2)}, u32[]{:S(2)}) collective-permute-start(bf16[64,1024]{1,0:T(8,128)(2,1)S(1)} %collective-permute-done.1.refs_6_), channel_id=1, source_target_pairs={{0,1},{1,0},{2,3},{3,2},{4,5},{5,4},{6,7},{7,6},{8,9},{9,8},{10,11... | collective-permute-start | bytes 393224 | tf_op jit(solution)/shard_map/ppermute | solution.py:223
  14.9 9.4 %collective-permute-start.7 = (bf16[64,1024]{1,0:T(8,128)(2,1)S(1)}, bf16[64,1024]{1,0:T(8,128)(2,1)S(1)}, u32[]{:S(2)}, u32[]{:S(2)}) collective-permute-start(bf16[64,1024]{1,0:T(8,128)(2,1)S(1)} %collective-permute-done.2.refs_7_), channel_id=1, source_target_pairs={{0,1},{1,0},{2,3},{3,2},{4,5},{5,4},{6,7},{7,6},{8,9},{9,8},{10,11... | collective-permute-start | bytes 393224 | tf_op jit(solution)/shard_map/ppermute | solution.py:223
  16.6 9.8 %collective-permute-start.8 = (bf16[256,1024]{1,0:T(8,128)(2,1)S(1)}, bf16[256,1024]{1,0:T(8,128)(2,1)S(1)}, u32[]{:S(2)}, u32[]{:S(2)}) collective-permute-start(bf16[256,1024]{1,0:T(8,128)(2,1)S(1)} %shard_map.115.refs_0_), channel_id=1, source_target_pairs={{0,2},{2,0},{4,6},{6,4},{8,10},{10,8},{12,14},{14,12},{16,18},{18,... | collective-permute-start | bytes 1572872 | tf_op jit(solution)/shard_map/ppermute | solution.py:226
  24.2 2.2 %collective-permute-start.9 = (bf16[256,1024]{1,0:T(8,128)(2,1)S(1)}, bf16[256,1024]{1,0:T(8,128)(2,1)S(1)}, u32[]{:S(2)}, u32[]{:S(2)}) collective-permute-start(bf16[256,1024]{1,0:T(8,128)(2,1)S(1)} %collective-permute-done.5.refs_1_), channel_id=1, source_target_pairs={{0,2},{2,0},{4,6},{6,4},{8,10},{10,8},{12,14},{14,12},{16,18},{18,... | collective-permute-start | bytes 1572872 | tf_op jit(solution)/shard_map/ppermute | solution.py:226
  24.4 9.0 %collective-permute-start.11 = (bf16[128,1024]{1,0:T(8,128)(2,1)S(1)}, bf16[128,1024]{1,0:T(8,128)(2,1)S(1)}, u32[]{:S(2)}, u32[]{:S(2)}) collective-permute-start(bf16[128,1024]{1,0:T(8,128)(2,1)S(1)} %pad_maximum_fusion.2), channel_id=1, source_target_pairs={{0,1},{1,0},{2,3},{3,2},{4,5},{5,4},{6,7},{7,6},{8,9},{9,8},{10,11... | collective-permute-start | bytes 786440 | tf_op jit(solution)/shard_map/ppermute | solution.py:223
  28.9 8.5 %collective-permute-start.10 = (bf16[128,1024]{1,0:T(8,128)(2,1)S(1)}, bf16[128,1024]{1,0:T(8,128)(2,1)S(1)}, u32[]{:S(2)}, u32[]{:S(2)}) collective-permute-start(bf16[128,1024]{1,0:T(8,128)(2,1)S(1)} %pad_maximum_fusion.1), channel_id=1, source_target_pairs={{0,4},{2,6},{4,0},{6,2},{8,12},{10,14},{12,8},{14,10},{16,20},{18,... | collective-permute-start | bytes 786440 | tf_op jit(solution)/shard_map/ppermute | solution.py:233
  38.2 7.7 %collective-permute-start.14 = (bf16[128,1024]{1,0:T(8,128)(2,1)S(1)}, bf16[128,1024]{1,0:T(8,128)(2,1)S(1)}, u32[]{:S(2)}, u32[]{:S(2)}) collective-permute-start(bf16[128,1024]{1,0:T(8,128)(2,1)S(1)} %pad_maximum_fusion.3), channel_id=1, source_target_pairs={{0,4},{2,6},{4,0},{6,2},{8,12},{10,14},{12,8},{14,10},{16,20},{18,... | collective-permute-start | bytes 786440 | tf_op jit(solution)/shard_map/ppermute | solution.py:233
  39.8 14.6 %collective-permute-start.12 = (bf16[64,1024]{1,0:T(8,128)(2,1)S(1)}, bf16[64,1024]{1,0:T(8,128)(2,1)S(1)}, u32[]{:S(2)}, u32[]{:S(2)}) collective-permute-start(bf16[64,1024]{1,0:T(8,128)(2,1)S(1)} %get-tuple-element.74), channel_id=1, source_target_pairs={{0,16},{2,26},{4,20},{6,30},{8,24},{10,18},{12,28},{14,22},{16,0},... | collective-permute-start | bytes 393224 | tf_op jit(solution)/shard_map/ppermute | solution.py:230
  42.7 11.7 %collective-permute-start.13 = (bf16[64,1024]{1,0:T(8,128)(2,1)S(1)}, bf16[64,1024]{1,0:T(8,128)(2,1)S(1)}, u32[]{:S(2)}, u32[]{:S(2)}) collective-permute-start(bf16[64,1024]{1,0:T(8,128)(2,1)S(1)} %get-tuple-element.73), channel_id=1, source_target_pairs={{0,0},{2,10},{4,4},{6,14},{8,8},{10,2},{12,12},{14,6},{16,16},{18,... | collective-permute-start | bytes 393224 | tf_op jit(solution)/shard_map/ppermute | solution.py:230
  45.9 8.5 %collective-permute-start.15 = (bf16[64,1024]{1,0:T(8,128)(2,1)S(1)}, bf16[64,1024]{1,0:T(8,128)(2,1)S(1)}, u32[]{:S(2)}, u32[]{:S(2)}) collective-permute-start(bf16[64,1024]{1,0:T(8,128)(2,1)S(1)} %get-tuple-element.72), channel_id=1, source_target_pairs={{0,16},{2,26},{4,20},{6,30},{8,24},{10,18},{12,28},{14,22},{16,0},... | collective-permute-start | bytes 393224 | tf_op jit(solution)/shard_map/ppermute | solution.py:230
  48.6 7.6 %copy-start.2 = (f32[1024]{0:T(1024)S(1)}, f32[1024]{0:T(1024)}, u32[]{:S(2)}) copy-start(f32[1024]{0:T(1024)} %param.12) | copy-start | bytes 12292
  48.6 5.8 %collective-permute-start.16 = (bf16[64,1024]{1,0:T(8,128)(2,1)S(1)}, bf16[64,1024]{1,0:T(8,128)(2,1)S(1)}, u32[]{:S(2)}, u32[]{:S(2)}) collective-permute-start(bf16[64,1024]{1,0:T(8,128)(2,1)S(1)} %get-tuple-element.71), channel_id=1, source_target_pairs={{0,0},{2,10},{4,4},{6,14},{8,8},{10,2},{12,12},{14,6},{16,16},{18,... | collective-permute-start | bytes 393224 | tf_op jit(solution)/shard_map/ppermute | solution.py:230
  54.6 1.6 %collective-permute-start.17 = (f32[2,32,1024]{2,1,0:T(8,128)S(1)}, f32[2,32,1024]{2,1,0:T(8,128)S(1)}, u32[]{:S(2)}, u32[]{:S(2)}) collective-permute-start(f32[2,32,1024]{2,1,0:T(8,128)S(1)} %select_bitcast_fusion), channel_id=1, source_target_pairs={{0,2},{2,0},{4,6},{6,4},{8,10},{10,8},{12,14},{14,12},{16,18},{18,... | collective-permute-start | bytes 786440 | tf_op jit(solution)/shard_map/ppermute | solution.py:226

commit v4 on v3

--- a/solution.py
+++ b/solution.py
@@ -154,18 +154,24 @@
     )(far(first), far(second), far(grad))
 
 
-def multiply(piece_refs, weight, out_refs):
-    rows = out_refs[0].shape[0]
+def multiply(piece_refs, labels, weight, plan, out_refs):
     stacked = jnp.concatenate([r[...] for r in piece_refs], axis=0)
     total = jnp.dot(stacked, weight, preferred_element_type=F32)
-    for k, out_ref in enumerate(out_refs):
-        out_ref[...] = total[k * rows : (k + 1) * rows].astype(out_ref.dtype)
-
-
-def merge_kernel(slabs, heads, stale_far, *refs):
+    tall = total.shape[0] // len(labels)
+    for wanted, out_ref in zip(plan, out_refs):
+        for n, label in enumerate(wanted):
+            at = labels.index(label) * tall
+            out_ref[n * tall : (n + 1) * tall, :] = total[at : at + tall].astype(out_ref.dtype)
+
+
+def joined(tall, cols, plan, types):
+    return [like((len(wanted) * tall, cols), t) for wanted, t in zip(plan, types)]
+
+
+def merge_kernel(heads, labels, plan, stale_far, *refs):
     blocks = PAIR * heads
-    delta_refs, piece_refs = refs[:blocks], refs[blocks : blocks + slabs]
-    weight_ref, *out_refs, stale_ref, sems = refs[blocks + slabs :]
+    delta_refs, piece_refs = refs[:blocks], refs[blocks : -(len(plan) + 3)]
+    weight_ref, *out_refs, stale_ref, sems = refs[-(len(plan) + 3) :]
     dp, mine = lax.axis_index("dp"), lax.axis_index("tensor")
     rows = delta_refs[0].shape[0]
     fetches, places = [], []
@@ -179,35 +185,36 @@
     for n, here in enumerate(places):
         fetches[n].wait()
         weight_ref[here, :] = (stale_ref[n].astype(F32) + delta_refs[n][...].astype(F32)).astype(BF16)
-    multiply(piece_refs, weight_ref[...], out_refs)
-
-
-def product_kernel(groups, *refs):
-    multiply(refs[:groups], refs[groups][...], refs[groups + 1 :])
-
-
-def merge_product(stale, deltas, pieces, heads, types):
+    multiply(piece_refs, labels, weight_ref[...], plan, out_refs)
+
+
+def product_kernel(labels, plan, *refs):
+    *piece_refs, weight_ref = refs[: -len(plan)]
+    multiply(piece_refs, labels, weight_ref[...], plan, refs[-len(plan) :])
+
+
+def merge_product(stale, deltas, pieces, heads, labels, plan, types):
     rows, cols = deltas[0].shape
     blocks = len(deltas)
-    return pl.pallas_call(
-        functools.partial(merge_kernel, len(pieces), heads),
+    tall = sum(p.shape[0] for p in pieces) // len(labels)
+    return pl.pallas_call(
+        functools.partial(merge_kernel, heads, labels, plan),
         in_specs=[FAR] + [NEAR] * (blocks + len(pieces)),
-        out_shape=[like((blocks * rows, cols), BF16)]
-        + [like((p.shape[0], cols), t) for p, t in zip(pieces, types)],
+        out_shape=[like((blocks * rows, cols), BF16)] + joined(tall, cols, plan, types),
         scratch_shapes=[pltpu.VMEM((blocks, rows, cols), BF16), pltpu.SemaphoreType.DMA((blocks,))],
         compiler_params=pltpu.CompilerParams(vmem_limit_bytes=16 * MIB),
         cost_estimate=pl.CostEstimate(flops=0, bytes_accessed=8 * blocks * rows * cols, transcendentals=0),
     )(far(stale), *[near_by(x) for x in (*deltas, *pieces)])
 
 
-def product(groups, weight, types):
-    rows = sum(g.shape[0] for g in groups) // len(types)
-    return pl.pallas_call(
-        functools.partial(product_kernel, len(groups)),
-        out_shape=[like((rows, weight.shape[1]), t) for t in types],
+def product(pieces, weight, labels, plan, types):
+    tall = sum(p.shape[0] for p in pieces) // len(labels)
+    return pl.pallas_call(
+        functools.partial(product_kernel, labels, plan),
+        out_shape=joined(tall, weight.shape[1], plan, types),
         compiler_params=pltpu.CompilerParams(vmem_limit_bytes=12 * MIB),
         cost_estimate=FREE,
-    )(*[near_by(x) for x in (*groups, weight)])
+    )(*[near_by(x) for x in (*pieces, weight)])
 
 
 def on_device(tokens, gain, stale, bias, first, second, grad, residual, exponent):
@@ -253,28 +260,40 @@
     moved_distant = over_heads([jnp.concatenate(distant, axis=0)])
     shared = [*ours, *arrived]
     shared = shared + [over_core(x) for x in shared]
-    pieces = dict(zip(order, (*distant, *close)))
-
-    def added(parts, met):
-        tall = parts[0].shape[0]
-        return [(x + met[i * tall : (i + 1) * tall].astype(F32)).astype(BF16) for i, x in enumerate(parts[::2])]
-
-    mixed = [F32, BF16] * (partners // 2)
-    weight, *parts = merge_product(stale, shared, [pieces[m] for m in order], heads, mixed)
-    met = over_next(jnp.concatenate(parts[1::2], axis=0))
+    peers = range(1, heads)
+    evens, odds = remote[::2], remote[1::2]
+    labels = [(0, m) for m in order] + [(j, m) for j in peers for m in near]
+    plan = [[(0, m)] for m in (*evens, *odds)] + [[(j, m) for j in range(heads)] for m in near]
+    types = [F32] * len(evens) + [BF16] * (len(odds) + len(near))
+    blocks = [*distant, *close, *[x for row in moved_close for x in row]]
+    weight, *parts = merge_product(stale, shared, blocks, heads, labels, plan, types)
+    ours_even, ours_odd, parts_near = parts[: len(evens)], parts[len(evens) : len(remote)], parts[len(remote) :]
+    met = [over_next(x) for x in ours_odd]
+    terms_near = [over_slab(x, m) for x, m in zip(parts_near, near)]
     met, moved_distant = lax.optimization_barrier((met, moved_distant))
-    rows = [(parts, met)]
-    for j in range(1, heads):
-        parts = product([*moved_distant[j - 1], *moved_close[j - 1]], weight, mixed)
-        rows.append((parts, over_next(jnp.concatenate(parts[1::2], axis=0))))
-    terms = [[over_slab(x, m) for x, m in zip(added(*row), order[::2])] for row in rows]
+
+    labels = [(j, m) for j in peers for m in remote]
+    plan = [[(j, m) for j in peers] for m in (*evens, *odds)]
+    parts = product([x for row in moved_distant for x in row], weight, labels, plan, types[: len(remote)])
+    theirs_even, theirs_odd = parts[: len(evens)], parts[len(evens) :]
+    met_theirs = [over_next(x) for x in theirs_odd]
+
+    def onward(even, arrived):
+        return [over_slab((x + y.astype(F32)).astype(BF16), m) for x, y, m in zip(even, arrived, evens)]
+
+    terms_ours = onward(ours_even, met)
+    terms_theirs = onward(theirs_even, met_theirs)
     new_first, new_second = moments(first, second, grad)
-    new_first, new_second, terms = lax.optimization_barrier((new_first, new_second, terms))
-
-    totals = [sum(x.astype(F32) for x in row).reshape(PAIR, height, -1) for row in terms]
-    total = jnp.stack(totals, axis=1)
-    keep = jnp.where(core == 0, total[0], total[1])
-    give = jnp.where(core == 0, total[1], total[0])
+    new_first, new_second, terms_near, terms_ours, terms_theirs = lax.optimization_barrier(
+        (new_first, new_second, terms_near, terms_ours, terms_theirs)
+    )
+
+    def added(terms):
+        return sum(x.astype(F32) for x in terms).reshape(-1, PAIR, height, weight.shape[1])
+
+    total = added(terms_near) + jnp.concatenate([added(terms_ours), added(terms_theirs)], axis=0)
+    keep = jnp.where(core == 0, total[:, 0], total[:, 1])
+    give = jnp.where(core == 0, total[:, 1], total[:, 0])
     results = (keep + over_core(give) + bias).astype(BF16)
     if heads == 2:
         ordered = jnp.where(mine == 0, results, results[::-1])

time: 57.1 us -> 55.3 us (0.968)
  waiting for transfers between devices: 14.3 us -> 12.7 us
    ppermute x4, waiting for transfers between devices: 2.86 us -> 1.36 us  [over_tensor(): lax.ppermute(x, 'tensor', [(i, i ^ j) for i in range(heads)])]
    ppermute x2, waiting for transfers between devices: 6.55 us -> 5.17 us  [over_next(): return lax.ppermute(x, 'dp', [(i, i ^ PAIR) for i in range(replicas)])]
    ppermute x8, waiting for transfers between devices: 3.64 us -> 4.64 us  [over_slab(): return lax.ppermute(x, 'dp', pairs)]
  transfers between devices with their start and end apart: 18 -> 18, of which waited for: 5 -> 6; matrix products, arithmetic and copies ran while one was open for 0% -> 0% of each run, Pallas kernels for 23% -> 25%
where the time goes in v4:
time: 55.3 us; the launch traced here: 55.1 us
  starting transfers between devices  26.8 us (48%)
  Pallas kernels  13.8 us (25%)
  waiting for transfers between devices  12.7 us (23%)
  other arithmetic  0.95 us (2%)
  between operations  0.84 us (2%)
    ppermute x8, starting transfers between devices, over_slab(): return lax.ppermute(x, 'dp', pairs)  12.2 us
    ppermute x4, starting transfers between devices, over_tensor(): lax.ppermute(x, 'tensor', [(i, i ^ j) for i in range(heads)])  6.72 us
    pallas_call x2, Pallas kernels, delta(): pl.pallas_call(functools.partial(delta_kernel, chunks, qrows, qcol, heads...  5.2 us
    ppermute x2, waiting for transfers between devices, over_next(): return lax.ppermute(x, 'dp', [(i, i ^ PAIR) for i in range(replicas)])  5.17 us
    pallas_call x1, Pallas kernels, moments(): pl.pallas_call(functools.partial(moments_kernel, chunks), in_specs=[FAR]...  4.98 us
    ppermute x4, starting transfers between devices, over_core(): return lax.ppermute(x, 'dp', [(i, i ^ 1) for i in range(replicas)])  4.69 us
    ppermute x8, waiting for transfers between devices, over_slab(): return lax.ppermute(x, 'dp', pairs)  4.64 us
    ppermute x2, starting transfers between devices, over_next(): return lax.ppermute(x, 'dp', [(i, i ^ PAIR) for i in range(replicas)])  3.16 us
  transfers between devices with their start and end apart: 18, of which 6 were waited for; matrix products, arithmetic and copies ran while one was open for 0% of the time, Pallas kernels for 25%

profile of v4, /device:TPU:0, one launch (start us, length us, event | category | flops | bytes accessed | tf_op | source)
XLA Modules:
  0.0 55.1 jit_solution(10339014530468327659)
XLA Ops:
  0.6 0.0 copy-start
  0.6 0.0 copy-start.1
  0.6 0.5 collective-permute-start
  1.2 2.6 %shard_map.113 = bf16[256,1024]{1,0:T(8,128)(2,1)S(1)} custom-call(s32[8,16]{1,0:T(8,128)} %refs_0_.4, f32[256,2048]{1,0:T(8,128)} %refs_1_.5, f32[256,2048]{1,0:T(8,128)} %refs_2_.5, f32[256,2048]{1,0:T(8,128)} %refs_3_.3, f32[256,2048]{1,0:T(8,128)} %refs_4_.3), custom_call_target="tpu_custom_call" | custom-call | tf_op jit(solution)/shard_map/pallas_call | solution.py:107
  3.8 0.0 collective-permute-done.theirs_ref
  3.8 2.6 %collective-permute-start.5 = (bf16[256,1024]{1,0:T(8,128)(2,1)S(1)}, bf16[256,1024]{1,0:T(8,128)(2,1)S(1)}, u32[]{:S(2)}, u32[]{:S(2)}) collective-permute-start(bf16[256,1024]{1,0:T(8,128)(2,1)S(1)} %shard_map.113), channel_id=1, source_target_pairs={{0,1},{1,0},{2,3},{3,2},{4,5},{5,4},{6,7},{7,6},{8,9},{9,8},{10,11... | collective-permute-start | bytes 1572872 | tf_op jit(solution)/shard_map/ppermute | solution.py:230
  6.4 0.0 copy-done
  6.4 0.0 copy-done.1
  6.4 0.4 shard_map.114
  6.8 0.7 %collective-permute-start.1 = (bf16[64,1024]{1,0:T(8,128)(2,1)S(1)}, bf16[64,1024]{1,0:T(8,128)(2,1)S(1)}, u32[]{:S(2)}, u32[]{:S(2)}) collective-permute-start(bf16[64,1024]{1,0:T(8,128)(2,1)S(1)} %get-tuple-element.38), channel_id=1, source_target_pairs={{0,0},{2,10},{4,4},{6,14},{8,8},{10,2},{12,12},{14,6},{16,16},{18,... | collective-permute-start | bytes 393224 | tf_op jit(solution)/shard_map/ppermute | solution.py:237
  7.5 1.6 %collective-permute-start.2 = (bf16[64,1024]{1,0:T(8,128)(2,1)S(1)}, bf16[64,1024]{1,0:T(8,128)(2,1)S(1)}, u32[]{:S(2)}, u32[]{:S(2)}) collective-permute-start(bf16[64,1024]{1,0:T(8,128)(2,1)S(1)} %get-tuple-element.39), channel_id=1, source_target_pairs={{0,4},{2,14},{4,0},{6,10},{8,12},{10,6},{12,8},{14,2},{16,20},{18,... | collective-permute-start | bytes 393224 | tf_op jit(solution)/shard_map/ppermute | solution.py:237
  9.1 2.6 %collective-permute-start.3 = (bf16[64,1024]{1,0:T(8,128)(2,1)S(1)}, bf16[64,1024]{1,0:T(8,128)(2,1)S(1)}, u32[]{:S(2)}, u32[]{:S(2)}) collective-permute-start(bf16[64,1024]{1,0:T(8,128)(2,1)S(1)} %get-tuple-element.40), channel_id=1, source_target_pairs={{0,16},{2,26},{4,20},{6,30},{8,24},{10,18},{12,28},{14,22},{16,0},... | collective-permute-start | bytes 393224 | tf_op jit(solution)/shard_map/ppermute | solution.py:237
  11.6 0.3 collective-permute-start.4
  11.9 2.6 %shard_map.115.refs_0_ = bf16[256,1024]{1,0:T(8,128)(2,1)S(1)} custom-call(s32[8,16]{1,0:T(8,128)} %refs_0_.4, f32[256,2048]{1,0:T(8,128)} %refs_1_.5, f32[256,2048]{1,0:T(8,128)} %refs_2_.5, f32[256,2048]{1,0:T(8,128)} %refs_3_.3, f32[256,2048]{1,0:T(8,128)} %refs_4_.3), custom_call_target="tpu_custom_call" | custom-call | tf_op jit(solution)/shard_map/pallas_call | solution.py:107
  14.5 0.0 collective-permute-done.1.refs_6_
  14.5 0.0 collective-permute-done.2.refs_7_
  14.6 0.3 collective-permute-start.6
  14.9 1.8 %collective-permute-start.7 = (bf16[64,1024]{1,0:T(8,128)(2,1)S(1)}, bf16[64,1024]{1,0:T(8,128)(2,1)S(1)}, u32[]{:S(2)}, u32[]{:S(2)}) collective-permute-start(bf16[64,1024]{1,0:T(8,128)(2,1)S(1)} %collective-permute-done.2.refs_7_), channel_id=1, source_target_pairs={{0,1},{1,0},{2,3},{3,2},{4,5},{5,4},{6,7},{7,6},{8,9},{9,8},{10,11... | collective-permute-start | bytes 393224 | tf_op jit(solution)/shard_map/ppermute | solution.py:230
  16.6 0.0 collective-permute-done.3.refs_4_
  16.6 4.0 %collective-permute-start.8 = (bf16[256,1024]{1,0:T(8,128)(2,1)S(1)}, bf16[256,1024]{1,0:T(8,128)(2,1)S(1)}, u32[]{:S(2)}, u32[]{:S(2)}) collective-permute-start(bf16[256,1024]{1,0:T(8,128)(2,1)S(1)} %shard_map.115.refs_0_), channel_id=1, source_target_pairs={{0,2},{2,0},{4,6},{6,4},{8,10},{10,8},{12,14},{14,12},{16,18},{18,... | collective-permute-start | bytes 1572872 | tf_op jit(solution)/shard_map/ppermute | solution.py:233
  20.6 3.6 %collective-permute-done.4.refs_5_ = bf16[64,1024]{1,0:T(8,128)(2,1)S(1)} collective-permute-done((bf16[64,1024]{1,0:T(8,128)(2,1)S(1)}, bf16[64,1024]{1,0:T(8,128)(2,1)S(1)}, u32[]{:S(2)}, u32[]{:S(2)}) %collective-permute-start.4) | collective-permute-done | bytes 131104 | tf_op jit(solution)/shard_map/ppermute | solution.py:237
  24.2 0.0 collective-permute-done.6.refs_8_
  24.2 0.0 collective-permute-done.7.refs_9_
  24.2 0.0 collective-permute-done.5.refs_1_
  24.2 0.1 collective-permute-start.9
  24.4 2.0 %collective-permute-start.13 = (bf16[128,1024]{1,0:T(8,128)(2,1)S(1)}, bf16[128,1024]{1,0:T(8,128)(2,1)S(1)}, u32[]{:S(2)}, u32[]{:S(2)}) collective-permute-start(bf16[128,1024]{1,0:T(8,128)(2,1)S(1)} %pad_maximum_fusion), channel_id=1, source_target_pairs={{0,1},{1,0},{2,3},{3,2},{4,5},{5,4},{6,7},{7,6},{8,9},{9,8},{10,11... | collective-permute-start | bytes 786440 | tf_op jit(solution)/shard_map/ppermute | solution.py:230
  26.4 0.0 collective-permute-done.8.refs_2_
  26.4 0.0 collective-permute-done.9.refs_3_
  26.4 2.8 %shard_map.116 = (bf16[1024,1024]{1,0:T(8,128)(2,1)S(1)}, f32[64,1024]{1,0:T(8,128)S(1)}, bf16[64,1024]{1,0:T(8,128)(2,1)S(1)}, bf16[128,1024]{1,0:T(8,128)(2,1)S(1)}, bf16[128,1024]{1,0:T(8,128)(2,1)S(1)}) custom-call(bf16[8192,1024]{1,0:T(8,128)(2,1)} %stale_far.1, bf16[256,1024]{1,0:T(8,128)(2,1)S(1)} %shard_map.115.refs_0_, ...), custom_call_target="tpu_custom_call" | custom-call | bytes 8388608 | tf_op jit(solution)/shard_map/pallas_call | solution.py:200
  29.2 1.6 %collective-permute-start.12 = (bf16[64,1024]{1,0:T(8,128)(2,1)S(1)}, bf16[64,1024]{1,0:T(8,128)(2,1)S(1)}, u32[]{:S(2)}, u32[]{:S(2)}) collective-permute-start(bf16[64,1024]{1,0:T(8,128)(2,1)S(1)} %get-tuple-element.55), channel_id=1, source_target_pairs={{0,4},{2,6},{4,0},{6,2},{8,12},{10,14},{12,8},{14,10},{16,20},{18,... | collective-permute-start | bytes 393224 | tf_op jit(solution)/shard_map/ppermute | solution.py:240
  30.8 0.7 %collective-permute-start.10 = (bf16[128,1024]{1,0:T(8,128)(2,1)S(1)}, bf16[128,1024]{1,0:T(8,128)(2,1)S(1)}, u32[]{:S(2)}, u32[]{:S(2)}) collective-permute-start(bf16[128,1024]{1,0:T(8,128)(2,1)S(1)} %get-tuple-element.52), channel_id=1, source_target_pairs={{0,0},{2,10},{4,4},{6,14},{8,8},{10,2},{12,12},{14,6},{16,16},{18,... | collective-permute-start | bytes 786440 | tf_op jit(solution)/shard_map/ppermute | solution.py:237
  31.4 0.6 %collective-permute-start.11 = (bf16[128,1024]{1,0:T(8,128)(2,1)S(1)}, bf16[128,1024]{1,0:T(8,128)(2,1)S(1)}, u32[]{:S(2)}, u32[]{:S(2)}) collective-permute-start(bf16[128,1024]{1,0:T(8,128)(2,1)S(1)} %get-tuple-element.53), channel_id=1, source_target_pairs={{0,4},{2,14},{4,0},{6,10},{8,12},{10,6},{12,8},{14,2},{16,20},{18,... | collective-permute-start | bytes 786440 | tf_op jit(solution)/shard_map/ppermute | solution.py:237
  32.0 1.4 %collective-permute-done.13.refs_0_ = bf16[128,1024]{1,0:T(8,128)(2,1)S(1)} collective-permute-done((bf16[128,1024]{1,0:T(8,128)(2,1)S(1)}, bf16[128,1024]{1,0:T(8,128)(2,1)S(1)}, u32[]{:S(2)}, u32[]{:S(2)}) %collective-permute-start.13) | collective-permute-done | bytes 262176 | tf_op jit(solution)/shard_map/ppermute | solution.py:230
  33.4 1.5 %collective-permute-done.12 = bf16[64,1024]{1,0:T(8,128)(2,1)S(1)} collective-permute-done((bf16[64,1024]{1,0:T(8,128)(2,1)S(1)}, bf16[64,1024]{1,0:T(8,128)(2,1)S(1)}, u32[]{:S(2)}, u32[]{:S(2)}) %collective-permute-start.12) | collective-permute-done | bytes 131104 | tf_op jit(solution)/shard_map/ppermute | solution.py:240
  34.9 0.4 shard_map.117
  35.3 1.6 %collective-permute-start.15 = (bf16[64,1024]{1,0:T(8,128)(2,1)S(1)}, bf16[64,1024]{1,0:T(8,128)(2,1)S(1)}, u32[]{:S(2)}, u32[]{:S(2)}) collective-permute-start(bf16[64,1024]{1,0:T(8,128)(2,1)S(1)} %get-tuple-element.60), channel_id=1, source_target_pairs={{0,4},{2,6},{4,0},{6,2},{8,12},{10,14},{12,8},{14,10},{16,20},{18,... | collective-permute-start | bytes 393224 | tf_op jit(solution)/shard_map/ppermute | solution.py:240
  36.9 2.9 %collective-permute-start.14 = (bf16[64,1024]{1,0:T(8,128)(2,1)S(1)}, bf16[64,1024]{1,0:T(8,128)(2,1)S(1)}, u32[]{:S(2)}, u32[]{:S(2)}) collective-permute-start(bf16[64,1024]{1,0:T(8,128)(2,1)S(1)} %add_convert_fusion.1), channel_id=1, source_target_pairs={{0,16},{2,26},{4,20},{6,30},{8,24},{10,18},{12,28},{14,22},{16,0},... | collective-permute-start | bytes 393224 | tf_op jit(solution)/shard_map/ppermute | solution.py:237
  39.8 3.7 %collective-permute-done.15 = bf16[64,1024]{1,0:T(8,128)(2,1)S(1)} collective-permute-done((bf16[64,1024]{1,0:T(8,128)(2,1)S(1)}, bf16[64,1024]{1,0:T(8,128)(2,1)S(1)}, u32[]{:S(2)}, u32[]{:S(2)}) %collective-permute-start.15) | collective-permute-done | bytes 131104 | tf_op jit(solution)/shard_map/ppermute | solution.py:240
  43.5 3.0 %collective-permute-start.16 = (bf16[64,1024]{1,0:T(8,128)(2,1)S(1)}, bf16[64,1024]{1,0:T(8,128)(2,1)S(1)}, u32[]{:S(2)}, u32[]{:S(2)}) collective-permute-start(bf16[64,1024]{1,0:T(8,128)(2,1)S(1)} %add_convert_fusion), channel_id=1, source_target_pairs={{0,16},{2,26},{4,20},{6,30},{8,24},{10,18},{12,28},{14,22},{16,0},... | collective-permute-start | bytes 393224 | tf_op jit(solution)/shard_map/ppermute | solution.py:237
  46.5 5.0 %shard_map.112 = (f32[256,2048]{1,0:T(8,128)}, f32[256,2048]{1,0:T(8,128)}) custom-call(f32[256,2048]{1,0:T(8,128)} %refs_1_.5, f32[256,2048]{1,0:T(8,128)} %refs_2_.5, f32[256,2048]{1,0:T(8,128)} %refs_3_.3), custom_call_target="tpu_custom_call" | custom-call | bytes 31457280 | tf_op jit(solution)/shard_map/pallas_call | solution.py:146
  51.5 0.0 copy-start.2
  51.5 0.0 collective-permute-done.10
  51.5 0.0 collective-permute-done.11
  51.5 0.0 collective-permute-done.14
  51.6 1.0 %collective-permute-done.16 = bf16[64,1024]{1,0:T(8,128)(2,1)S(1)} collective-permute-done((bf16[64,1024]{1,0:T(8,128)(2,1)S(1)}, bf16[64,1024]{1,0:T(8,128)(2,1)S(1)}, u32[]{:S(2)}, u32[]{:S(2)}) %collective-permute-start.16) | collective-permute-done | bytes 131104 | tf_op jit(solution)/shard_map/ppermute | solution.py:237
  52.6 0.1 convert_add_fusion.1
  52.6 0.1 convert_add_fusion
  52.7 0.1 collective-permute-start.17
  52.8 1.5 %collective-permute-done.17 = f32[2,32,1024]{2,1,0:T(8,128)S(1)} collective-permute-done((f32[2,32,1024]{2,1,0:T(8,128)S(1)}, f32[2,32,1024]{2,1,0:T(8,128)S(1)}, u32[]{:S(2)}, u32[]{:S(2)}) %collective-permute-start.17) | collective-permute-done | bytes 262176 | tf_op jit(solution)/shard_map/ppermute | solution.py:233
  54.3 0.0 copy-done.2
  54.4 0.7 %reverse_select_fusion = bf16[2,32,1024]{2,1,0:T(8,128)(2,1)} fusion(bf16[2,32,1024]{2,1,0:T(8,128)(2,1)S(1)} %fusion.3, pred[]{:T(512)S(6)} %eq.9), kind=kLoop, calls=%fused_computation.11 | loop fusion | flops 65536 | bytes 262145 | tf_op jit(solution)/shard_map/jit(_where)/select_n | solution.py:299
  (5 shorter events, 0.1 us)
Async XLA Ops:
  0.6 5.8 %copy-start = (bf16[32,8192]{1,0:T(8,128)(2,1)S(1)}, bf16[32,8192]{1,0:T(8,128)(2,1)}, u32[]{:S(2)}) copy-start(bf16[32,8192]{1,0:T(8,128)(2,1)} %ours_ref.1) | copy-start | bytes 1572868
  0.6 5.8 %copy-start.1 = (f32[8192]{0:T(1024)S(1)}, f32[8192]{0:T(1024)}, u32[]{:S(2)}) copy-start(f32[8192]{0:T(1024)} %param.10) | copy-start | bytes 98308
  0.6 3.1 %collective-permute-start = (bf16[32,8192]{1,0:T(8,128)(2,1)}, bf16[32,8192]{1,0:T(8,128)(2,1)S(1)}, u32[]{:S(2)}, u32[]{:S(2)}) collective-permute-start(bf16[32,8192]{1,0:T(8,128)(2,1)} %ours_ref.1), channel_id=1, source_target_pairs={{0,2},{2,0},{4,6},{6,4},{8,10},{10,8},{12,14},{14,12},{16,18},{18,... | collective-permute-start | bytes 1572872 | tf_op jit(solution)/shard_map/ppermute | solution.py:233
  3.8 20.5 %collective-permute-start.5 = (bf16[256,1024]{1,0:T(8,128)(2,1)S(1)}, bf16[256,1024]{1,0:T(8,128)(2,1)S(1)}, u32[]{:S(2)}, u32[]{:S(2)}) collective-permute-start(bf16[256,1024]{1,0:T(8,128)(2,1)S(1)} %shard_map.113), channel_id=1, source_target_pairs={{0,1},{1,0},{2,3},{3,2},{4,5},{5,4},{6,7},{7,6},{8,9},{9,8},{10,11... | collective-permute-start | bytes 1572872 | tf_op jit(solution)/shard_map/ppermute | solution.py:230
  6.8 7.7 %collective-permute-start.1 = (bf16[64,1024]{1,0:T(8,128)(2,1)S(1)}, bf16[64,1024]{1,0:T(8,128)(2,1)S(1)}, u32[]{:S(2)}, u32[]{:S(2)}) collective-permute-start(bf16[64,1024]{1,0:T(8,128)(2,1)S(1)} %get-tuple-element.38), channel_id=1, source_target_pairs={{0,0},{2,10},{4,4},{6,14},{8,8},{10,2},{12,12},{14,6},{16,16},{18,... | collective-permute-start | bytes 393224 | tf_op jit(solution)/shard_map/ppermute | solution.py:237
  7.5 7.1 %collective-permute-start.2 = (bf16[64,1024]{1,0:T(8,128)(2,1)S(1)}, bf16[64,1024]{1,0:T(8,128)(2,1)S(1)}, u32[]{:S(2)}, u32[]{:S(2)}) collective-permute-start(bf16[64,1024]{1,0:T(8,128)(2,1)S(1)} %get-tuple-element.39), channel_id=1, source_target_pairs={{0,4},{2,14},{4,0},{6,10},{8,12},{10,6},{12,8},{14,2},{16,20},{18,... | collective-permute-start | bytes 393224 | tf_op jit(solution)/shard_map/ppermute | solution.py:237
  9.1 7.6 %collective-permute-start.3 = (bf16[64,1024]{1,0:T(8,128)(2,1)S(1)}, bf16[64,1024]{1,0:T(8,128)(2,1)S(1)}, u32[]{:S(2)}, u32[]{:S(2)}) collective-permute-start(bf16[64,1024]{1,0:T(8,128)(2,1)S(1)} %get-tuple-element.40), channel_id=1, source_target_pairs={{0,16},{2,26},{4,20},{6,30},{8,24},{10,18},{12,28},{14,22},{16,0},... | collective-permute-start | bytes 393224 | tf_op jit(solution)/shard_map/ppermute | solution.py:237
  11.6 12.6 %collective-permute-start.4 = (bf16[64,1024]{1,0:T(8,128)(2,1)S(1)}, bf16[64,1024]{1,0:T(8,128)(2,1)S(1)}, u32[]{:S(2)}, u32[]{:S(2)}) collective-permute-start(bf16[64,1024]{1,0:T(8,128)(2,1)S(1)} %get-tuple-element.41), channel_id=1, source_target_pairs={{0,20},{2,30},{4,16},{6,26},{8,28},{10,22},{12,24},{14,18},{16,4},... | collective-permute-start | bytes 393224 | tf_op jit(solution)/shard_map/ppermute | solution.py:237
  14.6 9.7 %collective-permute-start.6 = (bf16[64,1024]{1,0:T(8,128)(2,1)S(1)}, bf16[64,1024]{1,0:T(8,128)(2,1)S(1)}, u32[]{:S(2)}, u32[]{:S(2)}) collective-permute-start(bf16[64,1024]{1,0:T(8,128)(2,1)S(1)} %collective-permute-done.1.refs_6_), channel_id=1, source_target_pairs={{0,1},{1,0},{2,3},{3,2},{4,5},{5,4},{6,7},{7,6},{8,9},{9,8},{10,11... | collective-permute-start | bytes 393224 | tf_op jit(solution)/shard_map/ppermute | solution.py:230
  14.9 9.4 %collective-permute-start.7 = (bf16[64,1024]{1,0:T(8,128)(2,1)S(1)}, bf16[64,1024]{1,0:T(8,128)(2,1)S(1)}, u32[]{:S(2)}, u32[]{:S(2)}) collective-permute-start(bf16[64,1024]{1,0:T(8,128)(2,1)S(1)} %collective-permute-done.2.refs_7_), channel_id=1, source_target_pairs={{0,1},{1,0},{2,3},{3,2},{4,5},{5,4},{6,7},{7,6},{8,9},{9,8},{10,11... | collective-permute-start | bytes 393224 | tf_op jit(solution)/shard_map/ppermute | solution.py:230
  16.6 9.8 %collective-permute-start.8 = (bf16[256,1024]{1,0:T(8,128)(2,1)S(1)}, bf16[256,1024]{1,0:T(8,128)(2,1)S(1)}, u32[]{:S(2)}, u32[]{:S(2)}) collective-permute-start(bf16[256,1024]{1,0:T(8,128)(2,1)S(1)} %shard_map.115.refs_0_), channel_id=1, source_target_pairs={{0,2},{2,0},{4,6},{6,4},{8,10},{10,8},{12,14},{14,12},{16,18},{18,... | collective-permute-start | bytes 1572872 | tf_op jit(solution)/shard_map/ppermute | solution.py:233
  24.2 2.2 %collective-permute-start.9 = (bf16[256,1024]{1,0:T(8,128)(2,1)S(1)}, bf16[256,1024]{1,0:T(8,128)(2,1)S(1)}, u32[]{:S(2)}, u32[]{:S(2)}) collective-permute-start(bf16[256,1024]{1,0:T(8,128)(2,1)S(1)} %collective-permute-done.5.refs_1_), channel_id=1, source_target_pairs={{0,2},{2,0},{4,6},{6,4},{8,10},{10,8},{12,14},{14,12},{16,18},{18,... | collective-permute-start | bytes 1572872 | tf_op jit(solution)/shard_map/ppermute | solution.py:233
  24.4 9.0 %collective-permute-start.13 = (bf16[128,1024]{1,0:T(8,128)(2,1)S(1)}, bf16[128,1024]{1,0:T(8,128)(2,1)S(1)}, u32[]{:S(2)}, u32[]{:S(2)}) collective-permute-start(bf16[128,1024]{1,0:T(8,128)(2,1)S(1)} %pad_maximum_fusion), channel_id=1, source_target_pairs={{0,1},{1,0},{2,3},{3,2},{4,5},{5,4},{6,7},{7,6},{8,9},{9,8},{10,11... | collective-permute-start | bytes 786440 | tf_op jit(solution)/shard_map/ppermute | solution.py:230
  29.2 5.7 %collective-permute-start.12 = (bf16[64,1024]{1,0:T(8,128)(2,1)S(1)}, bf16[64,1024]{1,0:T(8,128)(2,1)S(1)}, u32[]{:S(2)}, u32[]{:S(2)}) collective-permute-start(bf16[64,1024]{1,0:T(8,128)(2,1)S(1)} %get-tuple-element.55), channel_id=1, source_target_pairs={{0,4},{2,6},{4,0},{6,2},{8,12},{10,14},{12,8},{14,10},{16,20},{18,... | collective-permute-start | bytes 393224 | tf_op jit(solution)/shard_map/ppermute | solution.py:240
  30.8 20.7 %collective-permute-start.10 = (bf16[128,1024]{1,0:T(8,128)(2,1)S(1)}, bf16[128,1024]{1,0:T(8,128)(2,1)S(1)}, u32[]{:S(2)}, u32[]{:S(2)}) collective-permute-start(bf16[128,1024]{1,0:T(8,128)(2,1)S(1)} %get-tuple-element.52), channel_id=1, source_target_pairs={{0,0},{2,10},{4,4},{6,14},{8,8},{10,2},{12,12},{14,6},{16,16},{18,... | collective-permute-start | bytes 786440 | tf_op jit(solution)/shard_map/ppermute | solution.py:237
  31.4 20.1 %collective-permute-start.11 = (bf16[128,1024]{1,0:T(8,128)(2,1)S(1)}, bf16[128,1024]{1,0:T(8,128)(2,1)S(1)}, u32[]{:S(2)}, u32[]{:S(2)}) collective-permute-start(bf16[128,1024]{1,0:T(8,128)(2,1)S(1)} %get-tuple-element.53), channel_id=1, source_target_pairs={{0,4},{2,14},{4,0},{6,10},{8,12},{10,6},{12,8},{14,2},{16,20},{18,... | collective-permute-start | bytes 786440 | tf_op jit(solution)/shard_map/ppermute | solution.py:237
  35.3 8.2 %collective-permute-start.15 = (bf16[64,1024]{1,0:T(8,128)(2,1)S(1)}, bf16[64,1024]{1,0:T(8,128)(2,1)S(1)}, u32[]{:S(2)}, u32[]{:S(2)}) collective-permute-start(bf16[64,1024]{1,0:T(8,128)(2,1)S(1)} %get-tuple-element.60), channel_id=1, source_target_pairs={{0,4},{2,6},{4,0},{6,2},{8,12},{10,14},{12,8},{14,10},{16,20},{18,... | collective-permute-start | bytes 393224 | tf_op jit(solution)/shard_map/ppermute | solution.py:240
  36.9 14.6 %collective-permute-start.14 = (bf16[64,1024]{1,0:T(8,128)(2,1)S(1)}, bf16[64,1024]{1,0:T(8,128)(2,1)S(1)}, u32[]{:S(2)}, u32[]{:S(2)}) collective-permute-start(bf16[64,1024]{1,0:T(8,128)(2,1)S(1)} %add_convert_fusion.1), channel_id=1, source_target_pairs={{0,16},{2,26},{4,20},{6,30},{8,24},{10,18},{12,28},{14,22},{16,0},... | collective-permute-start | bytes 393224 | tf_op jit(solution)/shard_map/ppermute | solution.py:237
  43.5 9.0 %collective-permute-start.16 = (bf16[64,1024]{1,0:T(8,128)(2,1)S(1)}, bf16[64,1024]{1,0:T(8,128)(2,1)S(1)}, u32[]{:S(2)}, u32[]{:S(2)}) collective-permute-start(bf16[64,1024]{1,0:T(8,128)(2,1)S(1)} %add_convert_fusion), channel_id=1, source_target_pairs={{0,16},{2,26},{4,20},{6,30},{8,24},{10,18},{12,28},{14,22},{16,0},... | collective-permute-start | bytes 393224 | tf_op jit(solution)/shard_map/ppermute | solution.py:237
  51.5 2.8 %copy-start.2 = (f32[1024]{0:T(1024)S(1)}, f32[1024]{0:T(1024)}, u32[]{:S(2)}) copy-start(f32[1024]{0:T(1024)} %param.12) | copy-start | bytes 12292
  52.7 1.6 %collective-permute-start.17 = (f32[2,32,1024]{2,1,0:T(8,128)S(1)}, f32[2,32,1024]{2,1,0:T(8,128)S(1)}, u32[]{:S(2)}, u32[]{:S(2)}) collective-permute-start(f32[2,32,1024]{2,1,0:T(8,128)S(1)} %select_bitcast_fusion), channel_id=1, source_target_pairs={{0,2},{2,0},{4,6},{6,4},{8,10},{10,8},{12,14},{14,12},{16,18},{18,... | collective-permute-start | bytes 786440 | tf_op jit(solution)/shard_map/ppermute | solution.py:233

commit v5 on v4

--- a/solution.py
+++ b/solution.py
@@ -120,19 +120,25 @@
     )(*[far(x) for x in (exponent, *arrays)])
 
 
-def moments_kernel(chunks, *refs):
-    inputs, outs, bufs, sems = refs[:3], refs[3:5], refs[5:10], refs[10]
-    high = inputs[0].shape[0] // chunks
-    at = [pl.ds(c * high, high) for c in range(chunks)]
-    fetches = [[pltpu.make_async_copy(inputs[a].at[r], bufs[a].at[r], sems.at[c, a]) for a in range(3)] for c, r in enumerate(at)]
-    stores = [[pltpu.make_async_copy(bufs[3 + a].at[r], outs[a].at[r], sems.at[c, 3 + a]) for a in range(2)] for c, r in enumerate(at)]
+def moments_kernel(start, size, chunks, *refs):
+    inputs, outs, bufs, sems = refs[:3], refs[-8:-6], refs[-6:-1], refs[-1]
+    high = size // chunks
+    turns = [(pl.ds(start + c * high, high), pl.ds(c * high, high)) for c in range(chunks)]
+    fetches = [
+        [pltpu.make_async_copy(inputs[a].at[there], bufs[a].at[here], sems.at[c, a]) for a in range(3)]
+        for c, (there, here) in enumerate(turns)
+    ]
+    stores = [
+        [pltpu.make_async_copy(bufs[3 + a].at[here], outs[a].at[there], sems.at[c, 3 + a]) for a in range(2)]
+        for c, (there, here) in enumerate(turns)
+    ]
     for row in fetches:
         for f in row:
             f.start()
-    for c, r in enumerate(at):
+    for c, (_, here) in enumerate(turns):
         for f in fetches[c]:
             f.wait()
-        bufs[3][r, :], bufs[4][r, :] = step(bufs[0][r, :], bufs[1][r, :], bufs[2][r, :])
+        bufs[3][here, :], bufs[4][here, :] = step(bufs[0][here, :], bufs[1][here, :], bufs[2][here, :])
         for s in stores[c]:
             s.start()
     for row in stores:
@@ -140,18 +146,19 @@
             s.wait()
 
 
-def moments(first, second, grad, chunks=4):
-    rows, full = first.shape
-    chunks = min(chunks, rows // 8)
-    return pl.pallas_call(
-        functools.partial(moments_kernel, chunks),
-        in_specs=[FAR] * 3,
+def moments(arrays, start, size, made=(), chunks=4):
+    rows, full = arrays[0].shape
+    chunks = min(chunks, size // 8)
+    return pl.pallas_call(
+        functools.partial(moments_kernel, start, size, chunks),
+        in_specs=[FAR] * (3 + len(made)),
         out_specs=[FAR] * 2,
         out_shape=[like((rows, full), F32)] * 2,
-        scratch_shapes=[pltpu.VMEM((rows, full), F32)] * 5 + [pltpu.SemaphoreType.DMA((chunks, 5))],
+        scratch_shapes=[pltpu.VMEM((size, full), F32)] * 5 + [pltpu.SemaphoreType.DMA((chunks, 5))],
+        input_output_aliases={3 + i: i for i in range(len(made))},
         compiler_params=pltpu.CompilerParams(vmem_limit_bytes=16 * MIB),
         cost_estimate=pl.CostEstimate(flops=0, bytes_accessed=60 * rows * full, transcendentals=0),
-    )(far(first), far(second), far(grad))
+    )(*[far(x) for x in (*arrays, *made)])
 
 
 def multiply(piece_refs, labels, weight, plan, out_refs):
@@ -168,22 +175,44 @@
     return [like((len(wanted) * tall, cols), t) for wanted, t in zip(plan, types)]
 
 
-def merge_kernel(heads, labels, plan, stale_far, *refs):
+def places(heads, rows):
+    core, mine = lax.axis_index("dp") % PAIR, lax.axis_index("tensor")
+    for n in range(PAIR * heads):
+        yield ((core ^ (n // heads)) * heads + (mine ^ (n % heads))) * rows
+
+
+def fetch_kernel(heads, stale_far, out_ref, sems):
+    blocks, rows = out_ref.shape[:2]
+    copies = []
+    for n, at in enumerate(places(heads, rows)):
+        first = (lax.axis_index("dp") // PAIR) * (blocks * rows) + at
+        source = stale_far.at[pl.ds(pl.multiple_of(first, rows), rows), :]
+        copies.append(pltpu.make_async_copy(source, out_ref.at[n], sems.at[n]))
+        copies[-1].start()
+    for copy in copies:
+        copy.wait()
+
+
+def fetch(stale, heads, slabs):
     blocks = PAIR * heads
-    delta_refs, piece_refs = refs[:blocks], refs[blocks : -(len(plan) + 3)]
-    weight_ref, *out_refs, stale_ref, sems = refs[-(len(plan) + 3) :]
-    dp, mine = lax.axis_index("dp"), lax.axis_index("tensor")
+    return pl.pallas_call(
+        functools.partial(fetch_kernel, heads),
+        in_specs=[FAR],
+        out_specs=NEAR,
+        out_shape=like((blocks, stale.shape[0] // slabs // blocks, stale.shape[1]), BF16),
+        scratch_shapes=[pltpu.SemaphoreType.DMA((blocks,))],
+        compiler_params=pltpu.CompilerParams(vmem_limit_bytes=8 * MIB),
+        cost_estimate=FREE,
+    )(far(stale))
+
+
+def merge_kernel(heads, labels, plan, stale_ref, *refs):
+    blocks = PAIR * heads
+    delta_refs, piece_refs = refs[:blocks], refs[blocks : -(len(plan) + 1)]
+    weight_ref, *out_refs = refs[-(len(plan) + 1) :]
     rows = delta_refs[0].shape[0]
-    fetches, places = [], []
-    for n in range(blocks):
-        at = ((dp % PAIR ^ (n // heads)) * heads + (mine ^ (n % heads))) * rows
-        first = (dp // PAIR) * (blocks * rows) + at
-        source = stale_far.at[pl.ds(pl.multiple_of(first, rows), rows), :]
-        fetches.append(pltpu.make_async_copy(source, stale_ref.at[n], sems.at[n]))
-        places.append(pl.ds(pl.multiple_of(at, rows), rows))
-        fetches[-1].start()
-    for n, here in enumerate(places):
-        fetches[n].wait()
+    for n, at in enumerate(places(heads, rows)):
+        here = pl.ds(pl.multiple_of(at, rows), rows)
         weight_ref[here, :] = (stale_ref[n].astype(F32) + delta_refs[n][...].astype(F32)).astype(BF16)
     multiply(piece_refs, labels, weight_ref[...], plan, out_refs)
 
@@ -199,12 +228,10 @@
     tall = sum(p.shape[0] for p in pieces) // len(labels)
     return pl.pallas_call(
         functools.partial(merge_kernel, heads, labels, plan),
-        in_specs=[FAR] + [NEAR] * (blocks + len(pieces)),
         out_shape=[like((blocks * rows, cols), BF16)] + joined(tall, cols, plan, types),
-        scratch_shapes=[pltpu.VMEM((blocks, rows, cols), BF16), pltpu.SemaphoreType.DMA((blocks,))],
         compiler_params=pltpu.CompilerParams(vmem_limit_bytes=16 * MIB),
         cost_estimate=pl.CostEstimate(flops=0, bytes_accessed=8 * blocks * rows * cols, transcendentals=0),
-    )(far(stale), *[near_by(x) for x in (*deltas, *pieces)])
+    )(*[near_by(x) for x in (stale, *deltas, *pieces)])
 
 
 def product(pieces, weight, labels, plan, types):
@@ -256,20 +283,29 @@
 
     ours, close = lax.optimization_barrier((ours, close))
     moved_close = over_heads(close)
-    distant, arrived, moved_close = lax.optimization_barrier((distant, arrived, moved_close))
+    first_rows = first.shape[0]
+    bulk = first_rows // 2
+    made = moments(arrays[:3], 0, bulk)
+    held = fetch(stale, heads, slabs)
+    made, held, distant, arrived, moved_close = lax.optimization_barrier((made, held, distant, arrived, moved_close))
     moved_distant = over_heads([jnp.concatenate(distant, axis=0)])
     shared = [*ours, *arrived]
     shared = shared + [over_core(x) for x in shared]
     peers = range(1, heads)
     evens, odds = remote[::2], remote[1::2]
     labels = [(0, m) for m in order] + [(j, m) for j in peers for m in near]
-    plan = [[(0, m)] for m in (*evens, *odds)] + [[(j, m) for j in range(heads)] for m in near]
-    types = [F32] * len(evens) + [BF16] * (len(odds) + len(near))
+    plan = [[(0, m)] for m in (*evens, *odds)] + [[(j, m) for j in range(heads)] for m in near[::2]]
+    plan += [[(j, m) for j in group] for group in ([0], peers) for m in near[1::2]]
+    types = [F32] * len(evens) + [BF16] * (len(odds) + len(near) + len(near[1::2]))
     blocks = [*distant, *close, *[x for row in moved_close for x in row]]
-    weight, *parts = merge_product(stale, shared, blocks, heads, labels, plan, types)
+    weight, *parts = merge_product(held, shared, blocks, heads, labels, plan, types)
     ours_even, ours_odd, parts_near = parts[: len(evens)], parts[len(evens) : len(remote)], parts[len(remote) :]
     met = [over_next(x) for x in ours_odd]
-    terms_near = [over_slab(x, m) for x, m in zip(parts_near, near)]
+    split = len(near[::2])
+    last = split + len(near[1::2])
+    terms_near = [over_slab(x, m) for x, m in zip(parts_near[:split], near[::2])]
+    terms_ours = [over_slab(x, m) for x, m in zip(parts_near[split:last], near[1::2])]
+    late = parts_near[last:]
     met, moved_distant = lax.optimization_barrier((met, moved_distant))
 
     labels = [(j, m) for j in peers for m in remote]
@@ -281,9 +317,11 @@
     def onward(even, arrived):
         return [over_slab((x + y.astype(F32)).astype(BF16), m) for x, y, m in zip(even, arrived, evens)]
 
-    terms_ours = onward(ours_even, met)
+    terms_ours += onward(ours_even, met)
+    met_theirs, late = lax.optimization_barrier((met_theirs, late))
     terms_theirs = onward(theirs_even, met_theirs)
-    new_first, new_second = moments(first, second, grad)
+    terms_theirs += [over_slab(x, m) for x, m in zip(late, near[1::2])]
+    new_first, new_second = moments(arrays[:3], bulk, first_rows - bulk, made)
     new_first, new_second, terms_near, terms_ours, terms_theirs = lax.optimization_barrier(
         (new_first, new_second, terms_near, terms_ours, terms_theirs)
     )

time: 55.3 us -> 53.3 us (0.964)
  waiting for transfers between devices: 12.7 us -> 9.57 us
  Pallas kernels: 13.8 us -> 15.2 us
    ppermute x2, waiting for transfers between devices: 5.17 us -> 2.49 us  [over_next(): return lax.ppermute(x, 'dp', [(i, i ^ PAIR) for i in range(replicas)])]
    ppermute x4, starting transfers between devices: 4.69 us -> 3 us  [over_core(): return lax.ppermute(x, 'dp', [(i, i ^ 1) for i in range(replicas)])]
    pallas_call x2 -> x4, Pallas kernels: 7.76 us -> 9.18 us  [the longest x2 5.64 us: moments(): pl.pallas_call(functools.partial(moments_kernel, start, size, chunks), in...]
    ppermute x8 -> x9, starting transfers between devices: 12.2 us -> 13.6 us  [over_slab(): return lax.ppermute(x, 'dp', pairs)]
    ppermute x8 -> x9, waiting for transfers between devices: 4.64 us -> 3.4 us  [over_slab(): return lax.ppermute(x, 'dp', pairs)]
    ppermute x4, waiting for transfers between devices: 1.36 us -> 2.16 us  [over_tensor(): lax.ppermute(x, 'tensor', [(i, i ^ j) for i in range(heads)])]
  transfers between devices with their start and end apart: 18 -> 19, of which waited for: 6 -> 6; matrix products, arithmetic and copies ran while one was open for 0% -> 0% of each run, Pallas kernels for 25% -> 29%
where the time goes in v5:
time: 53.3 us; the launch traced here: 53 us
  starting transfers between devices  26.4 us (50%)
  Pallas kernels  15.2 us (29%)
  waiting for transfers between devices  9.57 us (18%)
  other arithmetic  0.96 us (2%)
  between operations  0.85 us (2%)
    ppermute x9, starting transfers between devices, over_slab(): return lax.ppermute(x, 'dp', pairs)  13.6 us
    ppermute x4, starting transfers between devices, over_tensor(): lax.ppermute(x, 'tensor', [(i, i ^ j) for i in range(heads)])  6.72 us
    pallas_call x2, Pallas kernels, moments(): pl.pallas_call(functools.partial(moments_kernel, start, size, chunks), in...  5.64 us
    pallas_call x2, Pallas kernels, delta(): pl.pallas_call(functools.partial(delta_kernel, chunks, qrows, qcol, heads...  5.2 us
    ppermute x9, waiting for transfers between devices, over_slab(): return lax.ppermute(x, 'dp', pairs)  3.4 us
    ppermute x2, starting transfers between devices, over_next(): return lax.ppermute(x, 'dp', [(i, i ^ PAIR) for i in range(replicas)])  3.17 us
    ppermute x4, starting transfers between devices, over_core(): return lax.ppermute(x, 'dp', [(i, i ^ 1) for i in range(replicas)])  3 us
    ppermute x2, waiting for transfers between devices, over_next(): return lax.ppermute(x, 'dp', [(i, i ^ PAIR) for i in range(replicas)])  2.49 us
  transfers between devices with their start and end apart: 19, of which 6 were waited for; matrix products, arithmetic and copies ran while one was open for 0% of the time, Pallas kernels for 29%

profile of v5, /device:TPU:0, one launch (start us, length us, event | category | flops | bytes accessed | tf_op | source)
XLA Modules:
  0.0 53.0 jit_solution(8276751379038012590)
XLA Ops:
  0.6 0.0 copy-start
  0.6 0.0 copy-start.1
  0.6 0.5 collective-permute-start
  1.2 2.6 %shard_map.114 = bf16[256,1024]{1,0:T(8,128)(2,1)S(1)} custom-call(s32[8,16]{1,0:T(8,128)} %refs_0_.5, f32[256,2048]{1,0:T(8,128)} %refs_0_.6, f32[256,2048]{1,0:T(8,128)} %refs_1_.7, f32[256,2048]{1,0:T(8,128)} %refs_2_.7, f32[256,2048]{1,0:T(8,128)} %refs_4_.3), custom_call_target="tpu_custom_call" | custom-call | tf_op jit(solution)/shard_map/pallas_call | solution.py:107
  3.8 0.0 collective-permute-done.theirs_ref
  3.8 2.6 %collective-permute-start.3 = (bf16[256,1024]{1,0:T(8,128)(2,1)S(1)}, bf16[256,1024]{1,0:T(8,128)(2,1)S(1)}, u32[]{:S(2)}, u32[]{:S(2)}) collective-permute-start(bf16[256,1024]{1,0:T(8,128)(2,1)S(1)} %shard_map.114), channel_id=1, source_target_pairs={{0,1},{1,0},{2,3},{3,2},{4,5},{5,4},{6,7},{7,6},{8,9},{9,8},{10,11... | collective-permute-start | bytes 1572872 | tf_op jit(solution)/shard_map/ppermute | solution.py:257
  6.4 0.0 copy-done
  6.4 0.0 copy-done.1
  6.4 0.4 shard_map.115
  6.8 0.7 %collective-permute-start.4 = (bf16[64,1024]{1,0:T(8,128)(2,1)S(1)}, bf16[64,1024]{1,0:T(8,128)(2,1)S(1)}, u32[]{:S(2)}, u32[]{:S(2)}) collective-permute-start(bf16[64,1024]{1,0:T(8,128)(2,1)S(1)} %get-tuple-element.50), channel_id=1, source_target_pairs={{0,0},{2,10},{4,4},{6,14},{8,8},{10,2},{12,12},{14,6},{16,16},{18,... | collective-permute-start | bytes 393224 | tf_op jit(solution)/shard_map/ppermute | solution.py:264
  7.5 1.6 %collective-permute-start.5 = (bf16[64,1024]{1,0:T(8,128)(2,1)S(1)}, bf16[64,1024]{1,0:T(8,128)(2,1)S(1)}, u32[]{:S(2)}, u32[]{:S(2)}) collective-permute-start(bf16[64,1024]{1,0:T(8,128)(2,1)S(1)} %get-tuple-element.51), channel_id=1, source_target_pairs={{0,4},{2,14},{4,0},{6,10},{8,12},{10,6},{12,8},{14,2},{16,20},{18,... | collective-permute-start | bytes 393224 | tf_op jit(solution)/shard_map/ppermute | solution.py:264
  9.1 2.6 %collective-permute-start.1 = (bf16[64,1024]{1,0:T(8,128)(2,1)S(1)}, bf16[64,1024]{1,0:T(8,128)(2,1)S(1)}, u32[]{:S(2)}, u32[]{:S(2)}) collective-permute-start(bf16[64,1024]{1,0:T(8,128)(2,1)S(1)} %get-tuple-element.47), channel_id=1, source_target_pairs={{0,16},{2,26},{4,20},{6,30},{8,24},{10,18},{12,28},{14,22},{16,0},... | collective-permute-start | bytes 393224 | tf_op jit(solution)/shard_map/ppermute | solution.py:264
  11.6 0.3 collective-permute-start.2
  11.9 2.6 %shard_map.116.refs_0_ = bf16[256,1024]{1,0:T(8,128)(2,1)S(1)} custom-call(s32[8,16]{1,0:T(8,128)} %refs_0_.5, f32[256,2048]{1,0:T(8,128)} %refs_0_.6, f32[256,2048]{1,0:T(8,128)} %refs_1_.7, f32[256,2048]{1,0:T(8,128)} %refs_2_.7, f32[256,2048]{1,0:T(8,128)} %refs_4_.3), custom_call_target="tpu_custom_call" | custom-call | tf_op jit(solution)/shard_map/pallas_call | solution.py:107
  14.5 0.0 collective-permute-done.4.refs_6_
  14.5 0.0 collective-permute-done.5.refs_7_
  14.6 0.3 collective-permute-start.6
  14.9 1.8 %collective-permute-start.7 = (bf16[64,1024]{1,0:T(8,128)(2,1)S(1)}, bf16[64,1024]{1,0:T(8,128)(2,1)S(1)}, u32[]{:S(2)}, u32[]{:S(2)}) collective-permute-start(bf16[64,1024]{1,0:T(8,128)(2,1)S(1)} %collective-permute-done.5.refs_7_), channel_id=1, source_target_pairs={{0,1},{1,0},{2,3},{3,2},{4,5},{5,4},{6,7},{7,6},{8,9},{9,8},{10,11... | collective-permute-start | bytes 393224 | tf_op jit(solution)/shard_map/ppermute | solution.py:257
  16.6 2.8 %shard_map.112 = (f32[256,2048]{1,0:T(8,128)}, f32[256,2048]{1,0:T(8,128)}) custom-call(f32[256,2048]{1,0:T(8,128)} %refs_0_.6, f32[256,2048]{1,0:T(8,128)} %refs_1_.7, f32[256,2048]{1,0:T(8,128)} %refs_2_.7), custom_call_target="tpu_custom_call" | custom-call | bytes 31457280 | tf_op jit(solution)/shard_map/pallas_call | solution.py:152
  19.5 1.6 %shard_map.113.stale_ref = bf16[4,256,1024]{2,1,0:T(8,128)(2,1)S(1)} custom-call(bf16[8192,1024]{1,0:T(8,128)(2,1)} %stale_far.1), custom_call_target="tpu_custom_call" | custom-call | tf_op jit(solution)/shard_map/pallas_call | solution.py:198
  21.0 0.0 collective-permute-done.1.refs_4_
  21.1 2.3 %collective-permute-start.8 = (bf16[256,1024]{1,0:T(8,128)(2,1)S(1)}, bf16[256,1024]{1,0:T(8,128)(2,1)S(1)}, u32[]{:S(2)}, u32[]{:S(2)}) collective-permute-start(bf16[256,1024]{1,0:T(8,128)(2,1)S(1)} %shard_map.116.refs_0_), channel_id=1, source_target_pairs={{0,2},{2,0},{4,6},{6,4},{8,10},{10,8},{12,14},{14,12},{16,18},{18,... | collective-permute-start | bytes 1572872 | tf_op jit(solution)/shard_map/ppermute | solution.py:260
  23.3 0.9 %collective-permute-done.2.refs_5_ = bf16[64,1024]{1,0:T(8,128)(2,1)S(1)} collective-permute-done((bf16[64,1024]{1,0:T(8,128)(2,1)S(1)}, bf16[64,1024]{1,0:T(8,128)(2,1)S(1)}, u32[]{:S(2)}, u32[]{:S(2)}) %collective-permute-start.2) | collective-permute-done | bytes 131104 | tf_op jit(solution)/shard_map/ppermute | solution.py:264
  24.2 0.0 collective-permute-done.6.refs_8_
  24.2 0.0 collective-permute-done.7.refs_9_
  24.2 0.0 collective-permute-done.3.refs_1_
  24.2 0.1 collective-permute-start.9
  24.4 2.0 %collective-permute-start.13 = (bf16[128,1024]{1,0:T(8,128)(2,1)S(1)}, bf16[128,1024]{1,0:T(8,128)(2,1)S(1)}, u32[]{:S(2)}, u32[]{:S(2)}) collective-permute-start(bf16[128,1024]{1,0:T(8,128)(2,1)S(1)} %pad_maximum_fusion), channel_id=1, source_target_pairs={{0,1},{1,0},{2,3},{3,2},{4,5},{5,4},{6,7},{7,6},{8,9},{9,8},{10,11... | collective-permute-start | bytes 786440 | tf_op jit(solution)/shard_map/ppermute | solution.py:257
  26.4 0.0 collective-permute-done.8.refs_2_
  26.4 0.0 collective-permute-done.9.refs_3_
  26.4 2.0 %shard_map.118 = (bf16[1024,1024]{1,0:T(8,128)(2,1)S(1)}, f32[64,1024]{1,0:T(8,128)S(1)}, bf16[64,1024]{1,0:T(8,128)(2,1)S(1)}, bf16[128,1024]{1,0:T(8,128)(2,1)...) custom-call(bf16[4,256,1024]{2,1,0:T(8,128)(2,1)S(1)} %shard_map.113.stale_ref, ...), custom_call_target="tpu_custom_call" | custom-call | bytes 8388608 | tf_op jit(solution)/shard_map/pallas_call | solution.py:229
  28.4 1.6 %collective-permute-start.12 = (bf16[64,1024]{1,0:T(8,128)(2,1)S(1)}, bf16[64,1024]{1,0:T(8,128)(2,1)S(1)}, u32[]{:S(2)}, u32[]{:S(2)}) collective-permute-start(bf16[64,1024]{1,0:T(8,128)(2,1)S(1)} %get-tuple-element.69), channel_id=1, source_target_pairs={{0,4},{2,6},{4,0},{6,2},{8,12},{10,14},{12,8},{14,10},{16,20},{18,... | collective-permute-start | bytes 393224 | tf_op jit(solution)/shard_map/ppermute | solution.py:267
  30.0 0.7 %collective-permute-start.10 = (bf16[128,1024]{1,0:T(8,128)(2,1)S(1)}, bf16[128,1024]{1,0:T(8,128)(2,1)S(1)}, u32[]{:S(2)}, u32[]{:S(2)}) collective-permute-start(bf16[128,1024]{1,0:T(8,128)(2,1)S(1)} %get-tuple-element.66), channel_id=1, source_target_pairs={{0,0},{2,10},{4,4},{6,14},{8,8},{10,2},{12,12},{14,6},{16,16},{18,... | collective-permute-start | bytes 786440 | tf_op jit(solution)/shard_map/ppermute | solution.py:264
  30.7 0.6 %collective-permute-start.11 = (bf16[64,1024]{1,0:T(8,128)(2,1)S(1)}, bf16[64,1024]{1,0:T(8,128)(2,1)S(1)}, u32[]{:S(2)}, u32[]{:S(2)}) collective-permute-start(bf16[64,1024]{1,0:T(8,128)(2,1)S(1)} %get-tuple-element.67), channel_id=1, source_target_pairs={{0,4},{2,14},{4,0},{6,10},{8,12},{10,6},{12,8},{14,2},{16,20},{18,... | collective-permute-start | bytes 393224 | tf_op jit(solution)/shard_map/ppermute | solution.py:264
  31.2 2.2 %collective-permute-done.13.refs_0_ = bf16[128,1024]{1,0:T(8,128)(2,1)S(1)} collective-permute-done((bf16[128,1024]{1,0:T(8,128)(2,1)S(1)}, bf16[128,1024]{1,0:T(8,128)(2,1)S(1)}, u32[]{:S(2)}, u32[]{:S(2)}) %collective-permute-start.13) | collective-permute-done | bytes 262176 | tf_op jit(solution)/shard_map/ppermute | solution.py:257
  33.4 0.7 %collective-permute-done.12 = bf16[64,1024]{1,0:T(8,128)(2,1)S(1)} collective-permute-done((bf16[64,1024]{1,0:T(8,128)(2,1)S(1)}, bf16[64,1024]{1,0:T(8,128)(2,1)S(1)}, u32[]{:S(2)}, u32[]{:S(2)}) %collective-permute-start.12) | collective-permute-done | bytes 131104 | tf_op jit(solution)/shard_map/ppermute | solution.py:267
  34.1 0.4 shard_map.119
  34.5 1.6 %collective-permute-start.15 = (bf16[64,1024]{1,0:T(8,128)(2,1)S(1)}, bf16[64,1024]{1,0:T(8,128)(2,1)S(1)}, u32[]{:S(2)}, u32[]{:S(2)}) collective-permute-start(bf16[64,1024]{1,0:T(8,128)(2,1)S(1)} %get-tuple-element.74), channel_id=1, source_target_pairs={{0,4},{2,6},{4,0},{6,2},{8,12},{10,14},{12,8},{14,10},{16,20},{18,... | collective-permute-start | bytes 393224 | tf_op jit(solution)/shard_map/ppermute | solution.py:267
  36.2 2.9 %collective-permute-start.14 = (bf16[64,1024]{1,0:T(8,128)(2,1)S(1)}, bf16[64,1024]{1,0:T(8,128)(2,1)S(1)}, u32[]{:S(2)}, u32[]{:S(2)}) collective-permute-start(bf16[64,1024]{1,0:T(8,128)(2,1)S(1)} %add_convert_fusion.1), channel_id=1, source_target_pairs={{0,16},{2,26},{4,20},{6,30},{8,24},{10,18},{12,28},{14,22},{16,0},... | collective-permute-start | bytes 393224 | tf_op jit(solution)/shard_map/ppermute | solution.py:264
  39.0 1.8 %collective-permute-done.15 = bf16[64,1024]{1,0:T(8,128)(2,1)S(1)} collective-permute-done((bf16[64,1024]{1,0:T(8,128)(2,1)S(1)}, bf16[64,1024]{1,0:T(8,128)(2,1)S(1)}, u32[]{:S(2)}, u32[]{:S(2)}) %collective-permute-start.15) | collective-permute-done | bytes 131104 | tf_op jit(solution)/shard_map/ppermute | solution.py:267
  40.9 2.7 %collective-permute-start.16 = (bf16[64,1024]{1,0:T(8,128)(2,1)S(1)}, bf16[64,1024]{1,0:T(8,128)(2,1)S(1)}, u32[]{:S(2)}, u32[]{:S(2)}) collective-permute-start(bf16[64,1024]{1,0:T(8,128)(2,1)S(1)} %add_convert_fusion), channel_id=1, source_target_pairs={{0,16},{2,26},{4,20},{6,30},{8,24},{10,18},{12,28},{14,22},{16,0},... | collective-permute-start | bytes 393224 | tf_op jit(solution)/shard_map/ppermute | solution.py:264
  43.5 1.6 %collective-permute-start.17 = (bf16[64,1024]{1,0:T(8,128)(2,1)S(1)}, bf16[64,1024]{1,0:T(8,128)(2,1)S(1)}, u32[]{:S(2)}, u32[]{:S(2)}) collective-permute-start(bf16[64,1024]{1,0:T(8,128)(2,1)S(1)} %get-tuple-element.77), channel_id=1, source_target_pairs={{0,4},{2,14},{4,0},{6,10},{8,12},{10,6},{12,8},{14,2},{16,20},{18,... | collective-permute-start | bytes 393224 | tf_op jit(solution)/shard_map/ppermute | solution.py:264
  45.2 2.8 %shard_map.117 = (f32[256,2048]{1,0:T(8,128)}, f32[256,2048]{1,0:T(8,128)}) custom-call(f32[256,2048]{1,0:T(8,128)} %refs_0_.6, f32[256,2048]{1,0:T(8,128)} %refs_1_.7, f32[256,2048]{1,0:T(8,128)} %refs_2_.7, f32[256,2048]{1,0:T(8,128)} %get-tuple-element.55.refs_3_, f32[256,2048]{1,0:T(8,128)} %get-tuple-element.56.refs_4_), custom_call_target="tpu_custom_call", output_to_operand_aliasing={{0}: (3, {}), {1}: (4, {})} | custom-call | bytes 31457280 | tf_op jit(solution)/shard_map/pallas_call | solution.py:152
  48.0 0.0 copy-start.2
  48.0 0.0 collective-permute-done.11
  48.0 0.0 collective-permute-done.10
  48.0 0.0 collective-permute-done.14
  48.0 2.5 %collective-permute-done.16 = bf16[64,1024]{1,0:T(8,128)(2,1)S(1)} collective-permute-done((bf16[64,1024]{1,0:T(8,128)(2,1)S(1)}, bf16[64,1024]{1,0:T(8,128)(2,1)S(1)}, u32[]{:S(2)}, u32[]{:S(2)}) %collective-permute-start.16) | collective-permute-done | bytes 131104 | tf_op jit(solution)/shard_map/ppermute | solution.py:264
  50.5 0.0 collective-permute-done.17
  50.5 0.1 convert_add_fusion
  50.6 0.1 maximum_add_fusion
  50.7 0.1 collective-permute-start.18
  50.8 1.5 %collective-permute-done.18 = f32[2,32,1024]{2,1,0:T(8,128)S(1)} collective-permute-done((f32[2,32,1024]{2,1,0:T(8,128)S(1)}, f32[2,32,1024]{2,1,0:T(8,128)S(1)}, u32[]{:S(2)}, u32[]{:S(2)}) %collective-permute-start.18) | collective-permute-done | bytes 262176 | tf_op jit(solution)/shard_map/ppermute | solution.py:260
  52.3 0.0 copy-done.2
  52.3 0.7 %reverse_select_fusion = bf16[2,32,1024]{2,1,0:T(8,128)(2,1)} fusion(bf16[2,32,1024]{2,1,0:T(8,128)(2,1)S(1)} %fusion.3, pred[]{:T(512)S(6)} %eq.9), kind=kLoop, calls=%fused_computation.12 | loop fusion | flops 65536 | bytes 262145 | tf_op jit(solution)/shard_map/jit(_where)/select_n | solution.py:337
  (5 shorter events, 0.1 us)
Async XLA Ops:
  0.6 5.8 %copy-start = (bf16[32,8192]{1,0:T(8,128)(2,1)S(1)}, bf16[32,8192]{1,0:T(8,128)(2,1)}, u32[]{:S(2)}) copy-start(bf16[32,8192]{1,0:T(8,128)(2,1)} %ours_ref.1) | copy-start | bytes 1572868
  0.6 5.8 %copy-start.1 = (f32[8192]{0:T(1024)S(1)}, f32[8192]{0:T(1024)}, u32[]{:S(2)}) copy-start(f32[8192]{0:T(1024)} %param.10) | copy-start | bytes 98308
  0.6 3.1 %collective-permute-start = (bf16[32,8192]{1,0:T(8,128)(2,1)}, bf16[32,8192]{1,0:T(8,128)(2,1)S(1)}, u32[]{:S(2)}, u32[]{:S(2)}) collective-permute-start(bf16[32,8192]{1,0:T(8,128)(2,1)} %ours_ref.1), channel_id=1, source_target_pairs={{0,2},{2,0},{4,6},{6,4},{8,10},{10,8},{12,14},{14,12},{16,18},{18,... | collective-permute-start | bytes 1572872 | tf_op jit(solution)/shard_map/ppermute | solution.py:260
  3.8 20.5 %collective-permute-start.3 = (bf16[256,1024]{1,0:T(8,128)(2,1)S(1)}, bf16[256,1024]{1,0:T(8,128)(2,1)S(1)}, u32[]{:S(2)}, u32[]{:S(2)}) collective-permute-start(bf16[256,1024]{1,0:T(8,128)(2,1)S(1)} %shard_map.114), channel_id=1, source_target_pairs={{0,1},{1,0},{2,3},{3,2},{4,5},{5,4},{6,7},{7,6},{8,9},{9,8},{10,11... | collective-permute-start | bytes 1572872 | tf_op jit(solution)/shard_map/ppermute | solution.py:257
  6.8 7.7 %collective-permute-start.4 = (bf16[64,1024]{1,0:T(8,128)(2,1)S(1)}, bf16[64,1024]{1,0:T(8,128)(2,1)S(1)}, u32[]{:S(2)}, u32[]{:S(2)}) collective-permute-start(bf16[64,1024]{1,0:T(8,128)(2,1)S(1)} %get-tuple-element.50), channel_id=1, source_target_pairs={{0,0},{2,10},{4,4},{6,14},{8,8},{10,2},{12,12},{14,6},{16,16},{18,... | collective-permute-start | bytes 393224 | tf_op jit(solution)/shard_map/ppermute | solution.py:264
  7.5 7.1 %collective-permute-start.5 = (bf16[64,1024]{1,0:T(8,128)(2,1)S(1)}, bf16[64,1024]{1,0:T(8,128)(2,1)S(1)}, u32[]{:S(2)}, u32[]{:S(2)}) collective-permute-start(bf16[64,1024]{1,0:T(8,128)(2,1)S(1)} %get-tuple-element.51), channel_id=1, source_target_pairs={{0,4},{2,14},{4,0},{6,10},{8,12},{10,6},{12,8},{14,2},{16,20},{18,... | collective-permute-start | bytes 393224 | tf_op jit(solution)/shard_map/ppermute | solution.py:264
  9.1 12.0 %collective-permute-start.1 = (bf16[64,1024]{1,0:T(8,128)(2,1)S(1)}, bf16[64,1024]{1,0:T(8,128)(2,1)S(1)}, u32[]{:S(2)}, u32[]{:S(2)}) collective-permute-start(bf16[64,1024]{1,0:T(8,128)(2,1)S(1)} %get-tuple-element.47), channel_id=1, source_target_pairs={{0,16},{2,26},{4,20},{6,30},{8,24},{10,18},{12,28},{14,22},{16,0},... | collective-permute-start | bytes 393224 | tf_op jit(solution)/shard_map/ppermute | solution.py:264
  11.6 12.6 %collective-permute-start.2 = (bf16[64,1024]{1,0:T(8,128)(2,1)S(1)}, bf16[64,1024]{1,0:T(8,128)(2,1)S(1)}, u32[]{:S(2)}, u32[]{:S(2)}) collective-permute-start(bf16[64,1024]{1,0:T(8,128)(2,1)S(1)} %get-tuple-element.48), channel_id=1, source_target_pairs={{0,20},{2,30},{4,16},{6,26},{8,28},{10,22},{12,24},{14,18},{16,4},... | collective-permute-start | bytes 393224 | tf_op jit(solution)/shard_map/ppermute | solution.py:264
  14.6 9.7 %collective-permute-start.6 = (bf16[64,1024]{1,0:T(8,128)(2,1)S(1)}, bf16[64,1024]{1,0:T(8,128)(2,1)S(1)}, u32[]{:S(2)}, u32[]{:S(2)}) collective-permute-start(bf16[64,1024]{1,0:T(8,128)(2,1)S(1)} %collective-permute-done.4.refs_6_), channel_id=1, source_target_pairs={{0,1},{1,0},{2,3},{3,2},{4,5},{5,4},{6,7},{7,6},{8,9},{9,8},{10,11... | collective-permute-start | bytes 393224 | tf_op jit(solution)/shard_map/ppermute | solution.py:257
  14.9 9.4 %collective-permute-start.7 = (bf16[64,1024]{1,0:T(8,128)(2,1)S(1)}, bf16[64,1024]{1,0:T(8,128)(2,1)S(1)}, u32[]{:S(2)}, u32[]{:S(2)}) collective-permute-start(bf16[64,1024]{1,0:T(8,128)(2,1)S(1)} %collective-permute-done.5.refs_7_), channel_id=1, source_target_pairs={{0,1},{1,0},{2,3},{3,2},{4,5},{5,4},{6,7},{7,6},{8,9},{9,8},{10,11... | collective-permute-start | bytes 393224 | tf_op jit(solution)/shard_map/ppermute | solution.py:257
  21.1 5.3 %collective-permute-start.8 = (bf16[256,1024]{1,0:T(8,128)(2,1)S(1)}, bf16[256,1024]{1,0:T(8,128)(2,1)S(1)}, u32[]{:S(2)}, u32[]{:S(2)}) collective-permute-start(bf16[256,1024]{1,0:T(8,128)(2,1)S(1)} %shard_map.116.refs_0_), channel_id=1, source_target_pairs={{0,2},{2,0},{4,6},{6,4},{8,10},{10,8},{12,14},{14,12},{16,18},{18,... | collective-permute-start | bytes 1572872 | tf_op jit(solution)/shard_map/ppermute | solution.py:260
  24.2 2.2 %collective-permute-start.9 = (bf16[256,1024]{1,0:T(8,128)(2,1)S(1)}, bf16[256,1024]{1,0:T(8,128)(2,1)S(1)}, u32[]{:S(2)}, u32[]{:S(2)}) collective-permute-start(bf16[256,1024]{1,0:T(8,128)(2,1)S(1)} %collective-permute-done.3.refs_1_), channel_id=1, source_target_pairs={{0,2},{2,0},{4,6},{6,4},{8,10},{10,8},{12,14},{14,12},{16,18},{18,... | collective-permute-start | bytes 1572872 | tf_op jit(solution)/shard_map/ppermute | solution.py:260
  24.4 9.0 %collective-permute-start.13 = (bf16[128,1024]{1,0:T(8,128)(2,1)S(1)}, bf16[128,1024]{1,0:T(8,128)(2,1)S(1)}, u32[]{:S(2)}, u32[]{:S(2)}) collective-permute-start(bf16[128,1024]{1,0:T(8,128)(2,1)S(1)} %pad_maximum_fusion), channel_id=1, source_target_pairs={{0,1},{1,0},{2,3},{3,2},{4,5},{5,4},{6,7},{7,6},{8,9},{9,8},{10,11... | collective-permute-start | bytes 786440 | tf_op jit(solution)/shard_map/ppermute | solution.py:257
  28.4 5.7 %collective-permute-start.12 = (bf16[64,1024]{1,0:T(8,128)(2,1)S(1)}, bf16[64,1024]{1,0:T(8,128)(2,1)S(1)}, u32[]{:S(2)}, u32[]{:S(2)}) collective-permute-start(bf16[64,1024]{1,0:T(8,128)(2,1)S(1)} %get-tuple-element.69), channel_id=1, source_target_pairs={{0,4},{2,6},{4,0},{6,2},{8,12},{10,14},{12,8},{14,10},{16,20},{18,... | collective-permute-start | bytes 393224 | tf_op jit(solution)/shard_map/ppermute | solution.py:267
  30.0 18.0 %collective-permute-start.10 = (bf16[128,1024]{1,0:T(8,128)(2,1)S(1)}, bf16[128,1024]{1,0:T(8,128)(2,1)S(1)}, u32[]{:S(2)}, u32[]{:S(2)}) collective-permute-start(bf16[128,1024]{1,0:T(8,128)(2,1)S(1)} %get-tuple-element.66), channel_id=1, source_target_pairs={{0,0},{2,10},{4,4},{6,14},{8,8},{10,2},{12,12},{14,6},{16,16},{18,... | collective-permute-start | bytes 786440 | tf_op jit(solution)/shard_map/ppermute | solution.py:264
  30.7 17.4 %collective-permute-start.11 = (bf16[64,1024]{1,0:T(8,128)(2,1)S(1)}, bf16[64,1024]{1,0:T(8,128)(2,1)S(1)}, u32[]{:S(2)}, u32[]{:S(2)}) collective-permute-start(bf16[64,1024]{1,0:T(8,128)(2,1)S(1)} %get-tuple-element.67), channel_id=1, source_target_pairs={{0,4},{2,14},{4,0},{6,10},{8,12},{10,6},{12,8},{14,2},{16,20},{18,... | collective-permute-start | bytes 393224 | tf_op jit(solution)/shard_map/ppermute | solution.py:264
  34.5 6.3 %collective-permute-start.15 = (bf16[64,1024]{1,0:T(8,128)(2,1)S(1)}, bf16[64,1024]{1,0:T(8,128)(2,1)S(1)}, u32[]{:S(2)}, u32[]{:S(2)}) collective-permute-start(bf16[64,1024]{1,0:T(8,128)(2,1)S(1)} %get-tuple-element.74), channel_id=1, source_target_pairs={{0,4},{2,6},{4,0},{6,2},{8,12},{10,14},{12,8},{14,10},{16,20},{18,... | collective-permute-start | bytes 393224 | tf_op jit(solution)/shard_map/ppermute | solution.py:267
  36.2 11.9 %collective-permute-start.14 = (bf16[64,1024]{1,0:T(8,128)(2,1)S(1)}, bf16[64,1024]{1,0:T(8,128)(2,1)S(1)}, u32[]{:S(2)}, u32[]{:S(2)}) collective-permute-start(bf16[64,1024]{1,0:T(8,128)(2,1)S(1)} %add_convert_fusion.1), channel_id=1, source_target_pairs={{0,16},{2,26},{4,20},{6,30},{8,24},{10,18},{12,28},{14,22},{16,0},... | collective-permute-start | bytes 393224 | tf_op jit(solution)/shard_map/ppermute | solution.py:264
  40.9 9.7 %collective-permute-start.16 = (bf16[64,1024]{1,0:T(8,128)(2,1)S(1)}, bf16[64,1024]{1,0:T(8,128)(2,1)S(1)}, u32[]{:S(2)}, u32[]{:S(2)}) collective-permute-start(bf16[64,1024]{1,0:T(8,128)(2,1)S(1)} %add_convert_fusion), channel_id=1, source_target_pairs={{0,16},{2,26},{4,20},{6,30},{8,24},{10,18},{12,28},{14,22},{16,0},... | collective-permute-start | bytes 393224 | tf_op jit(solution)/shard_map/ppermute | solution.py:264
  43.5 7.0 %collective-permute-start.17 = (bf16[64,1024]{1,0:T(8,128)(2,1)S(1)}, bf16[64,1024]{1,0:T(8,128)(2,1)S(1)}, u32[]{:S(2)}, u32[]{:S(2)}) collective-permute-start(bf16[64,1024]{1,0:T(8,128)(2,1)S(1)} %get-tuple-element.77), channel_id=1, source_target_pairs={{0,4},{2,14},{4,0},{6,10},{8,12},{10,6},{12,8},{14,2},{16,20},{18,... | collective-permute-start | bytes 393224 | tf_op jit(solution)/shard_map/ppermute | solution.py:264
  48.0 4.3 %copy-start.2 = (f32[1024]{0:T(1024)S(1)}, f32[1024]{0:T(1024)}, u32[]{:S(2)}) copy-start(f32[1024]{0:T(1024)} %param.12) | copy-start | bytes 12292
  50.7 1.6 %collective-permute-start.18 = (f32[2,32,1024]{2,1,0:T(8,128)S(1)}, f32[2,32,1024]{2,1,0:T(8,128)S(1)}, u32[]{:S(2)}, u32[]{:S(2)}) collective-permute-start(f32[2,32,1024]{2,1,0:T(8,128)S(1)} %select_bitcast_fusion), channel_id=1, source_target_pairs={{0,2},{2,0},{4,6},{6,4},{8,10},{10,8},{12,14},{14,12},{16,18},{18,... | collective-permute-start | bytes 786440 | tf_op jit(solution)/shard_map/ppermute | solution.py:260

commit v6 on v5

--- a/solution.py
+++ b/solution.py
@@ -293,19 +293,21 @@
     shared = shared + [over_core(x) for x in shared]
     peers = range(1, heads)
     evens, odds = remote[::2], remote[1::2]
-    labels = [(0, m) for m in order] + [(j, m) for j in peers for m in near]
-    plan = [[(0, m)] for m in (*evens, *odds)] + [[(j, m) for j in range(heads)] for m in near[::2]]
+    labels = [(0, m) for m in remote]
+    plan = [[(0, m)] for m in (*evens, *odds)]
+    types = [F32] * len(evens) + [BF16] * len(odds)
+    weight, *parts = merge_product(held, shared, distant, heads, labels, plan, types)
+    ours_even, ours_odd = parts[: len(evens)], parts[len(evens) :]
+    met = [over_next(x) for x in ours_odd]
+    labels = [(j, m) for j in range(heads) for m in near]
+    plan = [[(j, m) for j in range(heads)] for m in near[::2]]
     plan += [[(j, m) for j in group] for group in ([0], peers) for m in near[1::2]]
-    types = [F32] * len(evens) + [BF16] * (len(odds) + len(near) + len(near[1::2]))
-    blocks = [*distant, *close, *[x for row in moved_close for x in row]]
-    weight, *parts = merge_product(held, shared, blocks, heads, labels, plan, types)
-    ours_even, ours_odd, parts_near = parts[: len(evens)], parts[len(evens) : len(remote)], parts[len(remote) :]
-    met = [over_next(x) for x in ours_odd]
+    blocks = [*close, *[x for row in moved_close for x in row]]
+    parts_near = product(blocks, weight, labels, plan, [BF16] * len(plan))
     split = len(near[::2])
     last = split + len(near[1::2])
     terms_near = [over_slab(x, m) for x, m in zip(parts_near[:split], near[::2])]
-    terms_ours = [over_slab(x, m) for x, m in zip(parts_near[split:last], near[1::2])]
-    late = parts_near[last:]
+    late = parts_near[split:]
     met, moved_distant = lax.optimization_barrier((met, moved_distant))
 
     labels = [(j, m) for j in peers for m in remote]
@@ -317,10 +319,11 @@
     def onward(even, arrived):
         return [over_slab((x + y.astype(F32)).astype(BF16), m) for x, y, m in zip(even, arrived, evens)]
 
-    terms_ours += onward(ours_even, met)
+    terms_ours = onward(ours_even, met)
     met_theirs, late = lax.optimization_barrier((met_theirs, late))
     terms_theirs = onward(theirs_even, met_theirs)
-    terms_theirs += [over_slab(x, m) for x, m in zip(late, near[1::2])]
+    terms_theirs += [over_slab(x, m) for x, m in zip(late[last - split :], near[1::2])]
+    terms_ours += [over_slab(x, m) for x, m in zip(late, near[1::2])]
     new_first, new_second = moments(arrays[:3], bulk, first_rows - bulk, made)
     new_first, new_second, terms_near, terms_ours, terms_theirs = lax.optimization_barrier(
         (new_first, new_second, terms_near, terms_ours, terms_theirs)
@@ -332,7 +335,7 @@
     total = added(terms_near) + jnp.concatenate([added(terms_ours), added(terms_theirs)], axis=0)
     keep = jnp.where(core == 0, total[:, 0], total[:, 1])
     give = jnp.where(core == 0, total[:, 1], total[:, 0])
-    results = (keep + over_core(give) + bias).astype(BF16)
+    results = (keep + over_core(give.astype(BF16)).astype(F32) + bias).astype(BF16)
     if heads == 2:
         ordered = jnp.where(mine == 0, results, results[::-1])
     else:

time: 53.3 us -> 53.1 us (level)
    ppermute x2, waiting for transfers between devices: 2.49 us -> 1.16 us  [over_next(): return lax.ppermute(x, 'dp', [(i, i ^ PAIR) for i in range(replicas)])]
    ppermute x9, waiting for transfers between devices: 3.4 us -> 4.62 us  [over_slab(): return lax.ppermute(x, 'dp', pairs)]
    pallas_call x1 -> x2, Pallas kernels: 0.45 us -> 1.15 us  [product(): pl.pallas_call(functools.partial(product_kernel, labels, plan), out_shape...]
  transfers between devices with their start and end apart: 19 -> 19, of which waited for: 6 -> 8; matrix products, arithmetic and copies ran while one was open for 0% -> 0% of each run, Pallas kernels for 29% -> 29%
where the time goes in v6:
time: 53.1 us; the launch traced here: 52.9 us
  starting transfers between devices  26 us (49%)
  Pallas kernels  15.4 us (29%)
  waiting for transfers between devices  9.64 us (18%)
  other arithmetic  0.96 us (2%)
  between operations  0.85 us (2%)
    ppermute x9, starting transfers between devices, over_slab(): return lax.ppermute(x, 'dp', pairs)  13.1 us
    ppermute x4, starting transfers between devices, over_tensor(): lax.ppermute(x, 'tensor', [(i, i ^ j) for i in range(heads)])  6.72 us
    pallas_call x2, Pallas kernels, moments(): pl.pallas_call(functools.partial(moments_kernel, start, size, chunks), in...  5.64 us
    pallas_call x2, Pallas kernels, delta(): pl.pallas_call(functools.partial(delta_kernel, chunks, qrows, qcol, heads...  5.2 us
    ppermute x9, waiting for transfers between devices, over_slab(): return lax.ppermute(x, 'dp', pairs)  4.62 us
    ppermute x2, starting transfers between devices, over_next(): return lax.ppermute(x, 'dp', [(i, i ^ PAIR) for i in range(replicas)])  3.19 us
    ppermute x4, starting transfers between devices, over_core(): return lax.ppermute(x, 'dp', [(i, i ^ 1) for i in range(replicas)])  3 us
    ppermute x4, waiting for transfers between devices, over_tensor(): lax.ppermute(x, 'tensor', [(i, i ^ j) for i in range(heads)])  2.53 us
  transfers between devices with their start and end apart: 19, of which 8 were waited for; matrix products, arithmetic and copies ran while one was open for 0% of the time, Pallas kernels for 29%

profile of v6, /device:TPU:0, one launch (start us, length us, event | category | flops | bytes accessed | tf_op | source)
XLA Modules:
  0.0 52.9 jit_solution(5056373661167273848)
XLA Ops:
  0.6 0.0 copy-start
  0.6 0.0 copy-start.1
  0.6 0.5 collective-permute-start
  1.2 2.6 %shard_map.114 = bf16[256,1024]{1,0:T(8,128)(2,1)S(1)} custom-call(s32[8,16]{1,0:T(8,128)} %refs_0_.5, f32[256,2048]{1,0:T(8,128)} %refs_0_.6, f32[256,2048]{1,0:T(8,128)} %refs_1_.7, f32[256,2048]{1,0:T(8,128)} %refs_2_.7, f32[256,2048]{1,0:T(8,128)} %refs_4_.3), custom_call_target="tpu_custom_call" | custom-call | tf_op jit(solution)/shard_map/pallas_call | solution.py:107
  3.8 0.0 collective-permute-done.theirs_ref
  3.8 2.6 %collective-permute-start.3 = (bf16[256,1024]{1,0:T(8,128)(2,1)S(1)}, bf16[256,1024]{1,0:T(8,128)(2,1)S(1)}, u32[]{:S(2)}, u32[]{:S(2)}) collective-permute-start(bf16[256,1024]{1,0:T(8,128)(2,1)S(1)} %shard_map.114), channel_id=1, source_target_pairs={{0,1},{1,0},{2,3},{3,2},{4,5},{5,4},{6,7},{7,6},{8,9},{9,8},{10,11... | collective-permute-start | bytes 1572872 | tf_op jit(solution)/shard_map/ppermute | solution.py:257
  6.4 0.0 copy-done
  6.4 0.0 copy-done.1
  6.4 0.4 shard_map.115
  6.8 0.7 %collective-permute-start.4 = (bf16[64,1024]{1,0:T(8,128)(2,1)S(1)}, bf16[64,1024]{1,0:T(8,128)(2,1)S(1)}, u32[]{:S(2)}, u32[]{:S(2)}) collective-permute-start(bf16[64,1024]{1,0:T(8,128)(2,1)S(1)} %get-tuple-element.51), channel_id=1, source_target_pairs={{0,0},{2,10},{4,4},{6,14},{8,8},{10,2},{12,12},{14,6},{16,16},{18,... | collective-permute-start | bytes 393224 | tf_op jit(solution)/shard_map/ppermute | solution.py:264
  7.5 1.6 %collective-permute-start.5 = (bf16[64,1024]{1,0:T(8,128)(2,1)S(1)}, bf16[64,1024]{1,0:T(8,128)(2,1)S(1)}, u32[]{:S(2)}, u32[]{:S(2)}) collective-permute-start(bf16[64,1024]{1,0:T(8,128)(2,1)S(1)} %get-tuple-element.52), channel_id=1, source_target_pairs={{0,4},{2,14},{4,0},{6,10},{8,12},{10,6},{12,8},{14,2},{16,20},{18,... | collective-permute-start | bytes 393224 | tf_op jit(solution)/shard_map/ppermute | solution.py:264
  9.1 2.6 %collective-permute-start.1 = (bf16[64,1024]{1,0:T(8,128)(2,1)S(1)}, bf16[64,1024]{1,0:T(8,128)(2,1)S(1)}, u32[]{:S(2)}, u32[]{:S(2)}) collective-permute-start(bf16[64,1024]{1,0:T(8,128)(2,1)S(1)} %get-tuple-element.48), channel_id=1, source_target_pairs={{0,16},{2,26},{4,20},{6,30},{8,24},{10,18},{12,28},{14,22},{16,0},... | collective-permute-start | bytes 393224 | tf_op jit(solution)/shard_map/ppermute | solution.py:264
  11.6 0.3 collective-permute-start.2
  11.9 2.6 %shard_map.116.refs_0_ = bf16[256,1024]{1,0:T(8,128)(2,1)S(1)} custom-call(s32[8,16]{1,0:T(8,128)} %refs_0_.5, f32[256,2048]{1,0:T(8,128)} %refs_0_.6, f32[256,2048]{1,0:T(8,128)} %refs_1_.7, f32[256,2048]{1,0:T(8,128)} %refs_2_.7, f32[256,2048]{1,0:T(8,128)} %refs_4_.3), custom_call_target="tpu_custom_call" | custom-call | tf_op jit(solution)/shard_map/pallas_call | solution.py:107
  14.5 0.0 collective-permute-done.4.refs_0_
  14.5 0.0 collective-permute-done.5.refs_1_
  14.6 0.3 collective-permute-start.6
  14.9 1.8 %collective-permute-start.7 = (bf16[64,1024]{1,0:T(8,128)(2,1)S(1)}, bf16[64,1024]{1,0:T(8,128)(2,1)S(1)}, u32[]{:S(2)}, u32[]{:S(2)}) collective-permute-start(bf16[64,1024]{1,0:T(8,128)(2,1)S(1)} %collective-permute-done.5.refs_1_), channel_id=1, source_target_pairs={{0,1},{1,0},{2,3},{3,2},{4,5},{5,4},{6,7},{7,6},{8,9},{9,8},{10,11... | collective-permute-start | bytes 393224 | tf_op jit(solution)/shard_map/ppermute | solution.py:257
  16.6 2.8 %shard_map.112 = (f32[256,2048]{1,0:T(8,128)}, f32[256,2048]{1,0:T(8,128)}) custom-call(f32[256,2048]{1,0:T(8,128)} %refs_0_.6, f32[256,2048]{1,0:T(8,128)} %refs_1_.7, f32[256,2048]{1,0:T(8,128)} %refs_2_.7), custom_call_target="tpu_custom_call" | custom-call | bytes 31457280 | tf_op jit(solution)/shard_map/pallas_call | solution.py:152
  19.5 1.6 %shard_map.113.stale_ref = bf16[4,256,1024]{2,1,0:T(8,128)(2,1)S(1)} custom-call(bf16[8192,1024]{1,0:T(8,128)(2,1)} %stale_far.1), custom_call_target="tpu_custom_call" | custom-call | tf_op jit(solution)/shard_map/pallas_call | solution.py:198
  21.0 0.0 collective-permute-done.1.refs_4_
  21.1 2.3 %collective-permute-start.8 = (bf16[256,1024]{1,0:T(8,128)(2,1)S(1)}, bf16[256,1024]{1,0:T(8,128)(2,1)S(1)}, u32[]{:S(2)}, u32[]{:S(2)}) collective-permute-start(bf16[256,1024]{1,0:T(8,128)(2,1)S(1)} %shard_map.116.refs_0_), channel_id=1, source_target_pairs={{0,2},{2,0},{4,6},{6,4},{8,10},{10,8},{12,14},{14,12},{16,18},{18,... | collective-permute-start | bytes 1572872 | tf_op jit(solution)/shard_map/ppermute | solution.py:260
  23.3 0.9 %collective-permute-done.2.refs_5_ = bf16[64,1024]{1,0:T(8,128)(2,1)S(1)} collective-permute-done((bf16[64,1024]{1,0:T(8,128)(2,1)S(1)}, bf16[64,1024]{1,0:T(8,128)(2,1)S(1)}, u32[]{:S(2)}, u32[]{:S(2)}) %collective-permute-start.2) | collective-permute-done | bytes 131104 | tf_op jit(solution)/shard_map/ppermute | solution.py:264
  24.2 0.0 collective-permute-done.6.refs_2_
  24.2 0.0 collective-permute-done.7.refs_3_
  24.2 0.0 collective-permute-done.3.refs_1_
  24.2 0.1 collective-permute-start.9
  24.4 2.0 %collective-permute-start.12 = (bf16[128,1024]{1,0:T(8,128)(2,1)S(1)}, bf16[128,1024]{1,0:T(8,128)(2,1)S(1)}, u32[]{:S(2)}, u32[]{:S(2)}) collective-permute-start(bf16[128,1024]{1,0:T(8,128)(2,1)S(1)} %pad_maximum_fusion), channel_id=1, source_target_pairs={{0,1},{1,0},{2,3},{3,2},{4,5},{5,4},{6,7},{7,6},{8,9},{9,8},{10,11... | collective-permute-start | bytes 786440 | tf_op jit(solution)/shard_map/ppermute | solution.py:257
  26.4 0.0 collective-permute-done.8.refs_2_
  26.4 0.0 collective-permute-done.9.refs_3_
  26.4 1.4 %shard_map.118 = (bf16[1024,1024]{1,0:T(8,128)(2,1)S(1)}, f32[64,1024]{1,0:T(8,128)S(1)}, bf16[64,1024]{1,0:T(8,128)(2,1)S(1)}) custom-call(bf16[4,256,1024]{2,1,0:T(8,128)(2,1)S(1)} %shard_map.113.stale_ref, bf16[256,1024]{1,0:T(8,128)(2,1)S(1)} %shard_map.116.refs_0_, bf16[256,1024]{1,0:T(8,128)(2,1)S(1)} %collective-permute-done.3.refs_1_, ...), custom_call_target="tpu_custom_call" | custom-call | bytes 8388608 | tf_op jit(solution)/shard_map/pallas_call | solution.py:229
  27.9 1.6 %collective-permute-start.11 = (bf16[64,1024]{1,0:T(8,128)(2,1)S(1)}, bf16[64,1024]{1,0:T(8,128)(2,1)S(1)}, u32[]{:S(2)}, u32[]{:S(2)}) collective-permute-start(bf16[64,1024]{1,0:T(8,128)(2,1)S(1)} %get-tuple-element.70), channel_id=1, source_target_pairs={{0,4},{2,6},{4,0},{6,2},{8,12},{10,14},{12,8},{14,10},{16,20},{18,... | collective-permute-start | bytes 393224 | tf_op jit(solution)/shard_map/ppermute | solution.py:267
  29.5 0.7 %shard_map.119 = (bf16[128,1024]{1,0:T(8,128)(2,1)S(1)}, bf16[64,1024]{1,0:T(8,128)(2,1)S(1)}, bf16[64,1024]{1,0:T(8,128)(2,1)S(1)}) custom-call(bf16[64,1024]{1,0:T(8,128)(2,1)S(1)} %collective-permute-done.4.refs_0_, bf16[64,1024]{1,0:T(8,128)(2,1)S(1)} %collective-permute-done.5.refs_1_, bf16[64,1024]{1,0:T(8,128)(2,1)S(1)} %collective-permute-done.6.refs_2_, ...), custom_call_target="tpu_custom_call" | custom-call | tf_op jit(solution)/shard_map/pallas_call | solution.py:239
  30.2 0.7 %collective-permute-start.10 = (bf16[128,1024]{1,0:T(8,128)(2,1)S(1)}, bf16[128,1024]{1,0:T(8,128)(2,1)S(1)}, u32[]{:S(2)}, u32[]{:S(2)}) collective-permute-start(bf16[128,1024]{1,0:T(8,128)(2,1)S(1)} %get-tuple-element.68), channel_id=1, source_target_pairs={{0,0},{2,10},{4,4},{6,14},{8,8},{10,2},{12,12},{14,6},{16,16},{18,... | collective-permute-start | bytes 786440 | tf_op jit(solution)/shard_map/ppermute | solution.py:264
  30.9 2.5 %collective-permute-done.12.refs_0_ = bf16[128,1024]{1,0:T(8,128)(2,1)S(1)} collective-permute-done((bf16[128,1024]{1,0:T(8,128)(2,1)S(1)}, bf16[128,1024]{1,0:T(8,128)(2,1)S(1)}, u32[]{:S(2)}, u32[]{:S(2)}) %collective-permute-start.12) | collective-permute-done | bytes 262176 | tf_op jit(solution)/shard_map/ppermute | solution.py:257
  33.4 0.2 collective-permute-done.11
  33.6 0.4 shard_map.120
  34.0 1.6 %collective-permute-start.14 = (bf16[64,1024]{1,0:T(8,128)(2,1)S(1)}, bf16[64,1024]{1,0:T(8,128)(2,1)S(1)}, u32[]{:S(2)}, u32[]{:S(2)}) collective-permute-start(bf16[64,1024]{1,0:T(8,128)(2,1)S(1)} %get-tuple-element.73), channel_id=1, source_target_pairs={{0,4},{2,6},{4,0},{6,2},{8,12},{10,14},{12,8},{14,10},{16,20},{18,... | collective-permute-start | bytes 393224 | tf_op jit(solution)/shard_map/ppermute | solution.py:267
  35.6 2.9 %collective-permute-start.13 = (bf16[64,1024]{1,0:T(8,128)(2,1)S(1)}, bf16[64,1024]{1,0:T(8,128)(2,1)S(1)}, u32[]{:S(2)}, u32[]{:S(2)}) collective-permute-start(bf16[64,1024]{1,0:T(8,128)(2,1)S(1)} %add_convert_fusion.1), channel_id=1, source_target_pairs={{0,16},{2,26},{4,20},{6,30},{8,24},{10,18},{12,28},{14,22},{16,0},... | collective-permute-start | bytes 393224 | tf_op jit(solution)/shard_map/ppermute | solution.py:264
  38.5 1.0 %collective-permute-done.14 = bf16[64,1024]{1,0:T(8,128)(2,1)S(1)} collective-permute-done((bf16[64,1024]{1,0:T(8,128)(2,1)S(1)}, bf16[64,1024]{1,0:T(8,128)(2,1)S(1)}, u32[]{:S(2)}, u32[]{:S(2)}) %collective-permute-start.14) | collective-permute-done | bytes 131104 | tf_op jit(solution)/shard_map/ppermute | solution.py:267
  39.5 2.4 %collective-permute-start.16 = (bf16[64,1024]{1,0:T(8,128)(2,1)S(1)}, bf16[64,1024]{1,0:T(8,128)(2,1)S(1)}, u32[]{:S(2)}, u32[]{:S(2)}) collective-permute-start(bf16[64,1024]{1,0:T(8,128)(2,1)S(1)} %add_convert_fusion), channel_id=1, source_target_pairs={{0,16},{2,26},{4,20},{6,30},{8,24},{10,18},{12,28},{14,22},{16,0},... | collective-permute-start | bytes 393224 | tf_op jit(solution)/shard_map/ppermute | solution.py:264
  42.0 1.5 %collective-permute-start.15 = (bf16[64,1024]{1,0:T(8,128)(2,1)S(1)}, bf16[64,1024]{1,0:T(8,128)(2,1)S(1)}, u32[]{:S(2)}, u32[]{:S(2)}) collective-permute-start(bf16[64,1024]{1,0:T(8,128)(2,1)S(1)} %get-tuple-element.76), channel_id=1, source_target_pairs={{0,4},{2,14},{4,0},{6,10},{8,12},{10,6},{12,8},{14,2},{16,20},{18,... | collective-permute-start | bytes 393224 | tf_op jit(solution)/shard_map/ppermute | solution.py:264
  43.5 0.5 collective-permute-start.17
  44.0 2.8 %shard_map.117 = (f32[256,2048]{1,0:T(8,128)}, f32[256,2048]{1,0:T(8,128)}) custom-call(f32[256,2048]{1,0:T(8,128)} %refs_0_.6, f32[256,2048]{1,0:T(8,128)} %refs_1_.7, f32[256,2048]{1,0:T(8,128)} %refs_2_.7, f32[256,2048]{1,0:T(8,128)} %get-tuple-element.56.refs_3_, f32[256,2048]{1,0:T(8,128)} %get-tuple-element.57.refs_4_), custom_call_target="tpu_custom_call", output_to_operand_aliasing={{0}: (3, {}), {1}: (4, {})} | custom-call | bytes 31457280 | tf_op jit(solution)/shard_map/pallas_call | solution.py:152
  46.8 0.0 copy-start.2
  46.8 0.0 collective-permute-done.10
  46.8 1.4 %collective-permute-done.13 = bf16[64,1024]{1,0:T(8,128)(2,1)S(1)} collective-permute-done((bf16[64,1024]{1,0:T(8,128)(2,1)S(1)}, bf16[64,1024]{1,0:T(8,128)(2,1)S(1)}, u32[]{:S(2)}, u32[]{:S(2)}) %collective-permute-start.13) | collective-permute-done | bytes 131104 | tf_op jit(solution)/shard_map/ppermute | solution.py:264
  48.2 1.8 %collective-permute-done.16 = bf16[64,1024]{1,0:T(8,128)(2,1)S(1)} collective-permute-done((bf16[64,1024]{1,0:T(8,128)(2,1)S(1)}, bf16[64,1024]{1,0:T(8,128)(2,1)S(1)}, u32[]{:S(2)}, u32[]{:S(2)}) %collective-permute-start.16) | collective-permute-done | bytes 131104 | tf_op jit(solution)/shard_map/ppermute | solution.py:264
  50.1 0.0 collective-permute-done.15
  50.1 0.5 collective-permute-done.17
  50.5 0.1 convert_add_fusion
  50.6 0.1 maximum_add_fusion
  50.7 0.1 collective-permute-start.18
  50.8 1.3 %collective-permute-done.18 = bf16[2,32,1024]{2,1,0:T(8,128)(2,1)S(1)} collective-permute-done((bf16[2,32,1024]{2,1,0:T(8,128)(2,1)S(1)}, bf16[2,32,1024]{2,1,0:T(8,128)(2,1)S(1)}, u32[]{:S(2)}, u32[]{:S(2)}) %collective-permute-start.18) | collective-permute-done | bytes 131104 | tf_op jit(solution)/shard_map/ppermute | solution.py:260
  52.1 0.0 copy-done.2
  52.2 0.7 %reverse_select_fusion = bf16[2,32,1024]{2,1,0:T(8,128)(2,1)} fusion(bf16[2,32,1024]{2,1,0:T(8,128)(2,1)S(1)} %fusion.3, pred[]{:T(512)S(6)} %eq.9), kind=kLoop, calls=%fused_computation.12 | loop fusion | flops 65536 | bytes 262145 | tf_op jit(solution)/shard_map/jit(_where)/select_n | solution.py:340
  (5 shorter events, 0.1 us)
Async XLA Ops:
  0.6 5.8 %copy-start = (bf16[32,8192]{1,0:T(8,128)(2,1)S(1)}, bf16[32,8192]{1,0:T(8,128)(2,1)}, u32[]{:S(2)}) copy-start(bf16[32,8192]{1,0:T(8,128)(2,1)} %ours_ref.1) | copy-start | bytes 1572868
  0.6 5.8 %copy-start.1 = (f32[8192]{0:T(1024)S(1)}, f32[8192]{0:T(1024)}, u32[]{:S(2)}) copy-start(f32[8192]{0:T(1024)} %param.10) | copy-start | bytes 98308
  0.6 3.1 %collective-permute-start = (bf16[32,8192]{1,0:T(8,128)(2,1)}, bf16[32,8192]{1,0:T(8,128)(2,1)S(1)}, u32[]{:S(2)}, u32[]{:S(2)}) collective-permute-start(bf16[32,8192]{1,0:T(8,128)(2,1)} %ours_ref.1), channel_id=1, source_target_pairs={{0,2},{2,0},{4,6},{6,4},{8,10},{10,8},{12,14},{14,12},{16,18},{18,... | collective-permute-start | bytes 1572872 | tf_op jit(solution)/shard_map/ppermute | solution.py:260
  3.8 20.5 %collective-permute-start.3 = (bf16[256,1024]{1,0:T(8,128)(2,1)S(1)}, bf16[256,1024]{1,0:T(8,128)(2,1)S(1)}, u32[]{:S(2)}, u32[]{:S(2)}) collective-permute-start(bf16[256,1024]{1,0:T(8,128)(2,1)S(1)} %shard_map.114), channel_id=1, source_target_pairs={{0,1},{1,0},{2,3},{3,2},{4,5},{5,4},{6,7},{7,6},{8,9},{9,8},{10,11... | collective-permute-start | bytes 1572872 | tf_op jit(solution)/shard_map/ppermute | solution.py:257
  6.8 7.7 %collective-permute-start.4 = (bf16[64,1024]{1,0:T(8,128)(2,1)S(1)}, bf16[64,1024]{1,0:T(8,128)(2,1)S(1)}, u32[]{:S(2)}, u32[]{:S(2)}) collective-permute-start(bf16[64,1024]{1,0:T(8,128)(2,1)S(1)} %get-tuple-element.51), channel_id=1, source_target_pairs={{0,0},{2,10},{4,4},{6,14},{8,8},{10,2},{12,12},{14,6},{16,16},{18,... | collective-permute-start | bytes 393224 | tf_op jit(solution)/shard_map/ppermute | solution.py:264
  7.5 7.1 %collective-permute-start.5 = (bf16[64,1024]{1,0:T(8,128)(2,1)S(1)}, bf16[64,1024]{1,0:T(8,128)(2,1)S(1)}, u32[]{:S(2)}, u32[]{:S(2)}) collective-permute-start(bf16[64,1024]{1,0:T(8,128)(2,1)S(1)} %get-tuple-element.52), channel_id=1, source_target_pairs={{0,4},{2,14},{4,0},{6,10},{8,12},{10,6},{12,8},{14,2},{16,20},{18,... | collective-permute-start | bytes 393224 | tf_op jit(solution)/shard_map/ppermute | solution.py:264
  9.1 12.0 %collective-permute-start.1 = (bf16[64,1024]{1,0:T(8,128)(2,1)S(1)}, bf16[64,1024]{1,0:T(8,128)(2,1)S(1)}, u32[]{:S(2)}, u32[]{:S(2)}) collective-permute-start(bf16[64,1024]{1,0:T(8,128)(2,1)S(1)} %get-tuple-element.48), channel_id=1, source_target_pairs={{0,16},{2,26},{4,20},{6,30},{8,24},{10,18},{12,28},{14,22},{16,0},... | collective-permute-start | bytes 393224 | tf_op jit(solution)/shard_map/ppermute | solution.py:264
  11.6 12.6 %collective-permute-start.2 = (bf16[64,1024]{1,0:T(8,128)(2,1)S(1)}, bf16[64,1024]{1,0:T(8,128)(2,1)S(1)}, u32[]{:S(2)}, u32[]{:S(2)}) collective-permute-start(bf16[64,1024]{1,0:T(8,128)(2,1)S(1)} %get-tuple-element.49), channel_id=1, source_target_pairs={{0,20},{2,30},{4,16},{6,26},{8,28},{10,22},{12,24},{14,18},{16,4},... | collective-permute-start | bytes 393224 | tf_op jit(solution)/shard_map/ppermute | solution.py:264
  14.6 9.7 %collective-permute-start.6 = (bf16[64,1024]{1,0:T(8,128)(2,1)S(1)}, bf16[64,1024]{1,0:T(8,128)(2,1)S(1)}, u32[]{:S(2)}, u32[]{:S(2)}) collective-permute-start(bf16[64,1024]{1,0:T(8,128)(2,1)S(1)} %collective-permute-done.4.refs_0_), channel_id=1, source_target_pairs={{0,1},{1,0},{2,3},{3,2},{4,5},{5,4},{6,7},{7,6},{8,9},{9,8},{10,11... | collective-permute-start | bytes 393224 | tf_op jit(solution)/shard_map/ppermute | solution.py:257
  14.9 9.4 %collective-permute-start.7 = (bf16[64,1024]{1,0:T(8,128)(2,1)S(1)}, bf16[64,1024]{1,0:T(8,128)(2,1)S(1)}, u32[]{:S(2)}, u32[]{:S(2)}) collective-permute-start(bf16[64,1024]{1,0:T(8,128)(2,1)S(1)} %collective-permute-done.5.refs_1_), channel_id=1, source_target_pairs={{0,1},{1,0},{2,3},{3,2},{4,5},{5,4},{6,7},{7,6},{8,9},{9,8},{10,11... | collective-permute-start | bytes 393224 | tf_op jit(solution)/shard_map/ppermute | solution.py:257
  21.1 5.3 %collective-permute-start.8 = (bf16[256,1024]{1,0:T(8,128)(2,1)S(1)}, bf16[256,1024]{1,0:T(8,128)(2,1)S(1)}, u32[]{:S(2)}, u32[]{:S(2)}) collective-permute-start(bf16[256,1024]{1,0:T(8,128)(2,1)S(1)} %shard_map.116.refs_0_), channel_id=1, source_target_pairs={{0,2},{2,0},{4,6},{6,4},{8,10},{10,8},{12,14},{14,12},{16,18},{18,... | collective-permute-start | bytes 1572872 | tf_op jit(solution)/shard_map/ppermute | solution.py:260
  24.2 2.2 %collective-permute-start.9 = (bf16[256,1024]{1,0:T(8,128)(2,1)S(1)}, bf16[256,1024]{1,0:T(8,128)(2,1)S(1)}, u32[]{:S(2)}, u32[]{:S(2)}) collective-permute-start(bf16[256,1024]{1,0:T(8,128)(2,1)S(1)} %collective-permute-done.3.refs_1_), channel_id=1, source_target_pairs={{0,2},{2,0},{4,6},{6,4},{8,10},{10,8},{12,14},{14,12},{16,18},{18,... | collective-permute-start | bytes 1572872 | tf_op jit(solution)/shard_map/ppermute | solution.py:260
  24.4 9.0 %collective-permute-start.12 = (bf16[128,1024]{1,0:T(8,128)(2,1)S(1)}, bf16[128,1024]{1,0:T(8,128)(2,1)S(1)}, u32[]{:S(2)}, u32[]{:S(2)}) collective-permute-start(bf16[128,1024]{1,0:T(8,128)(2,1)S(1)} %pad_maximum_fusion), channel_id=1, source_target_pairs={{0,1},{1,0},{2,3},{3,2},{4,5},{5,4},{6,7},{7,6},{8,9},{9,8},{10,11... | collective-permute-start | bytes 786440 | tf_op jit(solution)/shard_map/ppermute | solution.py:257
  27.9 5.7 %collective-permute-start.11 = (bf16[64,1024]{1,0:T(8,128)(2,1)S(1)}, bf16[64,1024]{1,0:T(8,128)(2,1)S(1)}, u32[]{:S(2)}, u32[]{:S(2)}) collective-permute-start(bf16[64,1024]{1,0:T(8,128)(2,1)S(1)} %get-tuple-element.70), channel_id=1, source_target_pairs={{0,4},{2,6},{4,0},{6,2},{8,12},{10,14},{12,8},{14,10},{16,20},{18,... | collective-permute-start | bytes 393224 | tf_op jit(solution)/shard_map/ppermute | solution.py:267
  30.2 16.6 %collective-permute-start.10 = (bf16[128,1024]{1,0:T(8,128)(2,1)S(1)}, bf16[128,1024]{1,0:T(8,128)(2,1)S(1)}, u32[]{:S(2)}, u32[]{:S(2)}) collective-permute-start(bf16[128,1024]{1,0:T(8,128)(2,1)S(1)} %get-tuple-element.68), channel_id=1, source_target_pairs={{0,0},{2,10},{4,4},{6,14},{8,8},{10,2},{12,12},{14,6},{16,16},{18,... | collective-permute-start | bytes 786440 | tf_op jit(solution)/shard_map/ppermute | solution.py:264
  34.0 5.5 %collective-permute-start.14 = (bf16[64,1024]{1,0:T(8,128)(2,1)S(1)}, bf16[64,1024]{1,0:T(8,128)(2,1)S(1)}, u32[]{:S(2)}, u32[]{:S(2)}) collective-permute-start(bf16[64,1024]{1,0:T(8,128)(2,1)S(1)} %get-tuple-element.73), channel_id=1, source_target_pairs={{0,4},{2,6},{4,0},{6,2},{8,12},{10,14},{12,8},{14,10},{16,20},{18,... | collective-permute-start | bytes 393224 | tf_op jit(solution)/shard_map/ppermute | solution.py:267
  35.6 12.6 %collective-permute-start.13 = (bf16[64,1024]{1,0:T(8,128)(2,1)S(1)}, bf16[64,1024]{1,0:T(8,128)(2,1)S(1)}, u32[]{:S(2)}, u32[]{:S(2)}) collective-permute-start(bf16[64,1024]{1,0:T(8,128)(2,1)S(1)} %add_convert_fusion.1), channel_id=1, source_target_pairs={{0,16},{2,26},{4,20},{6,30},{8,24},{10,18},{12,28},{14,22},{16,0},... | collective-permute-start | bytes 393224 | tf_op jit(solution)/shard_map/ppermute | solution.py:264
  39.5 10.5 %collective-permute-start.16 = (bf16[64,1024]{1,0:T(8,128)(2,1)S(1)}, bf16[64,1024]{1,0:T(8,128)(2,1)S(1)}, u32[]{:S(2)}, u32[]{:S(2)}) collective-permute-start(bf16[64,1024]{1,0:T(8,128)(2,1)S(1)} %add_convert_fusion), channel_id=1, source_target_pairs={{0,16},{2,26},{4,20},{6,30},{8,24},{10,18},{12,28},{14,22},{16,0},... | collective-permute-start | bytes 393224 | tf_op jit(solution)/shard_map/ppermute | solution.py:264
  42.0 8.1 %collective-permute-start.15 = (bf16[64,1024]{1,0:T(8,128)(2,1)S(1)}, bf16[64,1024]{1,0:T(8,128)(2,1)S(1)}, u32[]{:S(2)}, u32[]{:S(2)}) collective-permute-start(bf16[64,1024]{1,0:T(8,128)(2,1)S(1)} %get-tuple-element.76), channel_id=1, source_target_pairs={{0,4},{2,14},{4,0},{6,10},{8,12},{10,6},{12,8},{14,2},{16,20},{18,... | collective-permute-start | bytes 393224 | tf_op jit(solution)/shard_map/ppermute | solution.py:264
  43.5 7.0 %collective-permute-start.17 = (bf16[64,1024]{1,0:T(8,128)(2,1)S(1)}, bf16[64,1024]{1,0:T(8,128)(2,1)S(1)}, u32[]{:S(2)}, u32[]{:S(2)}) collective-permute-start(bf16[64,1024]{1,0:T(8,128)(2,1)S(1)} %get-tuple-element.79), channel_id=1, source_target_pairs={{0,4},{2,14},{4,0},{6,10},{8,12},{10,6},{12,8},{14,2},{16,20},{18,... | collective-permute-start | bytes 393224 | tf_op jit(solution)/shard_map/ppermute | solution.py:264
  46.8 5.3 %copy-start.2 = (f32[1024]{0:T(1024)S(1)}, f32[1024]{0:T(1024)}, u32[]{:S(2)}) copy-start(f32[1024]{0:T(1024)} %param.12) | copy-start | bytes 12292
  50.7 1.4 %collective-permute-start.18 = (bf16[2,32,1024]{2,1,0:T(8,128)(2,1)S(1)}, bf16[2,32,1024]{2,1,0:T(8,128)(2,1)S(1)}, u32[]{:S(2)}, u32[]{:S(2)}) collective-permute-start(bf16[2,32,1024]{2,1,0:T(8,128)(2,1)S(1)} %fusion.4), channel_id=1, source_target_pairs={{0,2},{2,0},{4,6},{6,4},{8,10},{10,8},{12,14},{14,12},{16,18},{18,... | collective-permute-start | bytes 393224 | tf_op jit(solution)/shard_map/ppermute | solution.py:260

commit v7 on v6

--- a/solution.py
+++ b/solution.py
@@ -307,23 +307,24 @@
     split = len(near[::2])
     last = split + len(near[1::2])
     terms_near = [over_slab(x, m) for x, m in zip(parts_near[:split], near[::2])]
-    late = parts_near[split:]
+    middle, late = parts_near[split:last], parts_near[last:]
     met, moved_distant = lax.optimization_barrier((met, moved_distant))
 
     labels = [(j, m) for j in peers for m in remote]
     plan = [[(j, m) for j in peers] for m in (*evens, *odds)]
     parts = product([x for row in moved_distant for x in row], weight, labels, plan, types[: len(remote)])
     theirs_even, theirs_odd = parts[: len(evens)], parts[len(evens) :]
+    theirs_odd, middle = lax.optimization_barrier((theirs_odd, middle))
     met_theirs = [over_next(x) for x in theirs_odd]
 
     def onward(even, arrived):
         return [over_slab((x + y.astype(F32)).astype(BF16), m) for x, y, m in zip(even, arrived, evens)]
 
-    terms_ours = onward(ours_even, met)
+    terms_ours = [over_slab(x, m) for x, m in zip(middle, near[1::2])]
+    terms_ours += onward(ours_even, met)
     met_theirs, late = lax.optimization_barrier((met_theirs, late))
     terms_theirs = onward(theirs_even, met_theirs)
-    terms_theirs += [over_slab(x, m) for x, m in zip(late[last - split :], near[1::2])]
-    terms_ours += [over_slab(x, m) for x, m in zip(late, near[1::2])]
+    terms_theirs += [over_slab(x, m) for x, m in zip(late, near[1::2])]
     new_first, new_second = moments(arrays[:3], bulk, first_rows - bulk, made)
     new_first, new_second, terms_near, terms_ours, terms_theirs = lax.optimization_barrier(
         (new_first, new_second, terms_near, terms_ours, terms_theirs)

time: 53.1 us -> 52.6 us (level)
  waiting for transfers between devices: 9.64 us -> 8.75 us
    ppermute x9, waiting for transfers between devices: 4.62 us -> 4.02 us  [over_slab(): return lax.ppermute(x, 'dp', pairs)]
  transfers between devices with their start and end apart: 19 -> 19, of which waited for: 8 -> 7; matrix products, arithmetic and copies ran while one was open for 0% -> 0% of each run, Pallas kernels for 29% -> 29%
where the time goes in v7:
time: 52.6 us; the launch traced here: 52.4 us
  starting transfers between devices  26.4 us (50%)
  Pallas kernels  15.4 us (29%)
  waiting for transfers between devices  8.75 us (17%)
  other arithmetic  0.96 us (2%)
  between operations  0.85 us (2%)
    ppermute x9, starting transfers between devices, over_slab(): return lax.ppermute(x, 'dp', pairs)  13.5 us
    ppermute x4, starting transfers between devices, over_tensor(): lax.ppermute(x, 'tensor', [(i, i ^ j) for i in range(heads)])  6.72 us
    pallas_call x2, Pallas kernels, moments(): pl.pallas_call(functools.partial(moments_kernel, start, size, chunks), in...  5.64 us
    pallas_call x2, Pallas kernels, delta(): pl.pallas_call(functools.partial(delta_kernel, chunks, qrows, qcol, heads...  5.2 us
    ppermute x9, waiting for transfers between devices, over_slab(): return lax.ppermute(x, 'dp', pairs)  4.02 us
    ppermute x2, starting transfers between devices, over_next(): return lax.ppermute(x, 'dp', [(i, i ^ PAIR) for i in range(replicas)])  3.19 us
    ppermute x4, starting transfers between devices, over_core(): return lax.ppermute(x, 'dp', [(i, i ^ 1) for i in range(replicas)])  3 us
    ppermute x4, waiting for transfers between devices, over_tensor(): lax.ppermute(x, 'tensor', [(i, i ^ j) for i in range(heads)])  2.53 us
  transfers between devices with their start and end apart: 19, of which 7 were waited for; matrix products, arithmetic and copies ran while one was open for 0% of the time, Pallas kernels for 29%

profile of v7, /device:TPU:0, one launch (start us, length us, event | category | flops | bytes accessed | tf_op | source)
XLA Modules:
  0.0 52.4 jit_solution(11404547163831431374)
XLA Ops:
  0.6 0.0 copy-start
  0.6 0.0 copy-start.1
  0.6 0.5 collective-permute-start
  1.2 2.6 %shard_map.114 = bf16[256,1024]{1,0:T(8,128)(2,1)S(1)} custom-call(s32[8,16]{1,0:T(8,128)} %refs_0_.5, f32[256,2048]{1,0:T(8,128)} %refs_0_.6, f32[256,2048]{1,0:T(8,128)} %refs_1_.7, f32[256,2048]{1,0:T(8,128)} %refs_2_.7, f32[256,2048]{1,0:T(8,128)} %refs_4_.3), custom_call_target="tpu_custom_call" | custom-call | tf_op jit(solution)/shard_map/pallas_call | solution.py:107
  3.8 0.0 collective-permute-done.theirs_ref
  3.8 2.6 %collective-permute-start.3 = (bf16[256,1024]{1,0:T(8,128)(2,1)S(1)}, bf16[256,1024]{1,0:T(8,128)(2,1)S(1)}, u32[]{:S(2)}, u32[]{:S(2)}) collective-permute-start(bf16[256,1024]{1,0:T(8,128)(2,1)S(1)} %shard_map.114), channel_id=1, source_target_pairs={{0,1},{1,0},{2,3},{3,2},{4,5},{5,4},{6,7},{7,6},{8,9},{9,8},{10,11... | collective-permute-start | bytes 1572872 | tf_op jit(solution)/shard_map/ppermute | solution.py:257
  6.4 0.0 copy-done
  6.4 0.0 copy-done.1
  6.4 0.4 shard_map.115
  6.8 0.7 %collective-permute-start.4 = (bf16[64,1024]{1,0:T(8,128)(2,1)S(1)}, bf16[64,1024]{1,0:T(8,128)(2,1)S(1)}, u32[]{:S(2)}, u32[]{:S(2)}) collective-permute-start(bf16[64,1024]{1,0:T(8,128)(2,1)S(1)} %get-tuple-element.52), channel_id=1, source_target_pairs={{0,0},{2,10},{4,4},{6,14},{8,8},{10,2},{12,12},{14,6},{16,16},{18,... | collective-permute-start | bytes 393224 | tf_op jit(solution)/shard_map/ppermute | solution.py:264
  7.5 1.6 %collective-permute-start.5 = (bf16[64,1024]{1,0:T(8,128)(2,1)S(1)}, bf16[64,1024]{1,0:T(8,128)(2,1)S(1)}, u32[]{:S(2)}, u32[]{:S(2)}) collective-permute-start(bf16[64,1024]{1,0:T(8,128)(2,1)S(1)} %get-tuple-element.53), channel_id=1, source_target_pairs={{0,4},{2,14},{4,0},{6,10},{8,12},{10,6},{12,8},{14,2},{16,20},{18,... | collective-permute-start | bytes 393224 | tf_op jit(solution)/shard_map/ppermute | solution.py:264
  9.1 2.6 %collective-permute-start.1 = (bf16[64,1024]{1,0:T(8,128)(2,1)S(1)}, bf16[64,1024]{1,0:T(8,128)(2,1)S(1)}, u32[]{:S(2)}, u32[]{:S(2)}) collective-permute-start(bf16[64,1024]{1,0:T(8,128)(2,1)S(1)} %get-tuple-element.49), channel_id=1, source_target_pairs={{0,16},{2,26},{4,20},{6,30},{8,24},{10,18},{12,28},{14,22},{16,0},... | collective-permute-start | bytes 393224 | tf_op jit(solution)/shard_map/ppermute | solution.py:264
  11.6 0.3 collective-permute-start.2
  11.9 2.6 %shard_map.116.refs_0_ = bf16[256,1024]{1,0:T(8,128)(2,1)S(1)} custom-call(s32[8,16]{1,0:T(8,128)} %refs_0_.5, f32[256,2048]{1,0:T(8,128)} %refs_0_.6, f32[256,2048]{1,0:T(8,128)} %refs_1_.7, f32[256,2048]{1,0:T(8,128)} %refs_2_.7, f32[256,2048]{1,0:T(8,128)} %refs_4_.3), custom_call_target="tpu_custom_call" | custom-call | tf_op jit(solution)/shard_map/pallas_call | solution.py:107
  14.5 0.0 collective-permute-done.4.refs_0_
  14.5 0.0 collective-permute-done.5.refs_1_
  14.6 0.3 collective-permute-start.6
  14.9 1.8 %collective-permute-start.7 = (bf16[64,1024]{1,0:T(8,128)(2,1)S(1)}, bf16[64,1024]{1,0:T(8,128)(2,1)S(1)}, u32[]{:S(2)}, u32[]{:S(2)}) collective-permute-start(bf16[64,1024]{1,0:T(8,128)(2,1)S(1)} %collective-permute-done.5.refs_1_), channel_id=1, source_target_pairs={{0,1},{1,0},{2,3},{3,2},{4,5},{5,4},{6,7},{7,6},{8,9},{9,8},{10,11... | collective-permute-start | bytes 393224 | tf_op jit(solution)/shard_map/ppermute | solution.py:257
  16.6 2.8 %shard_map.112 = (f32[256,2048]{1,0:T(8,128)}, f32[256,2048]{1,0:T(8,128)}) custom-call(f32[256,2048]{1,0:T(8,128)} %refs_0_.6, f32[256,2048]{1,0:T(8,128)} %refs_1_.7, f32[256,2048]{1,0:T(8,128)} %refs_2_.7), custom_call_target="tpu_custom_call" | custom-call | bytes 31457280 | tf_op jit(solution)/shard_map/pallas_call | solution.py:152
  19.5 1.6 %shard_map.113.stale_ref = bf16[4,256,1024]{2,1,0:T(8,128)(2,1)S(1)} custom-call(bf16[8192,1024]{1,0:T(8,128)(2,1)} %stale_far.1), custom_call_target="tpu_custom_call" | custom-call | tf_op jit(solution)/shard_map/pallas_call | solution.py:198
  21.0 0.0 collective-permute-done.1.refs_4_
  21.1 2.3 %collective-permute-start.8 = (bf16[256,1024]{1,0:T(8,128)(2,1)S(1)}, bf16[256,1024]{1,0:T(8,128)(2,1)S(1)}, u32[]{:S(2)}, u32[]{:S(2)}) collective-permute-start(bf16[256,1024]{1,0:T(8,128)(2,1)S(1)} %shard_map.116.refs_0_), channel_id=1, source_target_pairs={{0,2},{2,0},{4,6},{6,4},{8,10},{10,8},{12,14},{14,12},{16,18},{18,... | collective-permute-start | bytes 1572872 | tf_op jit(solution)/shard_map/ppermute | solution.py:260
  23.3 0.9 %collective-permute-done.2.refs_5_ = bf16[64,1024]{1,0:T(8,128)(2,1)S(1)} collective-permute-done((bf16[64,1024]{1,0:T(8,128)(2,1)S(1)}, bf16[64,1024]{1,0:T(8,128)(2,1)S(1)}, u32[]{:S(2)}, u32[]{:S(2)}) %collective-permute-start.2) | collective-permute-done | bytes 131104 | tf_op jit(solution)/shard_map/ppermute | solution.py:264
  24.2 0.0 collective-permute-done.6.refs_2_
  24.2 0.0 collective-permute-done.7.refs_3_
  24.2 0.0 collective-permute-done.3.refs_1_
  24.2 0.1 collective-permute-start.9
  24.4 2.0 %collective-permute-start.12 = (bf16[128,1024]{1,0:T(8,128)(2,1)S(1)}, bf16[128,1024]{1,0:T(8,128)(2,1)S(1)}, u32[]{:S(2)}, u32[]{:S(2)}) collective-permute-start(bf16[128,1024]{1,0:T(8,128)(2,1)S(1)} %pad_maximum_fusion), channel_id=1, source_target_pairs={{0,1},{1,0},{2,3},{3,2},{4,5},{5,4},{6,7},{7,6},{8,9},{9,8},{10,11... | collective-permute-start | bytes 786440 | tf_op jit(solution)/shard_map/ppermute | solution.py:257
  26.4 0.0 collective-permute-done.8.refs_2_
  26.4 0.0 collective-permute-done.9.refs_3_
  26.4 1.4 %shard_map.118 = (bf16[1024,1024]{1,0:T(8,128)(2,1)S(1)}, f32[64,1024]{1,0:T(8,128)S(1)}, bf16[64,1024]{1,0:T(8,128)(2,1)S(1)}) custom-call(bf16[4,256,1024]{2,1,0:T(8,128)(2,1)S(1)} %shard_map.113.stale_ref, bf16[256,1024]{1,0:T(8,128)(2,1)S(1)} %shard_map.116.refs_0_, bf16[256,1024]{1,0:T(8,128)(2,1)S(1)} %collective-permute-done.3.refs_1_, ...), custom_call_target="tpu_custom_call" | custom-call | bytes 8388608 | tf_op jit(solution)/shard_map/pallas_call | solution.py:229
  27.9 1.6 %collective-permute-start.11 = (bf16[64,1024]{1,0:T(8,128)(2,1)S(1)}, bf16[64,1024]{1,0:T(8,128)(2,1)S(1)}, u32[]{:S(2)}, u32[]{:S(2)}) collective-permute-start(bf16[64,1024]{1,0:T(8,128)(2,1)S(1)} %get-tuple-element.70), channel_id=1, source_target_pairs={{0,4},{2,6},{4,0},{6,2},{8,12},{10,14},{12,8},{14,10},{16,20},{18,... | collective-permute-start | bytes 393224 | tf_op jit(solution)/shard_map/ppermute | solution.py:267
  29.5 0.7 %shard_map.119 = (bf16[128,1024]{1,0:T(8,128)(2,1)S(1)}, bf16[64,1024]{1,0:T(8,128)(2,1)S(1)}, bf16[64,1024]{1,0:T(8,128)(2,1)S(1)}) custom-call(bf16[64,1024]{1,0:T(8,128)(2,1)S(1)} %collective-permute-done.4.refs_0_, bf16[64,1024]{1,0:T(8,128)(2,1)S(1)} %collective-permute-done.5.refs_1_, bf16[64,1024]{1,0:T(8,128)(2,1)S(1)} %collective-permute-done.6.refs_2_, ...), custom_call_target="tpu_custom_call" | custom-call | tf_op jit(solution)/shard_map/pallas_call | solution.py:239
  30.2 0.7 %collective-permute-start.10 = (bf16[128,1024]{1,0:T(8,128)(2,1)S(1)}, bf16[128,1024]{1,0:T(8,128)(2,1)S(1)}, u32[]{:S(2)}, u32[]{:S(2)}) collective-permute-start(bf16[128,1024]{1,0:T(8,128)(2,1)S(1)} %get-tuple-element.69), channel_id=1, source_target_pairs={{0,0},{2,10},{4,4},{6,14},{8,8},{10,2},{12,12},{14,6},{16,16},{18,... | collective-permute-start | bytes 786440 | tf_op jit(solution)/shard_map/ppermute | solution.py:264
  30.9 2.5 %collective-permute-done.12.refs_0_ = bf16[128,1024]{1,0:T(8,128)(2,1)S(1)} collective-permute-done((bf16[128,1024]{1,0:T(8,128)(2,1)S(1)}, bf16[128,1024]{1,0:T(8,128)(2,1)S(1)}, u32[]{:S(2)}, u32[]{:S(2)}) %collective-permute-start.12) | collective-permute-done | bytes 262176 | tf_op jit(solution)/shard_map/ppermute | solution.py:257
  33.4 0.2 collective-permute-done.11
  33.6 0.4 shard_map.120
  34.0 1.6 %collective-permute-start.15 = (bf16[64,1024]{1,0:T(8,128)(2,1)S(1)}, bf16[64,1024]{1,0:T(8,128)(2,1)S(1)}, u32[]{:S(2)}, u32[]{:S(2)}) collective-permute-start(bf16[64,1024]{1,0:T(8,128)(2,1)S(1)} %get-tuple-element.78), channel_id=1, source_target_pairs={{0,4},{2,6},{4,0},{6,2},{8,12},{10,14},{12,8},{14,10},{16,20},{18,... | collective-permute-start | bytes 393224 | tf_op jit(solution)/shard_map/ppermute | solution.py:267
  35.6 2.9 %collective-permute-start.14 = (bf16[64,1024]{1,0:T(8,128)(2,1)S(1)}, bf16[64,1024]{1,0:T(8,128)(2,1)S(1)}, u32[]{:S(2)}, u32[]{:S(2)}) collective-permute-start(bf16[64,1024]{1,0:T(8,128)(2,1)S(1)} %add_convert_fusion.1), channel_id=1, source_target_pairs={{0,16},{2,26},{4,20},{6,30},{8,24},{10,18},{12,28},{14,22},{16,0},... | collective-permute-start | bytes 393224 | tf_op jit(solution)/shard_map/ppermute | solution.py:264
  38.5 0.3 collective-permute-start.13
  38.8 0.7 %collective-permute-done.15 = bf16[64,1024]{1,0:T(8,128)(2,1)S(1)} collective-permute-done((bf16[64,1024]{1,0:T(8,128)(2,1)S(1)}, bf16[64,1024]{1,0:T(8,128)(2,1)S(1)}, u32[]{:S(2)}, u32[]{:S(2)}) %collective-permute-start.15) | collective-permute-done | bytes 131104 | tf_op jit(solution)/shard_map/ppermute | solution.py:267
  39.5 2.4 %collective-permute-start.16 = (bf16[64,1024]{1,0:T(8,128)(2,1)S(1)}, bf16[64,1024]{1,0:T(8,128)(2,1)S(1)}, u32[]{:S(2)}, u32[]{:S(2)}) collective-permute-start(bf16[64,1024]{1,0:T(8,128)(2,1)S(1)} %add_convert_fusion), channel_id=1, source_target_pairs={{0,16},{2,26},{4,20},{6,30},{8,24},{10,18},{12,28},{14,22},{16,0},... | collective-permute-start | bytes 393224 | tf_op jit(solution)/shard_map/ppermute | solution.py:264
  42.0 2.1 %collective-permute-start.17 = (bf16[64,1024]{1,0:T(8,128)(2,1)S(1)}, bf16[64,1024]{1,0:T(8,128)(2,1)S(1)}, u32[]{:S(2)}, u32[]{:S(2)}) collective-permute-start(bf16[64,1024]{1,0:T(8,128)(2,1)S(1)} %get-tuple-element.81), channel_id=1, source_target_pairs={{0,4},{2,14},{4,0},{6,10},{8,12},{10,6},{12,8},{14,2},{16,20},{18,... | collective-permute-start | bytes 393224 | tf_op jit(solution)/shard_map/ppermute | solution.py:264
  44.1 2.8 %shard_map.117 = (f32[256,2048]{1,0:T(8,128)}, f32[256,2048]{1,0:T(8,128)}) custom-call(f32[256,2048]{1,0:T(8,128)} %refs_0_.6, f32[256,2048]{1,0:T(8,128)} %refs_1_.7, f32[256,2048]{1,0:T(8,128)} %refs_2_.7, f32[256,2048]{1,0:T(8,128)} %get-tuple-element.57.refs_3_, f32[256,2048]{1,0:T(8,128)} %get-tuple-element.58.refs_4_), custom_call_target="tpu_custom_call", output_to_operand_aliasing={{0}: (3, {}), {1}: (4, {})} | custom-call | bytes 31457280 | tf_op jit(solution)/shard_map/pallas_call | solution.py:152
  46.9 0.0 copy-start.2
  46.9 0.0 collective-permute-done.10
  46.9 1.3 %collective-permute-done.14 = bf16[64,1024]{1,0:T(8,128)(2,1)S(1)} collective-permute-done((bf16[64,1024]{1,0:T(8,128)(2,1)S(1)}, bf16[64,1024]{1,0:T(8,128)(2,1)S(1)}, u32[]{:S(2)}, u32[]{:S(2)}) %collective-permute-start.14) | collective-permute-done | bytes 131104 | tf_op jit(solution)/shard_map/ppermute | solution.py:264
  48.2 0.0 collective-permute-done.13
  48.2 1.8 %collective-permute-done.16 = bf16[64,1024]{1,0:T(8,128)(2,1)S(1)} collective-permute-done((bf16[64,1024]{1,0:T(8,128)(2,1)S(1)}, bf16[64,1024]{1,0:T(8,128)(2,1)S(1)}, u32[]{:S(2)}, u32[]{:S(2)}) %collective-permute-start.16) | collective-permute-done | bytes 131104 | tf_op jit(solution)/shard_map/ppermute | solution.py:264
  50.1 0.0 collective-permute-done.17
  50.1 0.1 convert_add_fusion
  50.1 0.1 maximum_add_fusion
  50.2 0.1 collective-permute-start.18
  50.3 1.3 %collective-permute-done.18 = bf16[2,32,1024]{2,1,0:T(8,128)(2,1)S(1)} collective-permute-done((bf16[2,32,1024]{2,1,0:T(8,128)(2,1)S(1)}, bf16[2,32,1024]{2,1,0:T(8,128)(2,1)S(1)}, u32[]{:S(2)}, u32[]{:S(2)}) %collective-permute-start.18) | collective-permute-done | bytes 131104 | tf_op jit(solution)/shard_map/ppermute | solution.py:260
  51.6 0.0 copy-done.2
  51.7 0.7 %reverse_select_fusion = bf16[2,32,1024]{2,1,0:T(8,128)(2,1)} fusion(bf16[2,32,1024]{2,1,0:T(8,128)(2,1)S(1)} %fusion.3, pred[]{:T(512)S(6)} %eq.9), kind=kLoop, calls=%fused_computation.12 | loop fusion | flops 65536 | bytes 262145 | tf_op jit(solution)/shard_map/jit(_where)/select_n | solution.py:341
  (5 shorter events, 0.1 us)
Async XLA Ops:
  0.6 5.8 %copy-start = (bf16[32,8192]{1,0:T(8,128)(2,1)S(1)}, bf16[32,8192]{1,0:T(8,128)(2,1)}, u32[]{:S(2)}) copy-start(bf16[32,8192]{1,0:T(8,128)(2,1)} %ours_ref.1) | copy-start | bytes 1572868
  0.6 5.8 %copy-start.1 = (f32[8192]{0:T(1024)S(1)}, f32[8192]{0:T(1024)}, u32[]{:S(2)}) copy-start(f32[8192]{0:T(1024)} %param.10) | copy-start | bytes 98308
  0.6 3.1 %collective-permute-start = (bf16[32,8192]{1,0:T(8,128)(2,1)}, bf16[32,8192]{1,0:T(8,128)(2,1)S(1)}, u32[]{:S(2)}, u32[]{:S(2)}) collective-permute-start(bf16[32,8192]{1,0:T(8,128)(2,1)} %ours_ref.1), channel_id=1, source_target_pairs={{0,2},{2,0},{4,6},{6,4},{8,10},{10,8},{12,14},{14,12},{16,18},{18,... | collective-permute-start | bytes 1572872 | tf_op jit(solution)/shard_map/ppermute | solution.py:260
  3.8 20.5 %collective-permute-start.3 = (bf16[256,1024]{1,0:T(8,128)(2,1)S(1)}, bf16[256,1024]{1,0:T(8,128)(2,1)S(1)}, u32[]{:S(2)}, u32[]{:S(2)}) collective-permute-start(bf16[256,1024]{1,0:T(8,128)(2,1)S(1)} %shard_map.114), channel_id=1, source_target_pairs={{0,1},{1,0},{2,3},{3,2},{4,5},{5,4},{6,7},{7,6},{8,9},{9,8},{10,11... | collective-permute-start | bytes 1572872 | tf_op jit(solution)/shard_map/ppermute | solution.py:257
  6.8 7.7 %collective-permute-start.4 = (bf16[64,1024]{1,0:T(8,128)(2,1)S(1)}, bf16[64,1024]{1,0:T(8,128)(2,1)S(1)}, u32[]{:S(2)}, u32[]{:S(2)}) collective-permute-start(bf16[64,1024]{1,0:T(8,128)(2,1)S(1)} %get-tuple-element.52), channel_id=1, source_target_pairs={{0,0},{2,10},{4,4},{6,14},{8,8},{10,2},{12,12},{14,6},{16,16},{18,... | collective-permute-start | bytes 393224 | tf_op jit(solution)/shard_map/ppermute | solution.py:264
  7.5 7.1 %collective-permute-start.5 = (bf16[64,1024]{1,0:T(8,128)(2,1)S(1)}, bf16[64,1024]{1,0:T(8,128)(2,1)S(1)}, u32[]{:S(2)}, u32[]{:S(2)}) collective-permute-start(bf16[64,1024]{1,0:T(8,128)(2,1)S(1)} %get-tuple-element.53), channel_id=1, source_target_pairs={{0,4},{2,14},{4,0},{6,10},{8,12},{10,6},{12,8},{14,2},{16,20},{18,... | collective-permute-start | bytes 393224 | tf_op jit(solution)/shard_map/ppermute | solution.py:264
  9.1 12.0 %collective-permute-start.1 = (bf16[64,1024]{1,0:T(8,128)(2,1)S(1)}, bf16[64,1024]{1,0:T(8,128)(2,1)S(1)}, u32[]{:S(2)}, u32[]{:S(2)}) collective-permute-start(bf16[64,1024]{1,0:T(8,128)(2,1)S(1)} %get-tuple-element.49), channel_id=1, source_target_pairs={{0,16},{2,26},{4,20},{6,30},{8,24},{10,18},{12,28},{14,22},{16,0},... | collective-permute-start | bytes 393224 | tf_op jit(solution)/shard_map/ppermute | solution.py:264
  11.6 12.6 %collective-permute-start.2 = (bf16[64,1024]{1,0:T(8,128)(2,1)S(1)}, bf16[64,1024]{1,0:T(8,128)(2,1)S(1)}, u32[]{:S(2)}, u32[]{:S(2)}) collective-permute-start(bf16[64,1024]{1,0:T(8,128)(2,1)S(1)} %get-tuple-element.50), channel_id=1, source_target_pairs={{0,20},{2,30},{4,16},{6,26},{8,28},{10,22},{12,24},{14,18},{16,4},... | collective-permute-start | bytes 393224 | tf_op jit(solution)/shard_map/ppermute | solution.py:264
  14.6 9.7 %collective-permute-start.6 = (bf16[64,1024]{1,0:T(8,128)(2,1)S(1)}, bf16[64,1024]{1,0:T(8,128)(2,1)S(1)}, u32[]{:S(2)}, u32[]{:S(2)}) collective-permute-start(bf16[64,1024]{1,0:T(8,128)(2,1)S(1)} %collective-permute-done.4.refs_0_), channel_id=1, source_target_pairs={{0,1},{1,0},{2,3},{3,2},{4,5},{5,4},{6,7},{7,6},{8,9},{9,8},{10,11... | collective-permute-start | bytes 393224 | tf_op jit(solution)/shard_map/ppermute | solution.py:257
  14.9 9.4 %collective-permute-start.7 = (bf16[64,1024]{1,0:T(8,128)(2,1)S(1)}, bf16[64,1024]{1,0:T(8,128)(2,1)S(1)}, u32[]{:S(2)}, u32[]{:S(2)}) collective-permute-start(bf16[64,1024]{1,0:T(8,128)(2,1)S(1)} %collective-permute-done.5.refs_1_), channel_id=1, source_target_pairs={{0,1},{1,0},{2,3},{3,2},{4,5},{5,4},{6,7},{7,6},{8,9},{9,8},{10,11... | collective-permute-start | bytes 393224 | tf_op jit(solution)/shard_map/ppermute | solution.py:257
  21.1 5.3 %collective-permute-start.8 = (bf16[256,1024]{1,0:T(8,128)(2,1)S(1)}, bf16[256,1024]{1,0:T(8,128)(2,1)S(1)}, u32[]{:S(2)}, u32[]{:S(2)}) collective-permute-start(bf16[256,1024]{1,0:T(8,128)(2,1)S(1)} %shard_map.116.refs_0_), channel_id=1, source_target_pairs={{0,2},{2,0},{4,6},{6,4},{8,10},{10,8},{12,14},{14,12},{16,18},{18,... | collective-permute-start | bytes 1572872 | tf_op jit(solution)/shard_map/ppermute | solution.py:260
  24.2 2.2 %collective-permute-start.9 = (bf16[256,1024]{1,0:T(8,128)(2,1)S(1)}, bf16[256,1024]{1,0:T(8,128)(2,1)S(1)}, u32[]{:S(2)}, u32[]{:S(2)}) collective-permute-start(bf16[256,1024]{1,0:T(8,128)(2,1)S(1)} %collective-permute-done.3.refs_1_), channel_id=1, source_target_pairs={{0,2},{2,0},{4,6},{6,4},{8,10},{10,8},{12,14},{14,12},{16,18},{18,... | collective-permute-start | bytes 1572872 | tf_op jit(solution)/shard_map/ppermute | solution.py:260
  24.4 9.0 %collective-permute-start.12 = (bf16[128,1024]{1,0:T(8,128)(2,1)S(1)}, bf16[128,1024]{1,0:T(8,128)(2,1)S(1)}, u32[]{:S(2)}, u32[]{:S(2)}) collective-permute-start(bf16[128,1024]{1,0:T(8,128)(2,1)S(1)} %pad_maximum_fusion), channel_id=1, source_target_pairs={{0,1},{1,0},{2,3},{3,2},{4,5},{5,4},{6,7},{7,6},{8,9},{9,8},{10,11... | collective-permute-start | bytes 786440 | tf_op jit(solution)/shard_map/ppermute | solution.py:257
  27.9 5.7 %collective-permute-start.11 = (bf16[64,1024]{1,0:T(8,128)(2,1)S(1)}, bf16[64,1024]{1,0:T(8,128)(2,1)S(1)}, u32[]{:S(2)}, u32[]{:S(2)}) collective-permute-start(bf16[64,1024]{1,0:T(8,128)(2,1)S(1)} %get-tuple-element.70), channel_id=1, source_target_pairs={{0,4},{2,6},{4,0},{6,2},{8,12},{10,14},{12,8},{14,10},{16,20},{18,... | collective-permute-start | bytes 393224 | tf_op jit(solution)/shard_map/ppermute | solution.py:267
  30.2 16.8 %collective-permute-start.10 = (bf16[128,1024]{1,0:T(8,128)(2,1)S(1)}, bf16[128,1024]{1,0:T(8,128)(2,1)S(1)}, u32[]{:S(2)}, u32[]{:S(2)}) collective-permute-start(bf16[128,1024]{1,0:T(8,128)(2,1)S(1)} %get-tuple-element.69), channel_id=1, source_target_pairs={{0,0},{2,10},{4,4},{6,14},{8,8},{10,2},{12,12},{14,6},{16,16},{18,... | collective-permute-start | bytes 786440 | tf_op jit(solution)/shard_map/ppermute | solution.py:264
  34.0 5.5 %collective-permute-start.15 = (bf16[64,1024]{1,0:T(8,128)(2,1)S(1)}, bf16[64,1024]{1,0:T(8,128)(2,1)S(1)}, u32[]{:S(2)}, u32[]{:S(2)}) collective-permute-start(bf16[64,1024]{1,0:T(8,128)(2,1)S(1)} %get-tuple-element.78), channel_id=1, source_target_pairs={{0,4},{2,6},{4,0},{6,2},{8,12},{10,14},{12,8},{14,10},{16,20},{18,... | collective-permute-start | bytes 393224 | tf_op jit(solution)/shard_map/ppermute | solution.py:267
  35.6 12.6 %collective-permute-start.14 = (bf16[64,1024]{1,0:T(8,128)(2,1)S(1)}, bf16[64,1024]{1,0:T(8,128)(2,1)S(1)}, u32[]{:S(2)}, u32[]{:S(2)}) collective-permute-start(bf16[64,1024]{1,0:T(8,128)(2,1)S(1)} %add_convert_fusion.1), channel_id=1, source_target_pairs={{0,16},{2,26},{4,20},{6,30},{8,24},{10,18},{12,28},{14,22},{16,0},... | collective-permute-start | bytes 393224 | tf_op jit(solution)/shard_map/ppermute | solution.py:264
  38.5 9.7 %collective-permute-start.13 = (bf16[64,1024]{1,0:T(8,128)(2,1)S(1)}, bf16[64,1024]{1,0:T(8,128)(2,1)S(1)}, u32[]{:S(2)}, u32[]{:S(2)}) collective-permute-start(bf16[64,1024]{1,0:T(8,128)(2,1)S(1)} %get-tuple-element.74), channel_id=1, source_target_pairs={{0,4},{2,14},{4,0},{6,10},{8,12},{10,6},{12,8},{14,2},{16,20},{18,... | collective-permute-start | bytes 393224 | tf_op jit(solution)/shard_map/ppermute | solution.py:264
  39.5 10.5 %collective-permute-start.16 = (bf16[64,1024]{1,0:T(8,128)(2,1)S(1)}, bf16[64,1024]{1,0:T(8,128)(2,1)S(1)}, u32[]{:S(2)}, u32[]{:S(2)}) collective-permute-start(bf16[64,1024]{1,0:T(8,128)(2,1)S(1)} %add_convert_fusion), channel_id=1, source_target_pairs={{0,16},{2,26},{4,20},{6,30},{8,24},{10,18},{12,28},{14,22},{16,0},... | collective-permute-start | bytes 393224 | tf_op jit(solution)/shard_map/ppermute | solution.py:264
  42.0 8.1 %collective-permute-start.17 = (bf16[64,1024]{1,0:T(8,128)(2,1)S(1)}, bf16[64,1024]{1,0:T(8,128)(2,1)S(1)}, u32[]{:S(2)}, u32[]{:S(2)}) collective-permute-start(bf16[64,1024]{1,0:T(8,128)(2,1)S(1)} %get-tuple-element.81), channel_id=1, source_target_pairs={{0,4},{2,14},{4,0},{6,10},{8,12},{10,6},{12,8},{14,2},{16,20},{18,... | collective-permute-start | bytes 393224 | tf_op jit(solution)/shard_map/ppermute | solution.py:264
  46.9 4.7 %copy-start.2 = (f32[1024]{0:T(1024)S(1)}, f32[1024]{0:T(1024)}, u32[]{:S(2)}) copy-start(f32[1024]{0:T(1024)} %param.12) | copy-start | bytes 12292
  50.2 1.4 %collective-permute-start.18 = (bf16[2,32,1024]{2,1,0:T(8,128)(2,1)S(1)}, bf16[2,32,1024]{2,1,0:T(8,128)(2,1)S(1)}, u32[]{:S(2)}, u32[]{:S(2)}) collective-permute-start(bf16[2,32,1024]{2,1,0:T(8,128)(2,1)S(1)} %fusion.4), channel_id=1, source_target_pairs={{0,2},{2,0},{4,6},{6,4},{8,10},{10,8},{12,14},{14,12},{16,18},{18,... | collective-permute-start | bytes 393224 | tf_op jit(solution)/shard_map/ppermute | solution.py:260

commit v8 on v7

--- a/solution.py
+++ b/solution.py
@@ -90,16 +90,13 @@
             for g in range(groups):
                 lanes = pl.ds(g * qcol, qcol)
                 new_first, new_second = step(b0[j, here, lanes], b1[j, here, lanes], b2[j, here, lanes])
-                bottom = new_second * lax.rsqrt(new_second) + 1e-08
-                inverse = pl.reciprocal(bottom, approx=True)
-                inverse = inverse * (2.0 - bottom * inverse)
-                corrected = 0.02 * new_first * inverse + b3[j, here, lanes]
+                corrected = 0.02 * new_first / (jnp.sqrt(new_second) + 1e-08) + b3[j, here, lanes]
                 expo = jnp.full((1, qcol), expo_ref[row, (mine ^ (start + j)) * groups + g], jnp.int32).astype(F32)
                 most = CLIP * jnp.exp2(-expo)
                 delta_outs[j][here, lanes] = jnp.clip(corrected, -most, most).astype(BF16)
 
 
-def delta(arrays, exponent, heads, start, count, chunks=2):
+def delta(arrays, exponent, heads, start, count, chunks=4):
     rows, full = arrays[0].shape
     qrows, qcol = rows // exponent.shape[0], full // exponent.shape[1]
     cols = full // heads
@@ -284,7 +281,7 @@
     ours, close = lax.optimization_barrier((ours, close))
     moved_close = over_heads(close)
     first_rows = first.shape[0]
-    bulk = first_rows // 2
+    bulk = first_rows * 3 // 4
     made = moments(arrays[:3], 0, bulk)
     held = fetch(stale, heads, slabs)
     made, held, distant, arrived, moved_close = lax.optimization_barrier((made, held, distant, arrived, moved_close))

time: 52.6 us -> 52.5 us (level)
  transfers between devices with their start and end apart: 19 -> 19, of which waited for: 7 -> 7; matrix products, arithmetic and copies ran while one was open for 0% -> 0% of each run, Pallas kernels for 29% -> 30%
where the time goes in v8:
time: 52.5 us; the launch traced here: 52.3 us
  starting transfers between devices  26.4 us (50%)
  Pallas kernels  15.5 us (30%)
  waiting for transfers between devices  8.58 us (16%)
  other arithmetic  0.96 us (2%)
  between operations  0.85 us (2%)
    ppermute x9, starting transfers between devices, over_slab(): return lax.ppermute(x, 'dp', pairs)  13.6 us
    ppermute x4, starting transfers between devices, over_tensor(): lax.ppermute(x, 'tensor', [(i, i ^ j) for i in range(heads)])  6.72 us
    pallas_call x2, Pallas kernels, moments(): pl.pallas_call(functools.partial(moments_kernel, start, size, chunks), in...  5.96 us
    pallas_call x2, Pallas kernels, delta(): pl.pallas_call(functools.partial(delta_kernel, chunks, qrows, qcol, heads...  4.98 us
    ppermute x9, waiting for transfers between devices, over_slab(): return lax.ppermute(x, 'dp', pairs)  3.83 us
    ppermute x2, starting transfers between devices, over_next(): return lax.ppermute(x, 'dp', [(i, i ^ PAIR) for i in range(replicas)])  3.12 us
    ppermute x4, starting transfers between devices, over_core(): return lax.ppermute(x, 'dp', [(i, i ^ 1) for i in range(replicas)])  3 us
    ppermute x4, waiting for transfers between devices, over_tensor(): lax.ppermute(x, 'tensor', [(i, i ^ j) for i in range(heads)])  2.52 us
  transfers between devices with their start and end apart: 19, of which 7 were waited for; matrix products, arithmetic and copies ran while one was open for 0% of the time, Pallas kernels for 30%

profile of v8, /device:TPU:0, one launch (start us, length us, event | category | flops | bytes accessed | tf_op | source)
XLA Modules:
  0.0 52.3 jit_solution(15496948262946857138)
XLA Ops:
  0.6 0.0 copy-start
  0.6 0.0 copy-start.1
  0.6 0.5 collective-permute-start
  1.2 2.5 %shard_map.114 = bf16[256,1024]{1,0:T(8,128)(2,1)S(1)} custom-call(s32[8,16]{1,0:T(8,128)} %refs_0_.5, f32[256,2048]{1,0:T(8,128)} %refs_0_.6, f32[256,2048]{1,0:T(8,128)} %refs_1_.7, f32[256,2048]{1,0:T(8,128)} %refs_2_.7, f32[256,2048]{1,0:T(8,128)} %refs_4_.3), custom_call_target="tpu_custom_call" | custom-call | tf_op jit(solution)/shard_map/pallas_call | solution.py:104
  3.7 0.0 collective-permute-done.theirs_ref
  3.7 2.6 %collective-permute-start.3 = (bf16[256,1024]{1,0:T(8,128)(2,1)S(1)}, bf16[256,1024]{1,0:T(8,128)(2,1)S(1)}, u32[]{:S(2)}, u32[]{:S(2)}) collective-permute-start(bf16[256,1024]{1,0:T(8,128)(2,1)S(1)} %shard_map.114), channel_id=1, source_target_pairs={{0,1},{1,0},{2,3},{3,2},{4,5},{5,4},{6,7},{7,6},{8,9},{9,8},{10,11... | collective-permute-start | bytes 1572872 | tf_op jit(solution)/shard_map/ppermute | solution.py:254
  6.3 0.0 copy-done
  6.3 0.0 copy-done.1
  6.3 0.4 shard_map.115
  6.7 0.7 %collective-permute-start.4 = (bf16[64,1024]{1,0:T(8,128)(2,1)S(1)}, bf16[64,1024]{1,0:T(8,128)(2,1)S(1)}, u32[]{:S(2)}, u32[]{:S(2)}) collective-permute-start(bf16[64,1024]{1,0:T(8,128)(2,1)S(1)} %get-tuple-element.52), channel_id=1, source_target_pairs={{0,0},{2,10},{4,4},{6,14},{8,8},{10,2},{12,12},{14,6},{16,16},{18,... | collective-permute-start | bytes 393224 | tf_op jit(solution)/shard_map/ppermute | solution.py:261
  7.4 1.6 %collective-permute-start.5 = (bf16[64,1024]{1,0:T(8,128)(2,1)S(1)}, bf16[64,1024]{1,0:T(8,128)(2,1)S(1)}, u32[]{:S(2)}, u32[]{:S(2)}) collective-permute-start(bf16[64,1024]{1,0:T(8,128)(2,1)S(1)} %get-tuple-element.53), channel_id=1, source_target_pairs={{0,4},{2,14},{4,0},{6,10},{8,12},{10,6},{12,8},{14,2},{16,20},{18,... | collective-permute-start | bytes 393224 | tf_op jit(solution)/shard_map/ppermute | solution.py:261
  8.9 2.6 %collective-permute-start.1 = (bf16[64,1024]{1,0:T(8,128)(2,1)S(1)}, bf16[64,1024]{1,0:T(8,128)(2,1)S(1)}, u32[]{:S(2)}, u32[]{:S(2)}) collective-permute-start(bf16[64,1024]{1,0:T(8,128)(2,1)S(1)} %get-tuple-element.49), channel_id=1, source_target_pairs={{0,16},{2,26},{4,20},{6,30},{8,24},{10,18},{12,28},{14,22},{16,0},... | collective-permute-start | bytes 393224 | tf_op jit(solution)/shard_map/ppermute | solution.py:261
  11.5 0.3 collective-permute-start.2
  11.8 2.5 %shard_map.116.refs_0_ = bf16[256,1024]{1,0:T(8,128)(2,1)S(1)} custom-call(s32[8,16]{1,0:T(8,128)} %refs_0_.5, f32[256,2048]{1,0:T(8,128)} %refs_0_.6, f32[256,2048]{1,0:T(8,128)} %refs_1_.7, f32[256,2048]{1,0:T(8,128)} %refs_2_.7, f32[256,2048]{1,0:T(8,128)} %refs_4_.3), custom_call_target="tpu_custom_call" | custom-call | tf_op jit(solution)/shard_map/pallas_call | solution.py:104
  14.3 0.0 collective-permute-done.4.refs_0_
  14.3 0.0 collective-permute-done.5.refs_1_
  14.3 0.3 collective-permute-start.6
  14.7 1.8 %collective-permute-start.7 = (bf16[64,1024]{1,0:T(8,128)(2,1)S(1)}, bf16[64,1024]{1,0:T(8,128)(2,1)S(1)}, u32[]{:S(2)}, u32[]{:S(2)}) collective-permute-start(bf16[64,1024]{1,0:T(8,128)(2,1)S(1)} %collective-permute-done.5.refs_1_), channel_id=1, source_target_pairs={{0,1},{1,0},{2,3},{3,2},{4,5},{5,4},{6,7},{7,6},{8,9},{9,8},{10,11... | collective-permute-start | bytes 393224 | tf_op jit(solution)/shard_map/ppermute | solution.py:254
  16.4 3.6 %shard_map.112 = (f32[256,2048]{1,0:T(8,128)}, f32[256,2048]{1,0:T(8,128)}) custom-call(f32[256,2048]{1,0:T(8,128)} %refs_0_.6, f32[256,2048]{1,0:T(8,128)} %refs_1_.7, f32[256,2048]{1,0:T(8,128)} %refs_2_.7), custom_call_target="tpu_custom_call" | custom-call | bytes 31457280 | tf_op jit(solution)/shard_map/pallas_call | solution.py:149
  20.1 1.6 %shard_map.113.stale_ref = bf16[4,256,1024]{2,1,0:T(8,128)(2,1)S(1)} custom-call(bf16[8192,1024]{1,0:T(8,128)(2,1)} %stale_far.1), custom_call_target="tpu_custom_call" | custom-call | tf_op jit(solution)/shard_map/pallas_call | solution.py:195
  21.6 0.0 collective-permute-done.1.refs_4_
  21.6 2.3 %collective-permute-start.8 = (bf16[256,1024]{1,0:T(8,128)(2,1)S(1)}, bf16[256,1024]{1,0:T(8,128)(2,1)S(1)}, u32[]{:S(2)}, u32[]{:S(2)}) collective-permute-start(bf16[256,1024]{1,0:T(8,128)(2,1)S(1)} %shard_map.116.refs_0_), channel_id=1, source_target_pairs={{0,2},{2,0},{4,6},{6,4},{8,10},{10,8},{12,14},{14,12},{16,18},{18,... | collective-permute-start | bytes 1572872 | tf_op jit(solution)/shard_map/ppermute | solution.py:257
  23.9 0.2 collective-permute-done.2.refs_5_
  24.1 0.0 collective-permute-done.6.refs_2_
  24.1 0.0 collective-permute-done.7.refs_3_
  24.1 0.0 collective-permute-done.3.refs_1_
  24.1 0.1 collective-permute-start.9
  24.3 2.0 %collective-permute-start.12 = (bf16[128,1024]{1,0:T(8,128)(2,1)S(1)}, bf16[128,1024]{1,0:T(8,128)(2,1)S(1)}, u32[]{:S(2)}, u32[]{:S(2)}) collective-permute-start(bf16[128,1024]{1,0:T(8,128)(2,1)S(1)} %pad_maximum_fusion), channel_id=1, source_target_pairs={{0,1},{1,0},{2,3},{3,2},{4,5},{5,4},{6,7},{7,6},{8,9},{9,8},{10,11... | collective-permute-start | bytes 786440 | tf_op jit(solution)/shard_map/ppermute | solution.py:254
  26.3 0.0 collective-permute-done.8.refs_2_
  26.3 0.0 collective-permute-done.9.refs_3_
  26.3 1.5 %shard_map.118 = (bf16[1024,1024]{1,0:T(8,128)(2,1)S(1)}, f32[64,1024]{1,0:T(8,128)S(1)}, bf16[64,1024]{1,0:T(8,128)(2,1)S(1)}) custom-call(bf16[4,256,1024]{2,1,0:T(8,128)(2,1)S(1)} %shard_map.113.stale_ref, bf16[256,1024]{1,0:T(8,128)(2,1)S(1)} %shard_map.116.refs_0_, bf16[256,1024]{1,0:T(8,128)(2,1)S(1)} %collective-permute-done.3.refs_1_, ...), custom_call_target="tpu_custom_call" | custom-call | bytes 8388608 | tf_op jit(solution)/shard_map/pallas_call | solution.py:226
  27.8 1.6 %collective-permute-start.11 = (bf16[64,1024]{1,0:T(8,128)(2,1)S(1)}, bf16[64,1024]{1,0:T(8,128)(2,1)S(1)}, u32[]{:S(2)}, u32[]{:S(2)}) collective-permute-start(bf16[64,1024]{1,0:T(8,128)(2,1)S(1)} %get-tuple-element.70), channel_id=1, source_target_pairs={{0,4},{2,6},{4,0},{6,2},{8,12},{10,14},{12,8},{14,10},{16,20},{18,... | collective-permute-start | bytes 393224 | tf_op jit(solution)/shard_map/ppermute | solution.py:264
  29.4 0.7 %shard_map.119 = (bf16[128,1024]{1,0:T(8,128)(2,1)S(1)}, bf16[64,1024]{1,0:T(8,128)(2,1)S(1)}, bf16[64,1024]{1,0:T(8,128)(2,1)S(1)}) custom-call(bf16[64,1024]{1,0:T(8,128)(2,1)S(1)} %collective-permute-done.4.refs_0_, bf16[64,1024]{1,0:T(8,128)(2,1)S(1)} %collective-permute-done.5.refs_1_, bf16[64,1024]{1,0:T(8,128)(2,1)S(1)} %collective-permute-done.6.refs_2_, ...), custom_call_target="tpu_custom_call" | custom-call | tf_op jit(solution)/shard_map/pallas_call | solution.py:236
  30.1 0.7 %collective-permute-start.10 = (bf16[128,1024]{1,0:T(8,128)(2,1)S(1)}, bf16[128,1024]{1,0:T(8,128)(2,1)S(1)}, u32[]{:S(2)}, u32[]{:S(2)}) collective-permute-start(bf16[128,1024]{1,0:T(8,128)(2,1)S(1)} %get-tuple-element.69), channel_id=1, source_target_pairs={{0,0},{2,10},{4,4},{6,14},{8,8},{10,2},{12,12},{14,6},{16,16},{18,... | collective-permute-start | bytes 786440 | tf_op jit(solution)/shard_map/ppermute | solution.py:261
  30.8 2.5 %collective-permute-done.12.refs_0_ = bf16[128,1024]{1,0:T(8,128)(2,1)S(1)} collective-permute-done((bf16[128,1024]{1,0:T(8,128)(2,1)S(1)}, bf16[128,1024]{1,0:T(8,128)(2,1)S(1)}, u32[]{:S(2)}, u32[]{:S(2)}) %collective-permute-start.12) | collective-permute-done | bytes 262176 | tf_op jit(solution)/shard_map/ppermute | solution.py:254
  33.3 0.2 collective-permute-done.11
  33.5 0.4 shard_map.120
  34.0 1.5 %collective-permute-start.15 = (bf16[64,1024]{1,0:T(8,128)(2,1)S(1)}, bf16[64,1024]{1,0:T(8,128)(2,1)S(1)}, u32[]{:S(2)}, u32[]{:S(2)}) collective-permute-start(bf16[64,1024]{1,0:T(8,128)(2,1)S(1)} %get-tuple-element.78), channel_id=1, source_target_pairs={{0,4},{2,6},{4,0},{6,2},{8,12},{10,14},{12,8},{14,10},{16,20},{18,... | collective-permute-start | bytes 393224 | tf_op jit(solution)/shard_map/ppermute | solution.py:264
  35.5 2.9 %collective-permute-start.14 = (bf16[64,1024]{1,0:T(8,128)(2,1)S(1)}, bf16[64,1024]{1,0:T(8,128)(2,1)S(1)}, u32[]{:S(2)}, u32[]{:S(2)}) collective-permute-start(bf16[64,1024]{1,0:T(8,128)(2,1)S(1)} %add_convert_fusion.1), channel_id=1, source_target_pairs={{0,16},{2,26},{4,20},{6,30},{8,24},{10,18},{12,28},{14,22},{16,0},... | collective-permute-start | bytes 393224 | tf_op jit(solution)/shard_map/ppermute | solution.py:261
  38.4 0.3 collective-permute-start.13
  38.7 0.7 %collective-permute-done.15 = bf16[64,1024]{1,0:T(8,128)(2,1)S(1)} collective-permute-done((bf16[64,1024]{1,0:T(8,128)(2,1)S(1)}, bf16[64,1024]{1,0:T(8,128)(2,1)S(1)}, u32[]{:S(2)}, u32[]{:S(2)}) %collective-permute-start.15) | collective-permute-done | bytes 131104 | tf_op jit(solution)/shard_map/ppermute | solution.py:264
  39.4 2.4 %collective-permute-start.16 = (bf16[64,1024]{1,0:T(8,128)(2,1)S(1)}, bf16[64,1024]{1,0:T(8,128)(2,1)S(1)}, u32[]{:S(2)}, u32[]{:S(2)}) collective-permute-start(bf16[64,1024]{1,0:T(8,128)(2,1)S(1)} %add_convert_fusion), channel_id=1, source_target_pairs={{0,16},{2,26},{4,20},{6,30},{8,24},{10,18},{12,28},{14,22},{16,0},... | collective-permute-start | bytes 393224 | tf_op jit(solution)/shard_map/ppermute | solution.py:261
  41.9 2.1 %collective-permute-start.17 = (bf16[64,1024]{1,0:T(8,128)(2,1)S(1)}, bf16[64,1024]{1,0:T(8,128)(2,1)S(1)}, u32[]{:S(2)}, u32[]{:S(2)}) collective-permute-start(bf16[64,1024]{1,0:T(8,128)(2,1)S(1)} %get-tuple-element.81), channel_id=1, source_target_pairs={{0,4},{2,14},{4,0},{6,10},{8,12},{10,6},{12,8},{14,2},{16,20},{18,... | collective-permute-start | bytes 393224 | tf_op jit(solution)/shard_map/ppermute | solution.py:261
  44.0 2.3 %shard_map.117 = (f32[256,2048]{1,0:T(8,128)}, f32[256,2048]{1,0:T(8,128)}) custom-call(f32[256,2048]{1,0:T(8,128)} %refs_0_.6, f32[256,2048]{1,0:T(8,128)} %refs_1_.7, f32[256,2048]{1,0:T(8,128)} %refs_2_.7, f32[256,2048]{1,0:T(8,128)} %get-tuple-element.57.refs_3_, f32[256,2048]{1,0:T(8,128)} %get-tuple-element.58.refs_4_), custom_call_target="tpu_custom_call", output_to_operand_aliasing={{0}: (3, {}), {1}: (4, {})} | custom-call | bytes 31457280 | tf_op jit(solution)/shard_map/pallas_call | solution.py:149
  46.3 0.0 copy-start.2
  46.3 0.0 collective-permute-done.10
  46.4 1.8 %collective-permute-done.14 = bf16[64,1024]{1,0:T(8,128)(2,1)S(1)} collective-permute-done((bf16[64,1024]{1,0:T(8,128)(2,1)S(1)}, bf16[64,1024]{1,0:T(8,128)(2,1)S(1)}, u32[]{:S(2)}, u32[]{:S(2)}) %collective-permute-start.14) | collective-permute-done | bytes 131104 | tf_op jit(solution)/shard_map/ppermute | solution.py:261
  48.1 0.0 collective-permute-done.13
  48.1 1.8 %collective-permute-done.16 = bf16[64,1024]{1,0:T(8,128)(2,1)S(1)} collective-permute-done((bf16[64,1024]{1,0:T(8,128)(2,1)S(1)}, bf16[64,1024]{1,0:T(8,128)(2,1)S(1)}, u32[]{:S(2)}, u32[]{:S(2)}) %collective-permute-start.16) | collective-permute-done | bytes 131104 | tf_op jit(solution)/shard_map/ppermute | solution.py:261
  50.0 0.0 collective-permute-done.17
  50.0 0.1 convert_add_fusion
  50.0 0.1 maximum_add_fusion
  50.1 0.1 collective-permute-start.18
  50.2 1.3 %collective-permute-done.18 = bf16[2,32,1024]{2,1,0:T(8,128)(2,1)S(1)} collective-permute-done((bf16[2,32,1024]{2,1,0:T(8,128)(2,1)S(1)}, bf16[2,32,1024]{2,1,0:T(8,128)(2,1)S(1)}, u32[]{:S(2)}, u32[]{:S(2)}) %collective-permute-start.18) | collective-permute-done | bytes 131104 | tf_op jit(solution)/shard_map/ppermute | solution.py:257
  51.6 0.0 copy-done.2
  51.6 0.7 %reverse_select_fusion = bf16[2,32,1024]{2,1,0:T(8,128)(2,1)} fusion(bf16[2,32,1024]{2,1,0:T(8,128)(2,1)S(1)} %fusion.3, pred[]{:T(512)S(6)} %eq.9), kind=kLoop, calls=%fused_computation.12 | loop fusion | flops 65536 | bytes 262145 | tf_op jit(solution)/shard_map/jit(_where)/select_n | solution.py:338
  (5 shorter events, 0.1 us)
Async XLA Ops:
  0.6 5.7 %copy-start = (bf16[32,8192]{1,0:T(8,128)(2,1)S(1)}, bf16[32,8192]{1,0:T(8,128)(2,1)}, u32[]{:S(2)}) copy-start(bf16[32,8192]{1,0:T(8,128)(2,1)} %ours_ref.1) | copy-start | bytes 1572868
  0.6 5.7 %copy-start.1 = (f32[8192]{0:T(1024)S(1)}, f32[8192]{0:T(1024)}, u32[]{:S(2)}) copy-start(f32[8192]{0:T(1024)} %param.10) | copy-start | bytes 98308
  0.6 3.0 %collective-permute-start = (bf16[32,8192]{1,0:T(8,128)(2,1)}, bf16[32,8192]{1,0:T(8,128)(2,1)S(1)}, u32[]{:S(2)}, u32[]{:S(2)}) collective-permute-start(bf16[32,8192]{1,0:T(8,128)(2,1)} %ours_ref.1), channel_id=1, source_target_pairs={{0,2},{2,0},{4,6},{6,4},{8,10},{10,8},{12,14},{14,12},{16,18},{18,... | collective-permute-start | bytes 1572872 | tf_op jit(solution)/shard_map/ppermute | solution.py:257
  3.7 20.5 %collective-permute-start.3 = (bf16[256,1024]{1,0:T(8,128)(2,1)S(1)}, bf16[256,1024]{1,0:T(8,128)(2,1)S(1)}, u32[]{:S(2)}, u32[]{:S(2)}) collective-permute-start(bf16[256,1024]{1,0:T(8,128)(2,1)S(1)} %shard_map.114), channel_id=1, source_target_pairs={{0,1},{1,0},{2,3},{3,2},{4,5},{5,4},{6,7},{7,6},{8,9},{9,8},{10,11... | collective-permute-start | bytes 1572872 | tf_op jit(solution)/shard_map/ppermute | solution.py:254
  6.7 7.6 %collective-permute-start.4 = (bf16[64,1024]{1,0:T(8,128)(2,1)S(1)}, bf16[64,1024]{1,0:T(8,128)(2,1)S(1)}, u32[]{:S(2)}, u32[]{:S(2)}) collective-permute-start(bf16[64,1024]{1,0:T(8,128)(2,1)S(1)} %get-tuple-element.52), channel_id=1, source_target_pairs={{0,0},{2,10},{4,4},{6,14},{8,8},{10,2},{12,12},{14,6},{16,16},{18,... | collective-permute-start | bytes 393224 | tf_op jit(solution)/shard_map/ppermute | solution.py:261
  7.4 7.0 %collective-permute-start.5 = (bf16[64,1024]{1,0:T(8,128)(2,1)S(1)}, bf16[64,1024]{1,0:T(8,128)(2,1)S(1)}, u32[]{:S(2)}, u32[]{:S(2)}) collective-permute-start(bf16[64,1024]{1,0:T(8,128)(2,1)S(1)} %get-tuple-element.53), channel_id=1, source_target_pairs={{0,4},{2,14},{4,0},{6,10},{8,12},{10,6},{12,8},{14,2},{16,20},{18,... | collective-permute-start | bytes 393224 | tf_op jit(solution)/shard_map/ppermute | solution.py:261
  8.9 12.7 %collective-permute-start.1 = (bf16[64,1024]{1,0:T(8,128)(2,1)S(1)}, bf16[64,1024]{1,0:T(8,128)(2,1)S(1)}, u32[]{:S(2)}, u32[]{:S(2)}) collective-permute-start(bf16[64,1024]{1,0:T(8,128)(2,1)S(1)} %get-tuple-element.49), channel_id=1, source_target_pairs={{0,16},{2,26},{4,20},{6,30},{8,24},{10,18},{12,28},{14,22},{16,0},... | collective-permute-start | bytes 393224 | tf_op jit(solution)/shard_map/ppermute | solution.py:261
  11.5 12.6 %collective-permute-start.2 = (bf16[64,1024]{1,0:T(8,128)(2,1)S(1)}, bf16[64,1024]{1,0:T(8,128)(2,1)S(1)}, u32[]{:S(2)}, u32[]{:S(2)}) collective-permute-start(bf16[64,1024]{1,0:T(8,128)(2,1)S(1)} %get-tuple-element.50), channel_id=1, source_target_pairs={{0,20},{2,30},{4,16},{6,26},{8,28},{10,22},{12,24},{14,18},{16,4},... | collective-permute-start | bytes 393224 | tf_op jit(solution)/shard_map/ppermute | solution.py:261
  14.3 9.8 %collective-permute-start.6 = (bf16[64,1024]{1,0:T(8,128)(2,1)S(1)}, bf16[64,1024]{1,0:T(8,128)(2,1)S(1)}, u32[]{:S(2)}, u32[]{:S(2)}) collective-permute-start(bf16[64,1024]{1,0:T(8,128)(2,1)S(1)} %collective-permute-done.4.refs_0_), channel_id=1, source_target_pairs={{0,1},{1,0},{2,3},{3,2},{4,5},{5,4},{6,7},{7,6},{8,9},{9,8},{10,11... | collective-permute-start | bytes 393224 | tf_op jit(solution)/shard_map/ppermute | solution.py:254
  14.7 9.5 %collective-permute-start.7 = (bf16[64,1024]{1,0:T(8,128)(2,1)S(1)}, bf16[64,1024]{1,0:T(8,128)(2,1)S(1)}, u32[]{:S(2)}, u32[]{:S(2)}) collective-permute-start(bf16[64,1024]{1,0:T(8,128)(2,1)S(1)} %collective-permute-done.5.refs_1_), channel_id=1, source_target_pairs={{0,1},{1,0},{2,3},{3,2},{4,5},{5,4},{6,7},{7,6},{8,9},{9,8},{10,11... | collective-permute-start | bytes 393224 | tf_op jit(solution)/shard_map/ppermute | solution.py:254
  21.6 4.7 %collective-permute-start.8 = (bf16[256,1024]{1,0:T(8,128)(2,1)S(1)}, bf16[256,1024]{1,0:T(8,128)(2,1)S(1)}, u32[]{:S(2)}, u32[]{:S(2)}) collective-permute-start(bf16[256,1024]{1,0:T(8,128)(2,1)S(1)} %shard_map.116.refs_0_), channel_id=1, source_target_pairs={{0,2},{2,0},{4,6},{6,4},{8,10},{10,8},{12,14},{14,12},{16,18},{18,... | collective-permute-start | bytes 1572872 | tf_op jit(solution)/shard_map/ppermute | solution.py:257
  24.1 2.2 %collective-permute-start.9 = (bf16[256,1024]{1,0:T(8,128)(2,1)S(1)}, bf16[256,1024]{1,0:T(8,128)(2,1)S(1)}, u32[]{:S(2)}, u32[]{:S(2)}) collective-permute-start(bf16[256,1024]{1,0:T(8,128)(2,1)S(1)} %collective-permute-done.3.refs_1_), channel_id=1, source_target_pairs={{0,2},{2,0},{4,6},{6,4},{8,10},{10,8},{12,14},{14,12},{16,18},{18,... | collective-permute-start | bytes 1572872 | tf_op jit(solution)/shard_map/ppermute | solution.py:257
  24.3 9.0 %collective-permute-start.12 = (bf16[128,1024]{1,0:T(8,128)(2,1)S(1)}, bf16[128,1024]{1,0:T(8,128)(2,1)S(1)}, u32[]{:S(2)}, u32[]{:S(2)}) collective-permute-start(bf16[128,1024]{1,0:T(8,128)(2,1)S(1)} %pad_maximum_fusion), channel_id=1, source_target_pairs={{0,1},{1,0},{2,3},{3,2},{4,5},{5,4},{6,7},{7,6},{8,9},{9,8},{10,11... | collective-permute-start | bytes 786440 | tf_op jit(solution)/shard_map/ppermute | solution.py:254
  27.8 5.7 %collective-permute-start.11 = (bf16[64,1024]{1,0:T(8,128)(2,1)S(1)}, bf16[64,1024]{1,0:T(8,128)(2,1)S(1)}, u32[]{:S(2)}, u32[]{:S(2)}) collective-permute-start(bf16[64,1024]{1,0:T(8,128)(2,1)S(1)} %get-tuple-element.70), channel_id=1, source_target_pairs={{0,4},{2,6},{4,0},{6,2},{8,12},{10,14},{12,8},{14,10},{16,20},{18,... | collective-permute-start | bytes 393224 | tf_op jit(solution)/shard_map/ppermute | solution.py:264
  30.1 16.3 %collective-permute-start.10 = (bf16[128,1024]{1,0:T(8,128)(2,1)S(1)}, bf16[128,1024]{1,0:T(8,128)(2,1)S(1)}, u32[]{:S(2)}, u32[]{:S(2)}) collective-permute-start(bf16[128,1024]{1,0:T(8,128)(2,1)S(1)} %get-tuple-element.69), channel_id=1, source_target_pairs={{0,0},{2,10},{4,4},{6,14},{8,8},{10,2},{12,12},{14,6},{16,16},{18,... | collective-permute-start | bytes 786440 | tf_op jit(solution)/shard_map/ppermute | solution.py:261
  34.0 5.4 %collective-permute-start.15 = (bf16[64,1024]{1,0:T(8,128)(2,1)S(1)}, bf16[64,1024]{1,0:T(8,128)(2,1)S(1)}, u32[]{:S(2)}, u32[]{:S(2)}) collective-permute-start(bf16[64,1024]{1,0:T(8,128)(2,1)S(1)} %get-tuple-element.78), channel_id=1, source_target_pairs={{0,4},{2,6},{4,0},{6,2},{8,12},{10,14},{12,8},{14,10},{16,20},{18,... | collective-permute-start | bytes 393224 | tf_op jit(solution)/shard_map/ppermute | solution.py:264
  35.5 12.6 %collective-permute-start.14 = (bf16[64,1024]{1,0:T(8,128)(2,1)S(1)}, bf16[64,1024]{1,0:T(8,128)(2,1)S(1)}, u32[]{:S(2)}, u32[]{:S(2)}) collective-permute-start(bf16[64,1024]{1,0:T(8,128)(2,1)S(1)} %add_convert_fusion.1), channel_id=1, source_target_pairs={{0,16},{2,26},{4,20},{6,30},{8,24},{10,18},{12,28},{14,22},{16,0},... | collective-permute-start | bytes 393224 | tf_op jit(solution)/shard_map/ppermute | solution.py:261
  38.4 9.7 %collective-permute-start.13 = (bf16[64,1024]{1,0:T(8,128)(2,1)S(1)}, bf16[64,1024]{1,0:T(8,128)(2,1)S(1)}, u32[]{:S(2)}, u32[]{:S(2)}) collective-permute-start(bf16[64,1024]{1,0:T(8,128)(2,1)S(1)} %get-tuple-element.74), channel_id=1, source_target_pairs={{0,4},{2,14},{4,0},{6,10},{8,12},{10,6},{12,8},{14,2},{16,20},{18,... | collective-permute-start | bytes 393224 | tf_op jit(solution)/shard_map/ppermute | solution.py:261
  39.4 10.5 %collective-permute-start.16 = (bf16[64,1024]{1,0:T(8,128)(2,1)S(1)}, bf16[64,1024]{1,0:T(8,128)(2,1)S(1)}, u32[]{:S(2)}, u32[]{:S(2)}) collective-permute-start(bf16[64,1024]{1,0:T(8,128)(2,1)S(1)} %add_convert_fusion), channel_id=1, source_target_pairs={{0,16},{2,26},{4,20},{6,30},{8,24},{10,18},{12,28},{14,22},{16,0},... | collective-permute-start | bytes 393224 | tf_op jit(solution)/shard_map/ppermute | solution.py:261
  41.9 8.1 %collective-permute-start.17 = (bf16[64,1024]{1,0:T(8,128)(2,1)S(1)}, bf16[64,1024]{1,0:T(8,128)(2,1)S(1)}, u32[]{:S(2)}, u32[]{:S(2)}) collective-permute-start(bf16[64,1024]{1,0:T(8,128)(2,1)S(1)} %get-tuple-element.81), channel_id=1, source_target_pairs={{0,4},{2,14},{4,0},{6,10},{8,12},{10,6},{12,8},{14,2},{16,20},{18,... | collective-permute-start | bytes 393224 | tf_op jit(solution)/shard_map/ppermute | solution.py:261
  46.3 5.2 %copy-start.2 = (f32[1024]{0:T(1024)S(1)}, f32[1024]{0:T(1024)}, u32[]{:S(2)}) copy-start(f32[1024]{0:T(1024)} %param.12) | copy-start | bytes 12292
  50.1 1.4 %collective-permute-start.18 = (bf16[2,32,1024]{2,1,0:T(8,128)(2,1)S(1)}, bf16[2,32,1024]{2,1,0:T(8,128)(2,1)S(1)}, u32[]{:S(2)}, u32[]{:S(2)}) collective-permute-start(bf16[2,32,1024]{2,1,0:T(8,128)(2,1)S(1)} %fusion.4), channel_id=1, source_target_pairs={{0,2},{2,0},{4,6},{6,4},{8,10},{10,8},{12,14},{14,12},{16,18},{18,... | collective-permute-start | bytes 393224 | tf_op jit(solution)/shard_map/ppermute | solution.py:257

commit v9 on v8

--- a/solution.py
+++ b/solution.py
@@ -285,7 +285,7 @@
     made = moments(arrays[:3], 0, bulk)
     held = fetch(stale, heads, slabs)
     made, held, distant, arrived, moved_close = lax.optimization_barrier((made, held, distant, arrived, moved_close))
-    moved_distant = over_heads([jnp.concatenate(distant, axis=0)])
+    moved_distant = over_heads(distant)
     shared = [*ours, *arrived]
     shared = shared + [over_core(x) for x in shared]
     peers = range(1, heads)

time: 52.5 us -> 52.4 us (level)
    ppermute x4 -> x5, waiting for transfers between devices: 2.52 us -> 2.17 us  [over_tensor(): lax.ppermute(x, 'tensor', [(i, i ^ j) for i in range(heads)])]
    ppermute x4 -> x5, starting transfers between devices: 6.72 us -> 6.75 us  [over_tensor(): lax.ppermute(x, 'tensor', [(i, i ^ j) for i in range(heads)])]
  transfers between devices with their start and end apart: 19 -> 20, of which waited for: 7 -> 7; matrix products, arithmetic and copies ran while one was open for 0% -> 0% of each run, Pallas kernels for 30% -> 30%
where the time goes in v9:
time: 52.4 us; the launch traced here: 52.2 us
  starting transfers between devices  26.7 us (51%)
  Pallas kernels  15.5 us (30%)
  waiting for transfers between devices  8.22 us (16%)
  other arithmetic  0.93 us (2%)
  between operations  0.85 us (2%)
    ppermute x9, starting transfers between devices, over_slab(): return lax.ppermute(x, 'dp', pairs)  13.6 us
    ppermute x5, starting transfers between devices, over_tensor(): lax.ppermute(x, 'tensor', [(i, i ^ j) for i in range(heads)])  6.75 us
    pallas_call x2, Pallas kernels, moments(): pl.pallas_call(functools.partial(moments_kernel, start, size, chunks), in...  5.96 us
    pallas_call x2, Pallas kernels, delta(): pl.pallas_call(functools.partial(delta_kernel, chunks, qrows, qcol, heads...  4.98 us
    ppermute x9, waiting for transfers between devices, over_slab(): return lax.ppermute(x, 'dp', pairs)  3.73 us
    ppermute x2, starting transfers between devices, over_next(): return lax.ppermute(x, 'dp', [(i, i ^ PAIR) for i in range(replicas)])  3.36 us
    ppermute x4, starting transfers between devices, over_core(): return lax.ppermute(x, 'dp', [(i, i ^ 1) for i in range(replicas)])  3 us
    ppermute x5, waiting for transfers between devices, over_tensor(): lax.ppermute(x, 'tensor', [(i, i ^ j) for i in range(heads)])  2.17 us
  transfers between devices with their start and end apart: 20, of which 7 were waited for; matrix products, arithmetic and copies ran while one was open for 0% of the time, Pallas kernels for 30%

profile of v9, /device:TPU:0, one launch (start us, length us, event | category | flops | bytes accessed | tf_op | source)
XLA Modules:
  0.0 52.2 jit_solution(6928825128782437449)
XLA Ops:
  0.6 0.0 copy-start
  0.6 0.0 copy-start.1
  0.6 0.5 collective-permute-start
  1.2 2.5 %shard_map.114 = bf16[256,1024]{1,0:T(8,128)(2,1)S(1)} custom-call(s32[8,16]{1,0:T(8,128)} %refs_0_.5, f32[256,2048]{1,0:T(8,128)} %refs_0_.6, f32[256,2048]{1,0:T(8,128)} %refs_1_.7, f32[256,2048]{1,0:T(8,128)} %refs_2_.7, f32[256,2048]{1,0:T(8,128)} %refs_4_.3), custom_call_target="tpu_custom_call" | custom-call | tf_op jit(solution)/shard_map/pallas_call | solution.py:104
  3.7 0.0 collective-permute-done.theirs_ref
  3.7 2.6 %collective-permute-start.3 = (bf16[256,1024]{1,0:T(8,128)(2,1)S(1)}, bf16[256,1024]{1,0:T(8,128)(2,1)S(1)}, u32[]{:S(2)}, u32[]{:S(2)}) collective-permute-start(bf16[256,1024]{1,0:T(8,128)(2,1)S(1)} %shard_map.114), channel_id=1, source_target_pairs={{0,1},{1,0},{2,3},{3,2},{4,5},{5,4},{6,7},{7,6},{8,9},{9,8},{10,11... | collective-permute-start | bytes 1572872 | tf_op jit(solution)/shard_map/ppermute | solution.py:254
  6.3 0.0 copy-done
  6.3 0.0 copy-done.1
  6.3 0.4 shard_map.115
  6.7 0.7 %collective-permute-start.4 = (bf16[64,1024]{1,0:T(8,128)(2,1)S(1)}, bf16[64,1024]{1,0:T(8,128)(2,1)S(1)}, u32[]{:S(2)}, u32[]{:S(2)}) collective-permute-start(bf16[64,1024]{1,0:T(8,128)(2,1)S(1)} %get-tuple-element.53), channel_id=1, source_target_pairs={{0,0},{2,10},{4,4},{6,14},{8,8},{10,2},{12,12},{14,6},{16,16},{18,... | collective-permute-start | bytes 393224 | tf_op jit(solution)/shard_map/ppermute | solution.py:261
  7.4 1.6 %collective-permute-start.5 = (bf16[64,1024]{1,0:T(8,128)(2,1)S(1)}, bf16[64,1024]{1,0:T(8,128)(2,1)S(1)}, u32[]{:S(2)}, u32[]{:S(2)}) collective-permute-start(bf16[64,1024]{1,0:T(8,128)(2,1)S(1)} %get-tuple-element.54), channel_id=1, source_target_pairs={{0,4},{2,14},{4,0},{6,10},{8,12},{10,6},{12,8},{14,2},{16,20},{18,... | collective-permute-start | bytes 393224 | tf_op jit(solution)/shard_map/ppermute | solution.py:261
  8.9 2.6 %collective-permute-start.1 = (bf16[64,1024]{1,0:T(8,128)(2,1)S(1)}, bf16[64,1024]{1,0:T(8,128)(2,1)S(1)}, u32[]{:S(2)}, u32[]{:S(2)}) collective-permute-start(bf16[64,1024]{1,0:T(8,128)(2,1)S(1)} %get-tuple-element.50), channel_id=1, source_target_pairs={{0,16},{2,26},{4,20},{6,30},{8,24},{10,18},{12,28},{14,22},{16,0},... | collective-permute-start | bytes 393224 | tf_op jit(solution)/shard_map/ppermute | solution.py:261
  11.5 0.3 collective-permute-start.2
  11.8 2.5 %shard_map.116.refs_0_ = bf16[256,1024]{1,0:T(8,128)(2,1)S(1)} custom-call(s32[8,16]{1,0:T(8,128)} %refs_0_.5, f32[256,2048]{1,0:T(8,128)} %refs_0_.6, f32[256,2048]{1,0:T(8,128)} %refs_1_.7, f32[256,2048]{1,0:T(8,128)} %refs_2_.7, f32[256,2048]{1,0:T(8,128)} %refs_4_.3), custom_call_target="tpu_custom_call" | custom-call | tf_op jit(solution)/shard_map/pallas_call | solution.py:104
  14.3 0.0 collective-permute-done.4.refs_0_
  14.3 0.0 collective-permute-done.5.refs_1_
  14.3 0.3 collective-permute-start.6
  14.7 1.8 %collective-permute-start.7 = (bf16[64,1024]{1,0:T(8,128)(2,1)S(1)}, bf16[64,1024]{1,0:T(8,128)(2,1)S(1)}, u32[]{:S(2)}, u32[]{:S(2)}) collective-permute-start(bf16[64,1024]{1,0:T(8,128)(2,1)S(1)} %collective-permute-done.5.refs_1_), channel_id=1, source_target_pairs={{0,1},{1,0},{2,3},{3,2},{4,5},{5,4},{6,7},{7,6},{8,9},{9,8},{10,11... | collective-permute-start | bytes 393224 | tf_op jit(solution)/shard_map/ppermute | solution.py:254
  16.4 3.6 %shard_map.112 = (f32[256,2048]{1,0:T(8,128)}, f32[256,2048]{1,0:T(8,128)}) custom-call(f32[256,2048]{1,0:T(8,128)} %refs_0_.6, f32[256,2048]{1,0:T(8,128)} %refs_1_.7, f32[256,2048]{1,0:T(8,128)} %refs_2_.7), custom_call_target="tpu_custom_call" | custom-call | bytes 31457280 | tf_op jit(solution)/shard_map/pallas_call | solution.py:149
  20.1 1.6 %shard_map.113.stale_ref = bf16[4,256,1024]{2,1,0:T(8,128)(2,1)S(1)} custom-call(bf16[8192,1024]{1,0:T(8,128)(2,1)} %stale_far.1), custom_call_target="tpu_custom_call" | custom-call | tf_op jit(solution)/shard_map/pallas_call | solution.py:195
  21.6 0.0 collective-permute-done.1.refs_4_
  21.6 2.3 %collective-permute-start.8 = (bf16[256,1024]{1,0:T(8,128)(2,1)S(1)}, bf16[256,1024]{1,0:T(8,128)(2,1)S(1)}, u32[]{:S(2)}, u32[]{:S(2)}) collective-permute-start(bf16[256,1024]{1,0:T(8,128)(2,1)S(1)} %shard_map.116.refs_0_), channel_id=1, source_target_pairs={{0,2},{2,0},{4,6},{6,4},{8,10},{10,8},{12,14},{14,12},{16,18},{18,... | collective-permute-start | bytes 1572872 | tf_op jit(solution)/shard_map/ppermute | solution.py:257
  23.9 0.2 collective-permute-done.2.refs_5_
  24.1 0.0 collective-permute-done.6.refs_2_
  24.1 0.0 collective-permute-done.7.refs_3_
  24.1 0.0 collective-permute-done.3.refs_1_
  24.1 0.1 collective-permute-start.9
  24.3 1.9 %collective-permute-start.12 = (bf16[64,1024]{1,0:T(8,128)(2,1)S(1)}, bf16[64,1024]{1,0:T(8,128)(2,1)S(1)}, u32[]{:S(2)}, u32[]{:S(2)}) collective-permute-start(bf16[64,1024]{1,0:T(8,128)(2,1)S(1)} %collective-permute-done.1.refs_4_), channel_id=1, source_target_pairs={{0,1},{1,0},{2,3},{3,2},{4,5},{5,4},{6,7},{7,6},{8,9},{9,8},{10,11... | collective-permute-start | bytes 393224 | tf_op jit(solution)/shard_map/ppermute | solution.py:254
  26.2 0.1 collective-permute-start.13
  26.3 0.0 collective-permute-done.8.refs_2_
  26.3 0.0 collective-permute-done.9.refs_3_
  26.3 1.5 %shard_map.118 = (bf16[1024,1024]{1,0:T(8,128)(2,1)S(1)}, f32[64,1024]{1,0:T(8,128)S(1)}, bf16[64,1024]{1,0:T(8,128)(2,1)S(1)}) custom-call(bf16[4,256,1024]{2,1,0:T(8,128)(2,1)S(1)} %shard_map.113.stale_ref, bf16[256,1024]{1,0:T(8,128)(2,1)S(1)} %shard_map.116.refs_0_, bf16[256,1024]{1,0:T(8,128)(2,1)S(1)} %collective-permute-done.3.refs_1_, ...), custom_call_target="tpu_custom_call" | custom-call | bytes 8388608 | tf_op jit(solution)/shard_map/pallas_call | solution.py:226
  27.8 1.8 %collective-permute-start.11 = (bf16[64,1024]{1,0:T(8,128)(2,1)S(1)}, bf16[64,1024]{1,0:T(8,128)(2,1)S(1)}, u32[]{:S(2)}, u32[]{:S(2)}) collective-permute-start(bf16[64,1024]{1,0:T(8,128)(2,1)S(1)} %get-tuple-element.71), channel_id=1, source_target_pairs={{0,4},{2,6},{4,0},{6,2},{8,12},{10,14},{12,8},{14,10},{16,20},{18,... | collective-permute-start | bytes 393224 | tf_op jit(solution)/shard_map/ppermute | solution.py:264
  29.6 0.7 %shard_map.119 = (bf16[128,1024]{1,0:T(8,128)(2,1)S(1)}, bf16[64,1024]{1,0:T(8,128)(2,1)S(1)}, bf16[64,1024]{1,0:T(8,128)(2,1)S(1)}) custom-call(bf16[64,1024]{1,0:T(8,128)(2,1)S(1)} %collective-permute-done.4.refs_0_, bf16[64,1024]{1,0:T(8,128)(2,1)S(1)} %collective-permute-done.5.refs_1_, bf16[64,1024]{1,0:T(8,128)(2,1)S(1)} %collective-permute-done.6.refs_2_, ...), custom_call_target="tpu_custom_call" | custom-call | tf_op jit(solution)/shard_map/pallas_call | solution.py:236
  30.3 0.7 %collective-permute-start.10 = (bf16[128,1024]{1,0:T(8,128)(2,1)S(1)}, bf16[128,1024]{1,0:T(8,128)(2,1)S(1)}, u32[]{:S(2)}, u32[]{:S(2)}) collective-permute-start(bf16[128,1024]{1,0:T(8,128)(2,1)S(1)} %get-tuple-element.70), channel_id=1, source_target_pairs={{0,0},{2,10},{4,4},{6,14},{8,8},{10,2},{12,12},{14,6},{16,16},{18,... | collective-permute-start | bytes 786440 | tf_op jit(solution)/shard_map/ppermute | solution.py:261
  31.0 0.0 collective-permute-done.12.refs_0_
  31.0 2.2 %collective-permute-done.13.refs_1_ = bf16[64,1024]{1,0:T(8,128)(2,1)S(1)} collective-permute-done((bf16[64,1024]{1,0:T(8,128)(2,1)S(1)}, bf16[64,1024]{1,0:T(8,128)(2,1)S(1)}, u32[]{:S(2)}, u32[]{:S(2)}) %collective-permute-start.13) | collective-permute-done | bytes 131104 | tf_op jit(solution)/shard_map/ppermute | solution.py:254
  33.2 0.3 collective-permute-done.11
  33.5 0.4 shard_map.120
  34.0 1.5 %collective-permute-start.16 = (bf16[64,1024]{1,0:T(8,128)(2,1)S(1)}, bf16[64,1024]{1,0:T(8,128)(2,1)S(1)}, u32[]{:S(2)}, u32[]{:S(2)}) collective-permute-start(bf16[64,1024]{1,0:T(8,128)(2,1)S(1)} %get-tuple-element.80), channel_id=1, source_target_pairs={{0,4},{2,6},{4,0},{6,2},{8,12},{10,14},{12,8},{14,10},{16,20},{18,... | collective-permute-start | bytes 393224 | tf_op jit(solution)/shard_map/ppermute | solution.py:264
  35.5 2.9 %collective-permute-start.15 = (bf16[64,1024]{1,0:T(8,128)(2,1)S(1)}, bf16[64,1024]{1,0:T(8,128)(2,1)S(1)}, u32[]{:S(2)}, u32[]{:S(2)}) collective-permute-start(bf16[64,1024]{1,0:T(8,128)(2,1)S(1)} %add_convert_fusion.1), channel_id=1, source_target_pairs={{0,16},{2,26},{4,20},{6,30},{8,24},{10,18},{12,28},{14,22},{16,0},... | collective-permute-start | bytes 393224 | tf_op jit(solution)/shard_map/ppermute | solution.py:261
  38.4 0.3 collective-permute-start.14
  38.7 0.7 %collective-permute-done.16 = bf16[64,1024]{1,0:T(8,128)(2,1)S(1)} collective-permute-done((bf16[64,1024]{1,0:T(8,128)(2,1)S(1)}, bf16[64,1024]{1,0:T(8,128)(2,1)S(1)}, u32[]{:S(2)}, u32[]{:S(2)}) %collective-permute-start.16) | collective-permute-done | bytes 131104 | tf_op jit(solution)/shard_map/ppermute | solution.py:264
  39.4 2.4 %collective-permute-start.17 = (bf16[64,1024]{1,0:T(8,128)(2,1)S(1)}, bf16[64,1024]{1,0:T(8,128)(2,1)S(1)}, u32[]{:S(2)}, u32[]{:S(2)}) collective-permute-start(bf16[64,1024]{1,0:T(8,128)(2,1)S(1)} %add_convert_fusion), channel_id=1, source_target_pairs={{0,16},{2,26},{4,20},{6,30},{8,24},{10,18},{12,28},{14,22},{16,0},... | collective-permute-start | bytes 393224 | tf_op jit(solution)/shard_map/ppermute | solution.py:261
  41.9 2.1 %collective-permute-start.18 = (bf16[64,1024]{1,0:T(8,128)(2,1)S(1)}, bf16[64,1024]{1,0:T(8,128)(2,1)S(1)}, u32[]{:S(2)}, u32[]{:S(2)}) collective-permute-start(bf16[64,1024]{1,0:T(8,128)(2,1)S(1)} %get-tuple-element.83), channel_id=1, source_target_pairs={{0,4},{2,14},{4,0},{6,10},{8,12},{10,6},{12,8},{14,2},{16,20},{18,... | collective-permute-start | bytes 393224 | tf_op jit(solution)/shard_map/ppermute | solution.py:261
  44.0 2.3 %shard_map.117 = (f32[256,2048]{1,0:T(8,128)}, f32[256,2048]{1,0:T(8,128)}) custom-call(f32[256,2048]{1,0:T(8,128)} %refs_0_.6, f32[256,2048]{1,0:T(8,128)} %refs_1_.7, f32[256,2048]{1,0:T(8,128)} %refs_2_.7, f32[256,2048]{1,0:T(8,128)} %get-tuple-element.58.refs_3_, f32[256,2048]{1,0:T(8,128)} %get-tuple-element.59.refs_4_), custom_call_target="tpu_custom_call", output_to_operand_aliasing={{0}: (3, {}), {1}: (4, {})} | custom-call | bytes 31457280 | tf_op jit(solution)/shard_map/pallas_call | solution.py:149
  46.3 0.0 copy-start.2
  46.3 0.0 collective-permute-done.10
  46.3 1.8 %collective-permute-done.15 = bf16[64,1024]{1,0:T(8,128)(2,1)S(1)} collective-permute-done((bf16[64,1024]{1,0:T(8,128)(2,1)S(1)}, bf16[64,1024]{1,0:T(8,128)(2,1)S(1)}, u32[]{:S(2)}, u32[]{:S(2)}) %collective-permute-start.15) | collective-permute-done | bytes 131104 | tf_op jit(solution)/shard_map/ppermute | solution.py:261
  48.1 0.0 collective-permute-done.14
  48.1 1.7 %collective-permute-done.17 = bf16[64,1024]{1,0:T(8,128)(2,1)S(1)} collective-permute-done((bf16[64,1024]{1,0:T(8,128)(2,1)S(1)}, bf16[64,1024]{1,0:T(8,128)(2,1)S(1)}, u32[]{:S(2)}, u32[]{:S(2)}) %collective-permute-start.17) | collective-permute-done | bytes 131104 | tf_op jit(solution)/shard_map/ppermute | solution.py:261
  49.9 0.0 collective-permute-done.18
  49.9 0.1 convert_add_fusion
  49.9 0.1 maximum_add_fusion
  50.0 0.1 collective-permute-start.19
  50.1 1.3 %collective-permute-done.19 = bf16[2,32,1024]{2,1,0:T(8,128)(2,1)S(1)} collective-permute-done((bf16[2,32,1024]{2,1,0:T(8,128)(2,1)S(1)}, bf16[2,32,1024]{2,1,0:T(8,128)(2,1)S(1)}, u32[]{:S(2)}, u32[]{:S(2)}) %collective-permute-start.19) | collective-permute-done | bytes 131104 | tf_op jit(solution)/shard_map/ppermute | solution.py:257
  51.5 0.0 copy-done.2
  51.5 0.7 %reverse_select_fusion = bf16[2,32,1024]{2,1,0:T(8,128)(2,1)} fusion(bf16[2,32,1024]{2,1,0:T(8,128)(2,1)S(1)} %fusion.3, pred[]{:T(512)S(6)} %eq.9), kind=kLoop, calls=%fused_computation.11 | loop fusion | flops 65536 | bytes 262145 | tf_op jit(solution)/shard_map/jit(_where)/select_n | solution.py:338
  (4 shorter events, 0.1 us)
Async XLA Ops:
  0.6 5.7 %copy-start = (bf16[32,8192]{1,0:T(8,128)(2,1)S(1)}, bf16[32,8192]{1,0:T(8,128)(2,1)}, u32[]{:S(2)}) copy-start(bf16[32,8192]{1,0:T(8,128)(2,1)} %ours_ref.1) | copy-start | bytes 1572868
  0.6 5.7 %copy-start.1 = (f32[8192]{0:T(1024)S(1)}, f32[8192]{0:T(1024)}, u32[]{:S(2)}) copy-start(f32[8192]{0:T(1024)} %param.10) | copy-start | bytes 98308
  0.6 3.0 %collective-permute-start = (bf16[32,8192]{1,0:T(8,128)(2,1)}, bf16[32,8192]{1,0:T(8,128)(2,1)S(1)}, u32[]{:S(2)}, u32[]{:S(2)}) collective-permute-start(bf16[32,8192]{1,0:T(8,128)(2,1)} %ours_ref.1), channel_id=1, source_target_pairs={{0,2},{2,0},{4,6},{6,4},{8,10},{10,8},{12,14},{14,12},{16,18},{18,... | collective-permute-start | bytes 1572872 | tf_op jit(solution)/shard_map/ppermute | solution.py:257
  3.7 20.5 %collective-permute-start.3 = (bf16[256,1024]{1,0:T(8,128)(2,1)S(1)}, bf16[256,1024]{1,0:T(8,128)(2,1)S(1)}, u32[]{:S(2)}, u32[]{:S(2)}) collective-permute-start(bf16[256,1024]{1,0:T(8,128)(2,1)S(1)} %shard_map.114), channel_id=1, source_target_pairs={{0,1},{1,0},{2,3},{3,2},{4,5},{5,4},{6,7},{7,6},{8,9},{9,8},{10,11... | collective-permute-start | bytes 1572872 | tf_op jit(solution)/shard_map/ppermute | solution.py:254
  6.7 7.6 %collective-permute-start.4 = (bf16[64,1024]{1,0:T(8,128)(2,1)S(1)}, bf16[64,1024]{1,0:T(8,128)(2,1)S(1)}, u32[]{:S(2)}, u32[]{:S(2)}) collective-permute-start(bf16[64,1024]{1,0:T(8,128)(2,1)S(1)} %get-tuple-element.53), channel_id=1, source_target_pairs={{0,0},{2,10},{4,4},{6,14},{8,8},{10,2},{12,12},{14,6},{16,16},{18,... | collective-permute-start | bytes 393224 | tf_op jit(solution)/shard_map/ppermute | solution.py:261
  7.4 7.0 %collective-permute-start.5 = (bf16[64,1024]{1,0:T(8,128)(2,1)S(1)}, bf16[64,1024]{1,0:T(8,128)(2,1)S(1)}, u32[]{:S(2)}, u32[]{:S(2)}) collective-permute-start(bf16[64,1024]{1,0:T(8,128)(2,1)S(1)} %get-tuple-element.54), channel_id=1, source_target_pairs={{0,4},{2,14},{4,0},{6,10},{8,12},{10,6},{12,8},{14,2},{16,20},{18,... | collective-permute-start | bytes 393224 | tf_op jit(solution)/shard_map/ppermute | solution.py:261
  8.9 12.7 %collective-permute-start.1 = (bf16[64,1024]{1,0:T(8,128)(2,1)S(1)}, bf16[64,1024]{1,0:T(8,128)(2,1)S(1)}, u32[]{:S(2)}, u32[]{:S(2)}) collective-permute-start(bf16[64,1024]{1,0:T(8,128)(2,1)S(1)} %get-tuple-element.50), channel_id=1, source_target_pairs={{0,16},{2,26},{4,20},{6,30},{8,24},{10,18},{12,28},{14,22},{16,0},... | collective-permute-start | bytes 393224 | tf_op jit(solution)/shard_map/ppermute | solution.py:261
  11.5 12.6 %collective-permute-start.2 = (bf16[64,1024]{1,0:T(8,128)(2,1)S(1)}, bf16[64,1024]{1,0:T(8,128)(2,1)S(1)}, u32[]{:S(2)}, u32[]{:S(2)}) collective-permute-start(bf16[64,1024]{1,0:T(8,128)(2,1)S(1)} %get-tuple-element.51), channel_id=1, source_target_pairs={{0,20},{2,30},{4,16},{6,26},{8,28},{10,22},{12,24},{14,18},{16,4},... | collective-permute-start | bytes 393224 | tf_op jit(solution)/shard_map/ppermute | solution.py:261
  14.3 9.8 %collective-permute-start.6 = (bf16[64,1024]{1,0:T(8,128)(2,1)S(1)}, bf16[64,1024]{1,0:T(8,128)(2,1)S(1)}, u32[]{:S(2)}, u32[]{:S(2)}) collective-permute-start(bf16[64,1024]{1,0:T(8,128)(2,1)S(1)} %collective-permute-done.4.refs_0_), channel_id=1, source_target_pairs={{0,1},{1,0},{2,3},{3,2},{4,5},{5,4},{6,7},{7,6},{8,9},{9,8},{10,11... | collective-permute-start | bytes 393224 | tf_op jit(solution)/shard_map/ppermute | solution.py:254
  14.7 9.5 %collective-permute-start.7 = (bf16[64,1024]{1,0:T(8,128)(2,1)S(1)}, bf16[64,1024]{1,0:T(8,128)(2,1)S(1)}, u32[]{:S(2)}, u32[]{:S(2)}) collective-permute-start(bf16[64,1024]{1,0:T(8,128)(2,1)S(1)} %collective-permute-done.5.refs_1_), channel_id=1, source_target_pairs={{0,1},{1,0},{2,3},{3,2},{4,5},{5,4},{6,7},{7,6},{8,9},{9,8},{10,11... | collective-permute-start | bytes 393224 | tf_op jit(solution)/shard_map/ppermute | solution.py:254
  21.6 4.7 %collective-permute-start.8 = (bf16[256,1024]{1,0:T(8,128)(2,1)S(1)}, bf16[256,1024]{1,0:T(8,128)(2,1)S(1)}, u32[]{:S(2)}, u32[]{:S(2)}) collective-permute-start(bf16[256,1024]{1,0:T(8,128)(2,1)S(1)} %shard_map.116.refs_0_), channel_id=1, source_target_pairs={{0,2},{2,0},{4,6},{6,4},{8,10},{10,8},{12,14},{14,12},{16,18},{18,... | collective-permute-start | bytes 1572872 | tf_op jit(solution)/shard_map/ppermute | solution.py:257
  24.1 2.2 %collective-permute-start.9 = (bf16[256,1024]{1,0:T(8,128)(2,1)S(1)}, bf16[256,1024]{1,0:T(8,128)(2,1)S(1)}, u32[]{:S(2)}, u32[]{:S(2)}) collective-permute-start(bf16[256,1024]{1,0:T(8,128)(2,1)S(1)} %collective-permute-done.3.refs_1_), channel_id=1, source_target_pairs={{0,2},{2,0},{4,6},{6,4},{8,10},{10,8},{12,14},{14,12},{16,18},{18,... | collective-permute-start | bytes 1572872 | tf_op jit(solution)/shard_map/ppermute | solution.py:257
  24.3 6.7 %collective-permute-start.12 = (bf16[64,1024]{1,0:T(8,128)(2,1)S(1)}, bf16[64,1024]{1,0:T(8,128)(2,1)S(1)}, u32[]{:S(2)}, u32[]{:S(2)}) collective-permute-start(bf16[64,1024]{1,0:T(8,128)(2,1)S(1)} %collective-permute-done.1.refs_4_), channel_id=1, source_target_pairs={{0,1},{1,0},{2,3},{3,2},{4,5},{5,4},{6,7},{7,6},{8,9},{9,8},{10,11... | collective-permute-start | bytes 393224 | tf_op jit(solution)/shard_map/ppermute | solution.py:254
  26.2 7.0 %collective-permute-start.13 = (bf16[64,1024]{1,0:T(8,128)(2,1)S(1)}, bf16[64,1024]{1,0:T(8,128)(2,1)S(1)}, u32[]{:S(2)}, u32[]{:S(2)}) collective-permute-start(bf16[64,1024]{1,0:T(8,128)(2,1)S(1)} %collective-permute-done.2.refs_5_), channel_id=1, source_target_pairs={{0,1},{1,0},{2,3},{3,2},{4,5},{5,4},{6,7},{7,6},{8,9},{9,8},{10,11... | collective-permute-start | bytes 393224 | tf_op jit(solution)/shard_map/ppermute | solution.py:254
  27.8 5.7 %collective-permute-start.11 = (bf16[64,1024]{1,0:T(8,128)(2,1)S(1)}, bf16[64,1024]{1,0:T(8,128)(2,1)S(1)}, u32[]{:S(2)}, u32[]{:S(2)}) collective-permute-start(bf16[64,1024]{1,0:T(8,128)(2,1)S(1)} %get-tuple-element.71), channel_id=1, source_target_pairs={{0,4},{2,6},{4,0},{6,2},{8,12},{10,14},{12,8},{14,10},{16,20},{18,... | collective-permute-start | bytes 393224 | tf_op jit(solution)/shard_map/ppermute | solution.py:264
  30.3 16.0 %collective-permute-start.10 = (bf16[128,1024]{1,0:T(8,128)(2,1)S(1)}, bf16[128,1024]{1,0:T(8,128)(2,1)S(1)}, u32[]{:S(2)}, u32[]{:S(2)}) collective-permute-start(bf16[128,1024]{1,0:T(8,128)(2,1)S(1)} %get-tuple-element.70), channel_id=1, source_target_pairs={{0,0},{2,10},{4,4},{6,14},{8,8},{10,2},{12,12},{14,6},{16,16},{18,... | collective-permute-start | bytes 786440 | tf_op jit(solution)/shard_map/ppermute | solution.py:261
  34.0 5.4 %collective-permute-start.16 = (bf16[64,1024]{1,0:T(8,128)(2,1)S(1)}, bf16[64,1024]{1,0:T(8,128)(2,1)S(1)}, u32[]{:S(2)}, u32[]{:S(2)}) collective-permute-start(bf16[64,1024]{1,0:T(8,128)(2,1)S(1)} %get-tuple-element.80), channel_id=1, source_target_pairs={{0,4},{2,6},{4,0},{6,2},{8,12},{10,14},{12,8},{14,10},{16,20},{18,... | collective-permute-start | bytes 393224 | tf_op jit(solution)/shard_map/ppermute | solution.py:264
  35.5 12.6 %collective-permute-start.15 = (bf16[64,1024]{1,0:T(8,128)(2,1)S(1)}, bf16[64,1024]{1,0:T(8,128)(2,1)S(1)}, u32[]{:S(2)}, u32[]{:S(2)}) collective-permute-start(bf16[64,1024]{1,0:T(8,128)(2,1)S(1)} %add_convert_fusion.1), channel_id=1, source_target_pairs={{0,16},{2,26},{4,20},{6,30},{8,24},{10,18},{12,28},{14,22},{16,0},... | collective-permute-start | bytes 393224 | tf_op jit(solution)/shard_map/ppermute | solution.py:261
  38.4 9.7 %collective-permute-start.14 = (bf16[64,1024]{1,0:T(8,128)(2,1)S(1)}, bf16[64,1024]{1,0:T(8,128)(2,1)S(1)}, u32[]{:S(2)}, u32[]{:S(2)}) collective-permute-start(bf16[64,1024]{1,0:T(8,128)(2,1)S(1)} %get-tuple-element.76), channel_id=1, source_target_pairs={{0,4},{2,14},{4,0},{6,10},{8,12},{10,6},{12,8},{14,2},{16,20},{18,... | collective-permute-start | bytes 393224 | tf_op jit(solution)/shard_map/ppermute | solution.py:261
  39.4 10.4 %collective-permute-start.17 = (bf16[64,1024]{1,0:T(8,128)(2,1)S(1)}, bf16[64,1024]{1,0:T(8,128)(2,1)S(1)}, u32[]{:S(2)}, u32[]{:S(2)}) collective-permute-start(bf16[64,1024]{1,0:T(8,128)(2,1)S(1)} %add_convert_fusion), channel_id=1, source_target_pairs={{0,16},{2,26},{4,20},{6,30},{8,24},{10,18},{12,28},{14,22},{16,0},... | collective-permute-start | bytes 393224 | tf_op jit(solution)/shard_map/ppermute | solution.py:261
  41.9 8.0 %collective-permute-start.18 = (bf16[64,1024]{1,0:T(8,128)(2,1)S(1)}, bf16[64,1024]{1,0:T(8,128)(2,1)S(1)}, u32[]{:S(2)}, u32[]{:S(2)}) collective-permute-start(bf16[64,1024]{1,0:T(8,128)(2,1)S(1)} %get-tuple-element.83), channel_id=1, source_target_pairs={{0,4},{2,14},{4,0},{6,10},{8,12},{10,6},{12,8},{14,2},{16,20},{18,... | collective-permute-start | bytes 393224 | tf_op jit(solution)/shard_map/ppermute | solution.py:261
  46.3 5.1 %copy-start.2 = (f32[1024]{0:T(1024)S(1)}, f32[1024]{0:T(1024)}, u32[]{:S(2)}) copy-start(f32[1024]{0:T(1024)} %param.12) | copy-start | bytes 12292
  50.0 1.4 %collective-permute-start.19 = (bf16[2,32,1024]{2,1,0:T(8,128)(2,1)S(1)}, bf16[2,32,1024]{2,1,0:T(8,128)(2,1)S(1)}, u32[]{:S(2)}, u32[]{:S(2)}) collective-permute-start(bf16[2,32,1024]{2,1,0:T(8,128)(2,1)S(1)} %fusion.4), channel_id=1, source_target_pairs={{0,2},{2,0},{4,6},{6,4},{8,10},{10,8},{12,14},{14,12},{16,18},{18,... | collective-permute-start | bytes 393224 | tf_op jit(solution)/shard_map/ppermute | solution.py:257

commit v10 on v9

--- a/solution.py
+++ b/solution.py
@@ -96,7 +96,7 @@
                 delta_outs[j][here, lanes] = jnp.clip(corrected, -most, most).astype(BF16)
 
 
-def delta(arrays, exponent, heads, start, count, chunks=4):
+def delta(arrays, exponent, heads, start, count, chunks=8):
     rows, full = arrays[0].shape
     qrows, qcol = rows // exponent.shape[0], full // exponent.shape[1]
     cols = full // heads

time: 52.4 us -> 52.5 us (level)
  no operation moved by 1% of the time
where the time goes in v10:
time: 52.5 us; the launch traced here: 52.3 us
  starting transfers between devices  26.5 us (50%)
  Pallas kernels  15.7 us (30%)
  waiting for transfers between devices  8.24 us (16%)
  other arithmetic  0.93 us (2%)
  between operations  0.85 us (2%)
    ppermute x9, starting transfers between devices, over_slab(): return lax.ppermute(x, 'dp', pairs)  13.4 us
    ppermute x5, starting transfers between devices, over_tensor(): lax.ppermute(x, 'tensor', [(i, i ^ j) for i in range(heads)])  6.74 us
    pallas_call x2, Pallas kernels, moments(): pl.pallas_call(functools.partial(moments_kernel, start, size, chunks), in...  5.96 us
    pallas_call x2, Pallas kernels, delta(): pl.pallas_call(functools.partial(delta_kernel, chunks, qrows, qcol, heads...  5.25 us
    ppermute x9, waiting for transfers between devices, over_slab(): return lax.ppermute(x, 'dp', pairs)  3.6 us
    ppermute x2, starting transfers between devices, over_next(): return lax.ppermute(x, 'dp', [(i, i ^ PAIR) for i in range(replicas)])  3.33 us
    ppermute x4, starting transfers between devices, over_core(): return lax.ppermute(x, 'dp', [(i, i ^ 1) for i in range(replicas)])  3 us
    ppermute x5, waiting for transfers between devices, over_tensor(): lax.ppermute(x, 'tensor', [(i, i ^ j) for i in range(heads)])  2.16 us
  transfers between devices with their start and end apart: 20, of which 7 were waited for; matrix products, arithmetic and copies ran while one was open for 0% of the time, Pallas kernels for 30%

profile of v10, /device:TPU:0, one launch (start us, length us, event | category | flops | bytes accessed | tf_op | source)
XLA Modules:
  0.0 52.3 jit_solution(12227626754783617481)
XLA Ops:
  0.6 0.0 copy-start
  0.6 0.0 copy-start.1
  0.6 0.5 collective-permute-start
  1.2 2.6 %shard_map.114 = bf16[256,1024]{1,0:T(8,128)(2,1)S(1)} custom-call(s32[8,16]{1,0:T(8,128)} %refs_0_.5, f32[256,2048]{1,0:T(8,128)} %refs_0_.6, f32[256,2048]{1,0:T(8,128)} %refs_1_.7, f32[256,2048]{1,0:T(8,128)} %refs_2_.7, f32[256,2048]{1,0:T(8,128)} %refs_4_.3), custom_call_target="tpu_custom_call" | custom-call | tf_op jit(solution)/shard_map/pallas_call | solution.py:104
  3.8 0.0 collective-permute-done.theirs_ref
  3.8 2.6 %collective-permute-start.3 = (bf16[256,1024]{1,0:T(8,128)(2,1)S(1)}, bf16[256,1024]{1,0:T(8,128)(2,1)S(1)}, u32[]{:S(2)}, u32[]{:S(2)}) collective-permute-start(bf16[256,1024]{1,0:T(8,128)(2,1)S(1)} %shard_map.114), channel_id=1, source_target_pairs={{0,1},{1,0},{2,3},{3,2},{4,5},{5,4},{6,7},{7,6},{8,9},{9,8},{10,11... | collective-permute-start | bytes 1572872 | tf_op jit(solution)/shard_map/ppermute | solution.py:254
  6.4 0.0 copy-done
  6.4 0.0 copy-done.1
  6.4 0.4 shard_map.115
  6.8 0.7 %collective-permute-start.4 = (bf16[64,1024]{1,0:T(8,128)(2,1)S(1)}, bf16[64,1024]{1,0:T(8,128)(2,1)S(1)}, u32[]{:S(2)}, u32[]{:S(2)}) collective-permute-start(bf16[64,1024]{1,0:T(8,128)(2,1)S(1)} %get-tuple-element.53), channel_id=1, source_target_pairs={{0,0},{2,10},{4,4},{6,14},{8,8},{10,2},{12,12},{14,6},{16,16},{18,... | collective-permute-start | bytes 393224 | tf_op jit(solution)/shard_map/ppermute | solution.py:261
  7.5 1.6 %collective-permute-start.5 = (bf16[64,1024]{1,0:T(8,128)(2,1)S(1)}, bf16[64,1024]{1,0:T(8,128)(2,1)S(1)}, u32[]{:S(2)}, u32[]{:S(2)}) collective-permute-start(bf16[64,1024]{1,0:T(8,128)(2,1)S(1)} %get-tuple-element.54), channel_id=1, source_target_pairs={{0,4},{2,14},{4,0},{6,10},{8,12},{10,6},{12,8},{14,2},{16,20},{18,... | collective-permute-start | bytes 393224 | tf_op jit(solution)/shard_map/ppermute | solution.py:261
  9.1 2.6 %collective-permute-start.1 = (bf16[64,1024]{1,0:T(8,128)(2,1)S(1)}, bf16[64,1024]{1,0:T(8,128)(2,1)S(1)}, u32[]{:S(2)}, u32[]{:S(2)}) collective-permute-start(bf16[64,1024]{1,0:T(8,128)(2,1)S(1)} %get-tuple-element.50), channel_id=1, source_target_pairs={{0,16},{2,26},{4,20},{6,30},{8,24},{10,18},{12,28},{14,22},{16,0},... | collective-permute-start | bytes 393224 | tf_op jit(solution)/shard_map/ppermute | solution.py:261
  11.7 0.3 collective-permute-start.2
  11.9 2.6 %shard_map.116.refs_0_ = bf16[256,1024]{1,0:T(8,128)(2,1)S(1)} custom-call(s32[8,16]{1,0:T(8,128)} %refs_0_.5, f32[256,2048]{1,0:T(8,128)} %refs_0_.6, f32[256,2048]{1,0:T(8,128)} %refs_1_.7, f32[256,2048]{1,0:T(8,128)} %refs_2_.7, f32[256,2048]{1,0:T(8,128)} %refs_4_.3), custom_call_target="tpu_custom_call" | custom-call | tf_op jit(solution)/shard_map/pallas_call | solution.py:104
  14.6 0.0 collective-permute-done.4.refs_0_
  14.6 0.0 collective-permute-done.5.refs_1_
  14.6 0.3 collective-permute-start.6
  14.9 1.8 %collective-permute-start.7 = (bf16[64,1024]{1,0:T(8,128)(2,1)S(1)}, bf16[64,1024]{1,0:T(8,128)(2,1)S(1)}, u32[]{:S(2)}, u32[]{:S(2)}) collective-permute-start(bf16[64,1024]{1,0:T(8,128)(2,1)S(1)} %collective-permute-done.5.refs_1_), channel_id=1, source_target_pairs={{0,1},{1,0},{2,3},{3,2},{4,5},{5,4},{6,7},{7,6},{8,9},{9,8},{10,11... | collective-permute-start | bytes 393224 | tf_op jit(solution)/shard_map/ppermute | solution.py:254
  16.7 3.6 %shard_map.112 = (f32[256,2048]{1,0:T(8,128)}, f32[256,2048]{1,0:T(8,128)}) custom-call(f32[256,2048]{1,0:T(8,128)} %refs_0_.6, f32[256,2048]{1,0:T(8,128)} %refs_1_.7, f32[256,2048]{1,0:T(8,128)} %refs_2_.7), custom_call_target="tpu_custom_call" | custom-call | bytes 31457280 | tf_op jit(solution)/shard_map/pallas_call | solution.py:149
  20.3 1.6 %shard_map.113.stale_ref = bf16[4,256,1024]{2,1,0:T(8,128)(2,1)S(1)} custom-call(bf16[8192,1024]{1,0:T(8,128)(2,1)} %stale_far.1), custom_call_target="tpu_custom_call" | custom-call | tf_op jit(solution)/shard_map/pallas_call | solution.py:195
  21.9 0.0 collective-permute-done.1.refs_4_
  21.9 2.3 %collective-permute-start.8 = (bf16[256,1024]{1,0:T(8,128)(2,1)S(1)}, bf16[256,1024]{1,0:T(8,128)(2,1)S(1)}, u32[]{:S(2)}, u32[]{:S(2)}) collective-permute-start(bf16[256,1024]{1,0:T(8,128)(2,1)S(1)} %shard_map.116.refs_0_), channel_id=1, source_target_pairs={{0,2},{2,0},{4,6},{6,4},{8,10},{10,8},{12,14},{14,12},{16,18},{18,... | collective-permute-start | bytes 1572872 | tf_op jit(solution)/shard_map/ppermute | solution.py:257
  24.2 0.1 collective-permute-done.2.refs_5_
  24.2 0.0 collective-permute-done.6.refs_2_
  24.2 0.0 collective-permute-done.7.refs_3_
  24.2 0.0 collective-permute-done.3.refs_1_
  24.3 0.1 collective-permute-start.9
  24.4 1.9 %collective-permute-start.12 = (bf16[64,1024]{1,0:T(8,128)(2,1)S(1)}, bf16[64,1024]{1,0:T(8,128)(2,1)S(1)}, u32[]{:S(2)}, u32[]{:S(2)}) collective-permute-start(bf16[64,1024]{1,0:T(8,128)(2,1)S(1)} %collective-permute-done.1.refs_4_), channel_id=1, source_target_pairs={{0,1},{1,0},{2,3},{3,2},{4,5},{5,4},{6,7},{7,6},{8,9},{9,8},{10,11... | collective-permute-start | bytes 393224 | tf_op jit(solution)/shard_map/ppermute | solution.py:254
  26.3 0.1 collective-permute-start.13
  26.4 0.0 collective-permute-done.8.refs_2_
  26.4 0.0 collective-permute-done.9.refs_3_
  26.5 1.5 %shard_map.118 = (bf16[1024,1024]{1,0:T(8,128)(2,1)S(1)}, f32[64,1024]{1,0:T(8,128)S(1)}, bf16[64,1024]{1,0:T(8,128)(2,1)S(1)}) custom-call(bf16[4,256,1024]{2,1,0:T(8,128)(2,1)S(1)} %shard_map.113.stale_ref, bf16[256,1024]{1,0:T(8,128)(2,1)S(1)} %shard_map.116.refs_0_, bf16[256,1024]{1,0:T(8,128)(2,1)S(1)} %collective-permute-done.3.refs_1_, ...), custom_call_target="tpu_custom_call" | custom-call | bytes 8388608 | tf_op jit(solution)/shard_map/pallas_call | solution.py:226
  27.9 1.8 %collective-permute-start.11 = (bf16[64,1024]{1,0:T(8,128)(2,1)S(1)}, bf16[64,1024]{1,0:T(8,128)(2,1)S(1)}, u32[]{:S(2)}, u32[]{:S(2)}) collective-permute-start(bf16[64,1024]{1,0:T(8,128)(2,1)S(1)} %get-tuple-element.71), channel_id=1, source_target_pairs={{0,4},{2,6},{4,0},{6,2},{8,12},{10,14},{12,8},{14,10},{16,20},{18,... | collective-permute-start | bytes 393224 | tf_op jit(solution)/shard_map/ppermute | solution.py:264
  29.7 0.7 %shard_map.119 = (bf16[128,1024]{1,0:T(8,128)(2,1)S(1)}, bf16[64,1024]{1,0:T(8,128)(2,1)S(1)}, bf16[64,1024]{1,0:T(8,128)(2,1)S(1)}) custom-call(bf16[64,1024]{1,0:T(8,128)(2,1)S(1)} %collective-permute-done.4.refs_0_, bf16[64,1024]{1,0:T(8,128)(2,1)S(1)} %collective-permute-done.5.refs_1_, bf16[64,1024]{1,0:T(8,128)(2,1)S(1)} %collective-permute-done.6.refs_2_, ...), custom_call_target="tpu_custom_call" | custom-call | tf_op jit(solution)/shard_map/pallas_call | solution.py:236
  30.5 0.7 %collective-permute-start.10 = (bf16[128,1024]{1,0:T(8,128)(2,1)S(1)}, bf16[128,1024]{1,0:T(8,128)(2,1)S(1)}, u32[]{:S(2)}, u32[]{:S(2)}) collective-permute-start(bf16[128,1024]{1,0:T(8,128)(2,1)S(1)} %get-tuple-element.70), channel_id=1, source_target_pairs={{0,0},{2,10},{4,4},{6,14},{8,8},{10,2},{12,12},{14,6},{16,16},{18,... | collective-permute-start | bytes 786440 | tf_op jit(solution)/shard_map/ppermute | solution.py:261
  31.1 0.0 collective-permute-done.12.refs_0_
  31.1 2.2 %collective-permute-done.13.refs_1_ = bf16[64,1024]{1,0:T(8,128)(2,1)S(1)} collective-permute-done((bf16[64,1024]{1,0:T(8,128)(2,1)S(1)}, bf16[64,1024]{1,0:T(8,128)(2,1)S(1)}, u32[]{:S(2)}, u32[]{:S(2)}) %collective-permute-start.13) | collective-permute-done | bytes 131104 | tf_op jit(solution)/shard_map/ppermute | solution.py:254
  33.3 0.5 collective-permute-done.11
  33.8 0.4 shard_map.120
  34.2 1.5 %collective-permute-start.16 = (bf16[64,1024]{1,0:T(8,128)(2,1)S(1)}, bf16[64,1024]{1,0:T(8,128)(2,1)S(1)}, u32[]{:S(2)}, u32[]{:S(2)}) collective-permute-start(bf16[64,1024]{1,0:T(8,128)(2,1)S(1)} %get-tuple-element.80), channel_id=1, source_target_pairs={{0,4},{2,6},{4,0},{6,2},{8,12},{10,14},{12,8},{14,10},{16,20},{18,... | collective-permute-start | bytes 393224 | tf_op jit(solution)/shard_map/ppermute | solution.py:264
  35.8 2.8 %collective-permute-start.15 = (bf16[64,1024]{1,0:T(8,128)(2,1)S(1)}, bf16[64,1024]{1,0:T(8,128)(2,1)S(1)}, u32[]{:S(2)}, u32[]{:S(2)}) collective-permute-start(bf16[64,1024]{1,0:T(8,128)(2,1)S(1)} %add_convert_fusion.1), channel_id=1, source_target_pairs={{0,16},{2,26},{4,20},{6,30},{8,24},{10,18},{12,28},{14,22},{16,0},... | collective-permute-start | bytes 393224 | tf_op jit(solution)/shard_map/ppermute | solution.py:261
  38.5 0.3 collective-permute-start.14
  38.9 0.7 %collective-permute-done.16 = bf16[64,1024]{1,0:T(8,128)(2,1)S(1)} collective-permute-done((bf16[64,1024]{1,0:T(8,128)(2,1)S(1)}, bf16[64,1024]{1,0:T(8,128)(2,1)S(1)}, u32[]{:S(2)}, u32[]{:S(2)}) %collective-permute-start.16) | collective-permute-done | bytes 131104 | tf_op jit(solution)/shard_map/ppermute | solution.py:264
  39.5 2.7 %collective-permute-start.17 = (bf16[64,1024]{1,0:T(8,128)(2,1)S(1)}, bf16[64,1024]{1,0:T(8,128)(2,1)S(1)}, u32[]{:S(2)}, u32[]{:S(2)}) collective-permute-start(bf16[64,1024]{1,0:T(8,128)(2,1)S(1)} %add_convert_fusion), channel_id=1, source_target_pairs={{0,16},{2,26},{4,20},{6,30},{8,24},{10,18},{12,28},{14,22},{16,0},... | collective-permute-start | bytes 393224 | tf_op jit(solution)/shard_map/ppermute | solution.py:261
  42.3 1.8 %collective-permute-start.18 = (bf16[64,1024]{1,0:T(8,128)(2,1)S(1)}, bf16[64,1024]{1,0:T(8,128)(2,1)S(1)}, u32[]{:S(2)}, u32[]{:S(2)}) collective-permute-start(bf16[64,1024]{1,0:T(8,128)(2,1)S(1)} %get-tuple-element.83), channel_id=1, source_target_pairs={{0,4},{2,14},{4,0},{6,10},{8,12},{10,6},{12,8},{14,2},{16,20},{18,... | collective-permute-start | bytes 393224 | tf_op jit(solution)/shard_map/ppermute | solution.py:261
  44.1 2.3 %shard_map.117 = (f32[256,2048]{1,0:T(8,128)}, f32[256,2048]{1,0:T(8,128)}) custom-call(f32[256,2048]{1,0:T(8,128)} %refs_0_.6, f32[256,2048]{1,0:T(8,128)} %refs_1_.7, f32[256,2048]{1,0:T(8,128)} %refs_2_.7, f32[256,2048]{1,0:T(8,128)} %get-tuple-element.58.refs_3_, f32[256,2048]{1,0:T(8,128)} %get-tuple-element.59.refs_4_), custom_call_target="tpu_custom_call", output_to_operand_aliasing={{0}: (3, {}), {1}: (4, {})} | custom-call | bytes 31457280 | tf_op jit(solution)/shard_map/pallas_call | solution.py:149
  46.4 0.0 copy-start.2
  46.5 0.0 collective-permute-done.10
  46.5 1.8 %collective-permute-done.15 = bf16[64,1024]{1,0:T(8,128)(2,1)S(1)} collective-permute-done((bf16[64,1024]{1,0:T(8,128)(2,1)S(1)}, bf16[64,1024]{1,0:T(8,128)(2,1)S(1)}, u32[]{:S(2)}, u32[]{:S(2)}) %collective-permute-start.15) | collective-permute-done | bytes 131104 | tf_op jit(solution)/shard_map/ppermute | solution.py:261
  48.3 0.0 collective-permute-done.14
  48.3 1.7 %collective-permute-done.17 = bf16[64,1024]{1,0:T(8,128)(2,1)S(1)} collective-permute-done((bf16[64,1024]{1,0:T(8,128)(2,1)S(1)}, bf16[64,1024]{1,0:T(8,128)(2,1)S(1)}, u32[]{:S(2)}, u32[]{:S(2)}) %collective-permute-start.17) | collective-permute-done | bytes 131104 | tf_op jit(solution)/shard_map/ppermute | solution.py:261
  50.0 0.0 collective-permute-done.18
  50.0 0.1 convert_add_fusion
  50.1 0.1 maximum_add_fusion
  50.2 0.1 collective-permute-start.19
  50.2 1.3 %collective-permute-done.19 = bf16[2,32,1024]{2,1,0:T(8,128)(2,1)S(1)} collective-permute-done((bf16[2,32,1024]{2,1,0:T(8,128)(2,1)S(1)}, bf16[2,32,1024]{2,1,0:T(8,128)(2,1)S(1)}, u32[]{:S(2)}, u32[]{:S(2)}) %collective-permute-start.19) | collective-permute-done | bytes 131104 | tf_op jit(solution)/shard_map/ppermute | solution.py:257
  51.6 0.0 copy-done.2
  51.6 0.7 %reverse_select_fusion = bf16[2,32,1024]{2,1,0:T(8,128)(2,1)} fusion(bf16[2,32,1024]{2,1,0:T(8,128)(2,1)S(1)} %fusion.3, pred[]{:T(512)S(6)} %eq.9), kind=kLoop, calls=%fused_computation.11 | loop fusion | flops 65536 | bytes 262145 | tf_op jit(solution)/shard_map/jit(_where)/select_n | solution.py:338
  (4 shorter events, 0.1 us)
Async XLA Ops:
  0.6 5.8 %copy-start = (bf16[32,8192]{1,0:T(8,128)(2,1)S(1)}, bf16[32,8192]{1,0:T(8,128)(2,1)}, u32[]{:S(2)}) copy-start(bf16[32,8192]{1,0:T(8,128)(2,1)} %ours_ref.1) | copy-start | bytes 1572868
  0.6 5.8 %copy-start.1 = (f32[8192]{0:T(1024)S(1)}, f32[8192]{0:T(1024)}, u32[]{:S(2)}) copy-start(f32[8192]{0:T(1024)} %param.10) | copy-start | bytes 98308
  0.6 3.2 %collective-permute-start = (bf16[32,8192]{1,0:T(8,128)(2,1)}, bf16[32,8192]{1,0:T(8,128)(2,1)S(1)}, u32[]{:S(2)}, u32[]{:S(2)}) collective-permute-start(bf16[32,8192]{1,0:T(8,128)(2,1)} %ours_ref.1), channel_id=1, source_target_pairs={{0,2},{2,0},{4,6},{6,4},{8,10},{10,8},{12,14},{14,12},{16,18},{18,... | collective-permute-start | bytes 1572872 | tf_op jit(solution)/shard_map/ppermute | solution.py:257
  3.8 20.4 %collective-permute-start.3 = (bf16[256,1024]{1,0:T(8,128)(2,1)S(1)}, bf16[256,1024]{1,0:T(8,128)(2,1)S(1)}, u32[]{:S(2)}, u32[]{:S(2)}) collective-permute-start(bf16[256,1024]{1,0:T(8,128)(2,1)S(1)} %shard_map.114), channel_id=1, source_target_pairs={{0,1},{1,0},{2,3},{3,2},{4,5},{5,4},{6,7},{7,6},{8,9},{9,8},{10,11... | collective-permute-start | bytes 1572872 | tf_op jit(solution)/shard_map/ppermute | solution.py:254
  6.8 7.8 %collective-permute-start.4 = (bf16[64,1024]{1,0:T(8,128)(2,1)S(1)}, bf16[64,1024]{1,0:T(8,128)(2,1)S(1)}, u32[]{:S(2)}, u32[]{:S(2)}) collective-permute-start(bf16[64,1024]{1,0:T(8,128)(2,1)S(1)} %get-tuple-element.53), channel_id=1, source_target_pairs={{0,0},{2,10},{4,4},{6,14},{8,8},{10,2},{12,12},{14,6},{16,16},{18,... | collective-permute-start | bytes 393224 | tf_op jit(solution)/shard_map/ppermute | solution.py:261
  7.5 7.1 %collective-permute-start.5 = (bf16[64,1024]{1,0:T(8,128)(2,1)S(1)}, bf16[64,1024]{1,0:T(8,128)(2,1)S(1)}, u32[]{:S(2)}, u32[]{:S(2)}) collective-permute-start(bf16[64,1024]{1,0:T(8,128)(2,1)S(1)} %get-tuple-element.54), channel_id=1, source_target_pairs={{0,4},{2,14},{4,0},{6,10},{8,12},{10,6},{12,8},{14,2},{16,20},{18,... | collective-permute-start | bytes 393224 | tf_op jit(solution)/shard_map/ppermute | solution.py:261
  9.1 12.8 %collective-permute-start.1 = (bf16[64,1024]{1,0:T(8,128)(2,1)S(1)}, bf16[64,1024]{1,0:T(8,128)(2,1)S(1)}, u32[]{:S(2)}, u32[]{:S(2)}) collective-permute-start(bf16[64,1024]{1,0:T(8,128)(2,1)S(1)} %get-tuple-element.50), channel_id=1, source_target_pairs={{0,16},{2,26},{4,20},{6,30},{8,24},{10,18},{12,28},{14,22},{16,0},... | collective-permute-start | bytes 393224 | tf_op jit(solution)/shard_map/ppermute | solution.py:261
  11.7 12.6 %collective-permute-start.2 = (bf16[64,1024]{1,0:T(8,128)(2,1)S(1)}, bf16[64,1024]{1,0:T(8,128)(2,1)S(1)}, u32[]{:S(2)}, u32[]{:S(2)}) collective-permute-start(bf16[64,1024]{1,0:T(8,128)(2,1)S(1)} %get-tuple-element.51), channel_id=1, source_target_pairs={{0,20},{2,30},{4,16},{6,26},{8,28},{10,22},{12,24},{14,18},{16,4},... | collective-permute-start | bytes 393224 | tf_op jit(solution)/shard_map/ppermute | solution.py:261
  14.6 9.7 %collective-permute-start.6 = (bf16[64,1024]{1,0:T(8,128)(2,1)S(1)}, bf16[64,1024]{1,0:T(8,128)(2,1)S(1)}, u32[]{:S(2)}, u32[]{:S(2)}) collective-permute-start(bf16[64,1024]{1,0:T(8,128)(2,1)S(1)} %collective-permute-done.4.refs_0_), channel_id=1, source_target_pairs={{0,1},{1,0},{2,3},{3,2},{4,5},{5,4},{6,7},{7,6},{8,9},{9,8},{10,11... | collective-permute-start | bytes 393224 | tf_op jit(solution)/shard_map/ppermute | solution.py:254
  14.9 9.3 %collective-permute-start.7 = (bf16[64,1024]{1,0:T(8,128)(2,1)S(1)}, bf16[64,1024]{1,0:T(8,128)(2,1)S(1)}, u32[]{:S(2)}, u32[]{:S(2)}) collective-permute-start(bf16[64,1024]{1,0:T(8,128)(2,1)S(1)} %collective-permute-done.5.refs_1_), channel_id=1, source_target_pairs={{0,1},{1,0},{2,3},{3,2},{4,5},{5,4},{6,7},{7,6},{8,9},{9,8},{10,11... | collective-permute-start | bytes 393224 | tf_op jit(solution)/shard_map/ppermute | solution.py:254
  21.9 4.5 %collective-permute-start.8 = (bf16[256,1024]{1,0:T(8,128)(2,1)S(1)}, bf16[256,1024]{1,0:T(8,128)(2,1)S(1)}, u32[]{:S(2)}, u32[]{:S(2)}) collective-permute-start(bf16[256,1024]{1,0:T(8,128)(2,1)S(1)} %shard_map.116.refs_0_), channel_id=1, source_target_pairs={{0,2},{2,0},{4,6},{6,4},{8,10},{10,8},{12,14},{14,12},{16,18},{18,... | collective-permute-start | bytes 1572872 | tf_op jit(solution)/shard_map/ppermute | solution.py:257
  24.3 2.2 %collective-permute-start.9 = (bf16[256,1024]{1,0:T(8,128)(2,1)S(1)}, bf16[256,1024]{1,0:T(8,128)(2,1)S(1)}, u32[]{:S(2)}, u32[]{:S(2)}) collective-permute-start(bf16[256,1024]{1,0:T(8,128)(2,1)S(1)} %collective-permute-done.3.refs_1_), channel_id=1, source_target_pairs={{0,2},{2,0},{4,6},{6,4},{8,10},{10,8},{12,14},{14,12},{16,18},{18,... | collective-permute-start | bytes 1572872 | tf_op jit(solution)/shard_map/ppermute | solution.py:257
  24.4 6.7 %collective-permute-start.12 = (bf16[64,1024]{1,0:T(8,128)(2,1)S(1)}, bf16[64,1024]{1,0:T(8,128)(2,1)S(1)}, u32[]{:S(2)}, u32[]{:S(2)}) collective-permute-start(bf16[64,1024]{1,0:T(8,128)(2,1)S(1)} %collective-permute-done.1.refs_4_), channel_id=1, source_target_pairs={{0,1},{1,0},{2,3},{3,2},{4,5},{5,4},{6,7},{7,6},{8,9},{9,8},{10,11... | collective-permute-start | bytes 393224 | tf_op jit(solution)/shard_map/ppermute | solution.py:254
  26.3 7.0 %collective-permute-start.13 = (bf16[64,1024]{1,0:T(8,128)(2,1)S(1)}, bf16[64,1024]{1,0:T(8,128)(2,1)S(1)}, u32[]{:S(2)}, u32[]{:S(2)}) collective-permute-start(bf16[64,1024]{1,0:T(8,128)(2,1)S(1)} %collective-permute-done.2.refs_5_), channel_id=1, source_target_pairs={{0,1},{1,0},{2,3},{3,2},{4,5},{5,4},{6,7},{7,6},{8,9},{9,8},{10,11... | collective-permute-start | bytes 393224 | tf_op jit(solution)/shard_map/ppermute | solution.py:254
  27.9 5.8 %collective-permute-start.11 = (bf16[64,1024]{1,0:T(8,128)(2,1)S(1)}, bf16[64,1024]{1,0:T(8,128)(2,1)S(1)}, u32[]{:S(2)}, u32[]{:S(2)}) collective-permute-start(bf16[64,1024]{1,0:T(8,128)(2,1)S(1)} %get-tuple-element.71), channel_id=1, source_target_pairs={{0,4},{2,6},{4,0},{6,2},{8,12},{10,14},{12,8},{14,10},{16,20},{18,... | collective-permute-start | bytes 393224 | tf_op jit(solution)/shard_map/ppermute | solution.py:264
  30.5 16.0 %collective-permute-start.10 = (bf16[128,1024]{1,0:T(8,128)(2,1)S(1)}, bf16[128,1024]{1,0:T(8,128)(2,1)S(1)}, u32[]{:S(2)}, u32[]{:S(2)}) collective-permute-start(bf16[128,1024]{1,0:T(8,128)(2,1)S(1)} %get-tuple-element.70), channel_id=1, source_target_pairs={{0,0},{2,10},{4,4},{6,14},{8,8},{10,2},{12,12},{14,6},{16,16},{18,... | collective-permute-start | bytes 786440 | tf_op jit(solution)/shard_map/ppermute | solution.py:261
  34.2 5.3 %collective-permute-start.16 = (bf16[64,1024]{1,0:T(8,128)(2,1)S(1)}, bf16[64,1024]{1,0:T(8,128)(2,1)S(1)}, u32[]{:S(2)}, u32[]{:S(2)}) collective-permute-start(bf16[64,1024]{1,0:T(8,128)(2,1)S(1)} %get-tuple-element.80), channel_id=1, source_target_pairs={{0,4},{2,6},{4,0},{6,2},{8,12},{10,14},{12,8},{14,10},{16,20},{18,... | collective-permute-start | bytes 393224 | tf_op jit(solution)/shard_map/ppermute | solution.py:264
  35.8 12.5 %collective-permute-start.15 = (bf16[64,1024]{1,0:T(8,128)(2,1)S(1)}, bf16[64,1024]{1,0:T(8,128)(2,1)S(1)}, u32[]{:S(2)}, u32[]{:S(2)}) collective-permute-start(bf16[64,1024]{1,0:T(8,128)(2,1)S(1)} %add_convert_fusion.1), channel_id=1, source_target_pairs={{0,16},{2,26},{4,20},{6,30},{8,24},{10,18},{12,28},{14,22},{16,0},... | collective-permute-start | bytes 393224 | tf_op jit(solution)/shard_map/ppermute | solution.py:261
  38.5 9.7 %collective-permute-start.14 = (bf16[64,1024]{1,0:T(8,128)(2,1)S(1)}, bf16[64,1024]{1,0:T(8,128)(2,1)S(1)}, u32[]{:S(2)}, u32[]{:S(2)}) collective-permute-start(bf16[64,1024]{1,0:T(8,128)(2,1)S(1)} %get-tuple-element.76), channel_id=1, source_target_pairs={{0,4},{2,14},{4,0},{6,10},{8,12},{10,6},{12,8},{14,2},{16,20},{18,... | collective-permute-start | bytes 393224 | tf_op jit(solution)/shard_map/ppermute | solution.py:261
  39.5 10.4 %collective-permute-start.17 = (bf16[64,1024]{1,0:T(8,128)(2,1)S(1)}, bf16[64,1024]{1,0:T(8,128)(2,1)S(1)}, u32[]{:S(2)}, u32[]{:S(2)}) collective-permute-start(bf16[64,1024]{1,0:T(8,128)(2,1)S(1)} %add_convert_fusion), channel_id=1, source_target_pairs={{0,16},{2,26},{4,20},{6,30},{8,24},{10,18},{12,28},{14,22},{16,0},... | collective-permute-start | bytes 393224 | tf_op jit(solution)/shard_map/ppermute | solution.py:261
  42.3 7.7 %collective-permute-start.18 = (bf16[64,1024]{1,0:T(8,128)(2,1)S(1)}, bf16[64,1024]{1,0:T(8,128)(2,1)S(1)}, u32[]{:S(2)}, u32[]{:S(2)}) collective-permute-start(bf16[64,1024]{1,0:T(8,128)(2,1)S(1)} %get-tuple-element.83), channel_id=1, source_target_pairs={{0,4},{2,14},{4,0},{6,10},{8,12},{10,6},{12,8},{14,2},{16,20},{18,... | collective-permute-start | bytes 393224 | tf_op jit(solution)/shard_map/ppermute | solution.py:261
  46.4 5.1 %copy-start.2 = (f32[1024]{0:T(1024)S(1)}, f32[1024]{0:T(1024)}, u32[]{:S(2)}) copy-start(f32[1024]{0:T(1024)} %param.12) | copy-start | bytes 12292
  50.2 1.4 %collective-permute-start.19 = (bf16[2,32,1024]{2,1,0:T(8,128)(2,1)S(1)}, bf16[2,32,1024]{2,1,0:T(8,128)(2,1)S(1)}, u32[]{:S(2)}, u32[]{:S(2)}) collective-permute-start(bf16[2,32,1024]{2,1,0:T(8,128)(2,1)S(1)} %fusion.4), channel_id=1, source_target_pairs={{0,2},{2,0},{4,6},{6,4},{8,10},{10,8},{12,14},{14,12},{16,18},{18,... | collective-permute-start | bytes 393224 | tf_op jit(solution)/shard_map/ppermute | solution.py:257
